TPU v7x, 32 devices: a whole 2x2x4 slice. The times are simulated.
32 devices in a mesh: gx: 4 (over x, core), gy: 8 (over z, y).
Axes of the slice: x: 2, y: 2, z: 4, core: 2. Of those that a mesh axis runs over, the one named last changes fastest.
Arguments:
- state: float32 [48, 256, 2048], P(None, 'gx', 'gy'), may hold values from -6 to 6
- right_side: float32 [48, 256, 2048], P(None, 'gx', 'gy'), may hold values from -6 to 6
- sigma: float32 [256, 2048], P('gx', 'gy'), may hold values from 0.25 to 4
- coupling: float32 [6, 6], replicated, may hold values from -2 to 2
- omega: float32 [4], replicated, may hold values from 0.1 to 8
- pressure_coef: float32 [6], replicated, may hold values from 0.5 to 1.5
- tile_cells: int32 [8192, 128], P(('gx', 'gy')), may hold values from 0 to 16383
- tile_owner: int32 [8192, 1], P(('gx', 'gy')), may hold values from 0 to 7; in each aligned block of 256 rows (0 to 255, 256 to 511, ...) at most 48 rows name the same one
- tile_panel: int32 [8192, 1], P(('gx', 'gy')), may hold values from 0 to 31
- interp: float32 [8192, 128, 128], P(('gx', 'gy')), may hold values from -1 to 1
- correction: float32 [32768], P('gy'), may hold values from 0.5 to 2
- mode_shape: float32 [32, 32768], P(None, 'gy'), may hold values from -1 to 1
Outputs:
- new_state: float32 [48, 256, 2048], P(None, 'gx', 'gy')
- panel_pressure: float32 [8, 32768], P(None, 'gy')
- gaf: float32 [32, 8], P('gy')
Inputs may be any that keep to these rules, and one draw needn't show every extreme that they name: `tile_owner`: each device's 256 tiles name one owner at most 48 times, a bound that some block reaches.
All inputs are finite; a program needn't handle non-finite values.
Results may differ from a plain program's by a relative error of at most 0.0003.
Values sent between devices are 32-bit elements; how exact they have to be, the bound alone decides.
No kernel may reach another device: no remote copies, remote signals or barrier semaphores. Data moves between devices by JAX's collectives and lax.ppermute only.
A program may use at most 192 MiB of HBM per device.

v0:
```python
import jax
import jax.numpy as jnp
from jax import lax
from jax.sharding import PartitionSpec as P

SWEEPS = 2
CAP = 48


def with_halo(cells, sides, width):
    for axis, dim in sides:
        count = lax.axis_size(axis)
        ends = count - 1
        head = lax.slice_in_dim(cells, 0, width, axis=dim)
        tail = lax.slice_in_dim(cells, cells.shape[dim] - width, cells.shape[dim], axis=dim)
        cells = jnp.concatenate(
            [
                lax.ppermute(tail, axis, [(i, (i + 1) % count) for i in range(ends)]),
                cells,
                lax.ppermute(head, axis, [((i + 1) % count, i) for i in range(ends)]),
            ],
            axis=dim,
        )
    return cells


def relax(center, padded, rhs, dval, omega, coupling):
    modes = omega.shape[0]
    nvar = coupling.shape[0]
    lead = (modes, 2, nvar)
    nbs = padded[:, 2:, 1:-1] + padded[:, :-2, 1:-1]
    nbs = nbs + padded[:, 1:-1, 2:] + padded[:, 1:-1, :-2]
    field = center.reshape(lead + center.shape[1:])
    nbs = nbs.reshape(lead + center.shape[1:])
    rhs5 = rhs.reshape(lead + center.shape[1:])
    mixed = jnp.einsum("vw,mpwxy->mpvxy", coupling, nbs, precision=lax.Precision.HIGHEST)
    freq = omega[:, None, None, None]
    a_re = dval * field[:, 0] - mixed[:, 0] - freq * field[:, 1]
    a_im = dval * field[:, 1] - mixed[:, 1] + freq * field[:, 0]
    s_re = rhs5[:, 0] - a_re
    s_im = rhs5[:, 1] - a_im
    denom = dval * dval + freq * freq
    upd_re = (dval * s_re + freq * s_im) / denom
    upd_im = (dval * s_im - freq * s_re) / denom
    field = field + 0.8 * jnp.stack([upd_re, upd_im], axis=1)
    return field.reshape(center.shape)


def body(
    state,
    right_side,
    sigma,
    coupling,
    omega,
    pressure_coef,
    tile_cells,
    tile_owner,
    tile_panel,
    interp,
    correction,
    mode_shape,
):
    comp, rows, cols = state.shape
    modes = omega.shape[0]
    nvar = coupling.shape[0]
    field = state
    dval = 4.0 + sigma
    for sweep in range(SWEEPS):
        padded = with_halo(field, (("gx", 1), ("gy", 2)), 1)
        field = relax(field, padded, right_side, dval, omega, coupling)
    field5 = field.reshape(modes, 2, nvar, rows, cols)
    press = jnp.einsum("v,mpvxy->mpxy", pressure_coef, field5, precision=lax.Precision.HIGHEST)
    press = press.reshape(2 * modes, rows * cols)
    tiles = tile_cells.shape[0]
    surf = jnp.take(press, tile_cells.reshape(-1), axis=1).reshape(2 * modes, tiles, 128)
    contrib = jnp.einsum("qtc,tcp->tqp", surf, interp, precision=lax.Precision.HIGHEST)
    owners = lax.axis_size("gy")
    panel_tiles = mode_shape.shape[1] // 128
    owner = tile_owner[:, 0]
    panel = tile_panel[:, 0]
    owner_hot = (owner[:, None] == jnp.arange(owners, dtype=jnp.int32)[None, :]).astype(jnp.int32)
    rank = jnp.sum((jnp.cumsum(owner_hot, axis=0) - 1) * owner_hot, axis=1)
    slot = owner * CAP + rank
    place = slot[:, None] == jnp.arange(owners * CAP, dtype=jnp.int32)[None, :]
    send_buf = jnp.einsum(
        "ts,tqp->sqp", place.astype(jnp.float32), contrib, precision=lax.Precision.HIGHEST
    )
    send_buf = send_buf.reshape(owners, CAP, 2 * modes, 128)
    send_ids = (jnp.sum(jnp.where(place, panel[:, None] + 1, 0), axis=0) - 1).reshape(owners, CAP)
    got, got_ids = (
        lax.all_to_all(send_buf, "gy", split_axis=0, concat_axis=0, tiled=True),
        lax.all_to_all(send_ids, "gy", split_axis=0, concat_axis=0, tiled=True),
    )
    pick = (
        got_ids.reshape(-1)[:, None] == jnp.arange(panel_tiles, dtype=jnp.int32)[None, :]
    ).astype(jnp.float32)
    local = jnp.einsum(
        "sk,sqp->qkp", pick, got.reshape(-1, 2 * modes, 128), precision=lax.Precision.HIGHEST
    )
    local = local.reshape(2 * modes, panel_tiles * 128)
    total = lax.psum(local, "gx")
    corrected = total * correction[None, :]
    forces = jnp.dot(mode_shape, corrected.T, precision=lax.Precision.HIGHEST)
    gaf = lax.psum_scatter(forces, "gy", scatter_dimension=0, tiled=True)
    return (field, total, gaf)


def solution(mesh):
    placed = (
        P(None, "gx", "gy"),
        P(None, "gx", "gy"),
        P("gx", "gy"),
        P(),
        P(),
        P(),
        P(("gx", "gy"), None),
        P(("gx", "gy"), None),
        P(("gx", "gy"), None),
        P(("gx", "gy"), None, None),
        P("gy"),
        P(None, "gy"),
    )
    return jax.shard_map(
        body,
        mesh=mesh,
        in_specs=placed,
        out_specs=(P(None, "gx", "gy"), P(None, "gy"), P("gy", None)),
        check_vma=False,
    )
```

profile of v0, /device:TPU:0, one launch (start us, length us, event | category | flops | bytes accessed | tf_op | source)
XLA Modules:
  0.0 382.6 jit_solution(8527900563083574220)
XLA Ops:
  9.7 3.0 collective-permute-start.1
  17.3 7.3 %all-to-all-start.1 = ((s32[8,1,48]{2,1,0:T(1,128)}), s32[8,1,48]{2,1,0:T(1,128)S(1)}, u32[]{:S(2)}, u32[]{:S(2)}) async-start(s32[8,1,48]{2,1,0:T(1,128)} %sub.88), calls=%async_computation.1 | async-start | bytes 8192 | tf_op jit(solution)/shard_map/all_to_all | solution.py:92
  24.6 3.6 fusion.46
  28.9 2.3 fusion.44
  31.2 2.1 copy.57
  33.3 3.9 %collective-permute-start.3 = (f32[48,66,1]{1,0,2:T(8,128)S(1)}, f32[48,66,1]{1,0,2:T(8,128)S(1)}, u32[]{:S(2)}, u32[]{:S(2)}) collective-permute-start(f32[48,66,1]{1,0,2:T(8,128)S(1)} %copy.57), channel_id=1, source_target_pairs={{0,1},{1,2},{2,3},{3,4},{4,5},{5,6},{6,7},{8,9},{9,10},{10,11},{11... | collective-permute-start | bytes 38024 | tf_op jit(solution)/shard_map/ppermute | solution.py:18
  37.2 2.1 copy.55
  40.7 5.7 %copy.54 = f32[4,2,6,64,256]{4,2,3,1,0:T(8,128)} copy(f32[4,2,6,64,256]{4,3,2,1,0:T(8,128)} %bitcast.65) | data formatting | bytes 6291456 | tf_op jit(solution)/shard_map/reshape | solution.py:33
  50.2 9.4 %fusion.7 = f32[48,64,256]{2,1,0:T(8,128)S(1)} fusion(f32[48,66,1]{2,1,0:T(8,128)} %copy.58, f32[48,1,256]{2,1,0:T(1,128)S(1)} %collective-permute-done, f32[48,64,256]{2,1,0:T(8,128)} %param.12, f32[48,1,256]{2,1,0:T(1,128)S(1)} %collective-permute-done.1, f32[48,66,1]{2,1,0:T(8,128)} %copy.56), kind=kLoop, calls=%fused_computation.21 | loop fusion | flops 8650752 | bytes 6415104 | tf_op jit(solution)/shard_map/add | solution.py:32
  59.6 5.8 %fusion.10 = f32[4,2,6,64,256]{4,2,3,1,0:T(8,128)S(1)} fusion(f32[4,2,6,64,256]{4,3,2,1,0:T(8,128)S(1)} %bitcast.69, f32[6,6]{1,0:T(8,128)S(1)} %copy-done.10), kind=kOutput, calls=%fused_computation.37 | convolution fusion | flops 56623104 | bytes 6291600 | tf_op jit(solution)/shard_map/vw,mpwxy->mpvxy/dot_general | solution.py:36
  65.4 5.2 %add_divide_fusion.1 = (f32[4,1,6,64,256]{4,2,3,1,0:T(8,128)S(1)}, f32[4,1,6,64,256]{4,2,3,1,0:T(8,128)S(1)}, f32[4,1,6,64,256]{4,2,3,1,0:T(8,128)S(1)}) fusion(f32[4,64,256]{2,1,0:T(8,128)S(1)} %broadcast_add_fusion, f32[4]{0:T(128)S(1)} %copy-done.12, f32[64,256]{1,0:T(8,128)S(1)} %get-tuple-element.35, f32[4,2,6,64,256]{4,2,3,1,0:T(8,128)S(1)} %copy-done.5, ...), kind=kLoop, calls=%fused_computation.50 | loop fusion | flops 5505024 | bytes 14483472 | tf_op jit(solution)/shard_map/div | solution.py:43
  72.5 4.5 %copy_add_fusion = (f32[4,2,6,64,256]{4,2,3,1,0:T(8,128)}, f32[4,2,6,64,256]{4,2,3,1,0:T(8,128)S(1)}) fusion(f32[4,2,6,64,256]{4,3,2,1,0:T(8,128)S(1)} %bitcast.66, f32[4,1,6,64,256]{4,2,3,1,0:T(8,128)S(1)} %subtract_divide_fusion.1, f32[4,1,6,64,256]{4,2,3,1,0:T(8,128)S(1)} %get-tuple-element.18), kind=kLoop, calls=%fused_computation.64 | loop fusion | flops 2359296 | bytes 12582912 | tf_op jit(solution)/shard_map/add | solution.py:45
  79.9 3.0 collective-permute-start.5
  84.3 2.3 fusion.43
  88.7 4.6 %collective-permute-start.7 = (f32[48,66,1]{1,0,2:T(8,128)S(1)}, f32[48,66,1]{1,0,2:T(8,128)S(1)}, u32[]{:S(2)}, u32[]{:S(2)}) collective-permute-start(f32[48,66,1]{1,0,2:T(8,128)S(1)} %copy.66), channel_id=1, source_target_pairs={{0,1},{1,2},{2,3},{3,4},{4,5},{5,6},{6,7},{8,9},{9,10},{10,11},{11... | collective-permute-start | bytes 38024 | tf_op jit(solution)/shard_map/ppermute | solution.py:18
  93.3 2.1 copy.64
  98.6 2.8 collective-permute-done.6
  103.3 9.4 %fusion.4 = f32[48,64,256]{2,1,0:T(8,128)S(1)} fusion(f32[48,66,1]{2,1,0:T(8,128)} %copy.67, f32[48,1,256]{2,1,0:T(1,128)S(1)} %collective-permute-done.4, f32[48,64,256]{2,1,0:T(8,128)} %copy-done.3, f32[48,1,256]{2,1,0:T(1,128)S(1)} %collective-permute-done.5, f32[48,66,1]{2,1,0:T(8,128)} %copy.65), kind=kLoop, calls=%fused_computation.10 | loop fusion | flops 8650752 | bytes 6415104 | tf_op jit(solution)/shard_map/add | solution.py:32
  112.7 5.8 %fusion.13 = f32[4,2,6,64,256]{4,2,3,1,0:T(8,128)S(1)} fusion(f32[4,2,6,64,256]{4,3,2,1,0:T(8,128)S(1)} %bitcast.70, f32[6,6]{1,0:T(8,128)S(1)} %copy-done.10), kind=kOutput, calls=%fused_computation.38 | convolution fusion | flops 56623104 | bytes 6291600 | tf_op jit(solution)/shard_map/vw,mpwxy->mpvxy/dot_general | solution.py:36
  118.5 5.0 %add_divide_fusion = (f32[4,1,6,64,256]{4,2,3,1,0:T(8,128)S(1)}, f32[4,1,6,64,256]{4,2,3,1,0:T(8,128)S(1)}, f32[4,1,6,64,256]{4,2,3,1,0:T(8,128)S(1)}) fusion(f32[4,64,256]{2,1,0:T(8,128)S(1)} %broadcast_add_fusion, f32[4]{0:T(128)S(1)} %copy-done.12, f32[64,256]{1,0:T(8,128)S(1)} %get-tuple-element.35, f32[4,2,6,64,256]{4,2,3,1,0:T(8,128)S(1)} %copy-done.4, ...), kind=kLoop, calls=%fused_computation.48 | loop fusion | flops 5505024 | bytes 14483472 | tf_op jit(solution)/shard_map/div | solution.py:43
  124.1 2.8 fusion.42
  126.9 4.0 %fusion.38 = f32[1,8,16384]{2,0,1:T(1,128)S(1)} fusion(f32[8,16384,6]{1,2,0:T(8,128)S(1)} %bitcast.71, f32[6]{0:T(128)S(1)} %copy-done.13), kind=kOutput, calls=%fused_computation.87 | convolution fusion | flops 9437184 | bytes 3670040 | tf_op jit(solution)/shard_map/v,mpvxy->mpxy/dot_general | solution.py:72
  130.9 4.6 %copy.78 = f32[1,8,16384]{1,2,0:T(8,128)} copy(f32[1,8,16384]{2,0,1:T(1,128)S(1)} %fusion.38) | data formatting | bytes 1048576 | tf_op jit(solution)/shard_map/v,mpvxy->mpxy/dot_general | solution.py:72
  135.5 112.4 %gather_fusion = f32[32768,8]{1,0:T(8,128)} fusion(f32[8,16384]{0,1:T(8,128)} %bitcast.67, s32[32768]{0:T(1024)S(1)} %broadcast_clamp_fusion), kind=kCustom, calls=%fused_computation | custom fusion | bytes 2228224 | tf_op jit(solution)/shard_map/jit(_take)/gather | solution.py:75
  247.8 9.2 %copy.71 = f32[8,256,128]{2,0,1:T(8,128)S(1)} copy(f32[8,256,128]{0,2,1:T(8,128)} %bitcast.68) | data formatting | bytes 2097152 | tf_op jit(solution)/shard_map/jit(_take)/gather | solution.py:75
  257.0 16.6 %fusion.22 = f32[256,8,128]{2,1,0:T(8,128)S(1)} fusion(f32[256,128,128]{2,1,0:T(8,128)} %param.21, f32[8,256,128]{2,0,1:T(8,128)S(1)} %copy.71, pred[256,128]{1,0:T(8,128)(4,1)S(1)} %compare_and_fusion), kind=kOutput, calls=%fused_computation.55 | convolution fusion | flops 402915328 | bytes 18907136 | tf_op jit(solution)/shard_map/qtc,tcp->tqp/dot_general | solution.py:76
  275.9 6.0 %all-to-all-start = ((f32[8,48,8,128]{3,1,2,0:T(8,128)}), f32[8,48,8,128]{3,1,2,0:T(8,128)S(1)}, u32[]{:S(2)}, u32[]{:S(2)}) async-start(f32[8,48,8,128]{3,1,2,0:T(8,128)} %copy.73), calls=%async_computation | async-start | bytes 3145728 | tf_op jit(solution)/shard_map/all_to_all | solution.py:91
  284.5 4.8 %copy.69 = f32[4,2,6,64,256]{4,3,2,1,0:T(8,128)} copy(f32[4,2,6,64,256]{4,2,3,1,0:T(8,128)} %get-tuple-element.22) | data formatting | bytes 6291456 | tf_op jit(solution)/shard_map/mul | solution.py:45
  289.3 29.9 %all-to-all-done = f32[8,48,8,128]{3,1,2,0:T(8,128)S(1)} async-done(((f32[8,48,8,128]{3,1,2,0:T(8,128)}), f32[8,48,8,128]{3,1,2,0:T(8,128)S(1)}, u32[]{:S(2)}, u32[]{:S(2)}) %all-to-all-start) | async-done | bytes 1572896 | tf_op jit(solution)/shard_map/all_to_all | solution.py:91
  320.8 5.2 %bitcast_add_fusion = f32[48,64,256]{2,1,0:T(8,128)} fusion(f32[48,64,256]{2,1,0:T(8,128)} %copy-done.3, f32[4,2,6,64,256]{4,3,2,1,0:T(8,128)} %copy.69), kind=kLoop, calls=%fused_computation.31 | loop fusion | flops 786432 | bytes 9437184 | tf_op jit(solution)/shard_map/add | solution.py:45
  326.0 24.4 %all-reduce.3.cloned.1.call-done = f32[8,4096]{1,0:T(8,128)} async-done(((f32[8,4096]{1,0:T(8,128)}), f32[8,4096]{1,0:T(8,128)}) %all-reduce.3.cloned.1.call-update) | async-done | bytes 131088 | tf_op jit(solution)/shard_map/psum | solution.py:101
  351.9 21.4 %all-reduce = f32[32,8]{0,1:T(8,128)S(1)} all-reduce(f32[32,8]{0,1:T(8,128)S(1)} %convolution_bitcast_fusion.1), channel_id=2, replica_groups=mesh['gx'=4,'gy'=8] {'gy'}, use_global_device_ids=true, to_apply=%region_5.6.clone | all-reduce | flops 256 | bytes 2048
  (87 shorter events, 36.2 us)
Async XLA Ops:
  7.2 343.3 %copy-start = (f32[32,4096]{1,0:T(8,128)S(1)}, f32[32,4096]{1,0:T(8,128)}, u32[]{:S(2)}) copy-start(f32[32,4096]{1,0:T(8,128)} %param.23) | copy-start | bytes 1572868
  8.4 19.9 %collective-permute-start = (f32[48,1,256]{2,1,0:T(1,128)S(1)}, f32[48,1,256]{2,1,0:T(1,128)S(1)}, u32[]{:S(2)}, u32[]{:S(2)}) collective-permute-start(f32[48,1,256]{2,1,0:T(1,128)S(1)} %get-tuple-element.34), channel_id=1, source_target_pairs={{8,0},{16,8},{24,16},{9,1},{17,9},{25,17},{10,2},{18,10},{26,18},{... | collective-permute-start | bytes 147464 | tf_op jit(solution)/shard_map/ppermute | solution.py:20
  9.7 18.6 %collective-permute-start.1 = (f32[48,1,256]{2,1,0:T(1,128)S(1)}, f32[48,1,256]{2,1,0:T(1,128)S(1)}, u32[]{:S(2)}, u32[]{:S(2)}) collective-permute-start(f32[48,1,256]{2,1,0:T(1,128)S(1)} %get-tuple-element.33), channel_id=1, source_target_pairs={{0,8},{8,16},{16,24},{1,9},{9,17},{17,25},{2,10},{10,18},{18,26},{... | collective-permute-start | bytes 147464 | tf_op jit(solution)/shard_map/ppermute | solution.py:18
  17.3 258.7 %all-to-all-start.1 = ((s32[8,1,48]{2,1,0:T(1,128)}), s32[8,1,48]{2,1,0:T(1,128)S(1)}, u32[]{:S(2)}, u32[]{:S(2)}) async-start(s32[8,1,48]{2,1,0:T(1,128)} %sub.88), calls=%async_computation.1 | async-start | bytes 8192 | tf_op jit(solution)/shard_map/all_to_all | solution.py:92
  24.5 3.6 copy-start.8
  24.5 3.8 copy-start.9
  24.6 3.8 copy-start.12
  24.6 3.8 copy-start.1
  33.3 13.1 %collective-permute-start.3 = (f32[48,66,1]{1,0,2:T(8,128)S(1)}, f32[48,66,1]{1,0,2:T(8,128)S(1)}, u32[]{:S(2)}, u32[]{:S(2)}) collective-permute-start(f32[48,66,1]{1,0,2:T(8,128)S(1)} %copy.57), channel_id=1, source_target_pairs={{0,1},{1,2},{2,3},{3,4},{4,5},{5,6},{6,7},{8,9},{9,10},{10,11},{11... | collective-permute-start | bytes 38024 | tf_op jit(solution)/shard_map/ppermute | solution.py:18
  39.3 8.9 %collective-permute-start.2 = (f32[48,66,1]{1,0,2:T(8,128)S(1)}, f32[48,66,1]{1,0,2:T(8,128)S(1)}, u32[]{:S(2)}, u32[]{:S(2)}) collective-permute-start(f32[48,66,1]{1,0,2:T(8,128)S(1)} %copy.55), channel_id=1, source_target_pairs={{1,0},{2,1},{3,2},{4,3},{5,4},{6,5},{7,6},{9,8},{10,9},{11,10},{12... | collective-permute-start | bytes 38024 | tf_op jit(solution)/shard_map/ppermute | solution.py:20
  50.2 9.4 %copy-start.10 = (f32[6,6]{1,0:T(8,128)S(1)}, f32[6,6]{1,0:T(8,128)}, u32[]{:S(2)}) copy-start(f32[6,6]{1,0:T(8,128)} %param.15) | copy-start | bytes 436
  59.6 5.8 %copy-start.5 = (f32[4,2,6,64,256]{4,2,3,1,0:T(8,128)S(1)}, f32[4,2,6,64,256]{4,2,3,1,0:T(8,128)}, u32[]{:S(2)}) copy-start(f32[4,2,6,64,256]{4,2,3,1,0:T(8,128)} %copy.54) | copy-start | bytes 9437188
  59.6 5.8 %copy-start.6 = (f32[4,1,6,64,256]{4,3,2,1,0:T(8,128)S(1)}, f32[4,1,6,64,256]{4,3,2,1,0:T(8,128)}, u32[]{:S(2)}) copy-start(f32[4,1,6,64,256]{4,3,2,1,0:T(8,128)} %get-tuple-element.32) | copy-start | bytes 4718596
  70.6 1.9 copy-start.2
  78.5 5.8 %copy-start.3 = (f32[48,64,256]{2,1,0:T(8,128)}, f32[48,64,256]{2,1,0:T(8,128)S(1)}, u32[]{:S(2)}) copy-start(f32[48,64,256]{2,1,0:T(8,128)S(1)} %bitcast_add_fusion.1) | copy-start | bytes 9437188
  78.6 4.4 %collective-permute-start.4 = (f32[48,1,256]{2,1,0:T(1,128)S(1)}, f32[48,1,256]{2,1,0:T(1,128)S(1)}, u32[]{:S(2)}, u32[]{:S(2)}) collective-permute-start(f32[48,1,256]{2,1,0:T(1,128)S(1)} %get-tuple-element.30), channel_id=1, source_target_pairs={{8,0},{16,8},{24,16},{9,1},{17,9},{25,17},{10,2},{18,10},{26,18},{... | collective-permute-start | bytes 147464 | tf_op jit(solution)/shard_map/ppermute | solution.py:20
  79.9 3.9 %collective-permute-start.5 = (f32[48,1,256]{2,1,0:T(1,128)S(1)}, f32[48,1,256]{2,1,0:T(1,128)S(1)}, u32[]{:S(2)}, u32[]{:S(2)}) collective-permute-start(f32[48,1,256]{2,1,0:T(1,128)S(1)} %get-tuple-element.29), channel_id=1, source_target_pairs={{0,8},{8,16},{16,24},{1,9},{9,17},{17,25},{2,10},{10,18},{18,26},{... | collective-permute-start | bytes 147464 | tf_op jit(solution)/shard_map/ppermute | solution.py:18
  88.7 8.0 %collective-permute-start.7 = (f32[48,66,1]{1,0,2:T(8,128)S(1)}, f32[48,66,1]{1,0,2:T(8,128)S(1)}, u32[]{:S(2)}, u32[]{:S(2)}) collective-permute-start(f32[48,66,1]{1,0,2:T(8,128)S(1)} %copy.66), channel_id=1, source_target_pairs={{0,1},{1,2},{2,3},{3,4},{4,5},{5,6},{6,7},{8,9},{9,10},{10,11},{11... | collective-permute-start | bytes 38024 | tf_op jit(solution)/shard_map/ppermute | solution.py:18
  95.4 6.1 %collective-permute-start.6 = (f32[48,66,1]{1,0,2:T(8,128)S(1)}, f32[48,66,1]{1,0,2:T(8,128)S(1)}, u32[]{:S(2)}, u32[]{:S(2)}) collective-permute-start(f32[48,66,1]{1,0,2:T(8,128)S(1)} %copy.64), channel_id=1, source_target_pairs={{1,0},{2,1},{3,2},{4,3},{5,4},{6,5},{7,6},{9,8},{10,9},{11,10},{12... | collective-permute-start | bytes 38024 | tf_op jit(solution)/shard_map/ppermute | solution.py:20
  112.7 5.8 %copy-start.4 = (f32[4,2,6,64,256]{4,2,3,1,0:T(8,128)S(1)}, f32[4,2,6,64,256]{4,2,3,1,0:T(8,128)}, u32[]{:S(2)}) copy-start(f32[4,2,6,64,256]{4,2,3,1,0:T(8,128)} %get-tuple-element.23) | copy-start | bytes 9437188
  112.7 5.8 %copy-start.7 = (f32[4,1,6,64,256]{4,3,2,1,0:T(8,128)S(1)}, f32[4,1,6,64,256]{4,3,2,1,0:T(8,128)}, u32[]{:S(2)}) copy-start(f32[4,1,6,64,256]{4,3,2,1,0:T(8,128)} %get-tuple-element.32) | copy-start | bytes 4718596
  124.1 2.8 copy-start.13
  274.6 7.4 %copy-start.14 = (u32[32]{0:T(128)S(1)}, u32[32]{0:T(128)}, u32[]{:S(2)}) copy-start(u32[32]{0:T(128)} %constant.36) | copy-start | bytes 388
  275.9 43.3 %all-to-all-start = ((f32[8,48,8,128]{3,1,2,0:T(8,128)}), f32[8,48,8,128]{3,1,2,0:T(8,128)S(1)}, u32[]{:S(2)}, u32[]{:S(2)}) async-start(f32[8,48,8,128]{3,1,2,0:T(8,128)} %copy.73), calls=%async_computation | async-start | bytes 3145728 | tf_op jit(solution)/shard_map/all_to_all | solution.py:91
  281.9 68.5 %all-reduce.3.cloned.1.call-start = ((), (), s32[]{:S(2)}) async-start(), calls=%async_computation.2 | async-start | bytes 262144 | tf_op jit(solution)/shard_map/psum | solution.py:101
  320.8 29.7 %copy-start.11 = (f32[4096]{0:T(1024)S(1)}, f32[4096]{0:T(1024)}, u32[]{:S(2)}) copy-start(f32[4096]{0:T(1024)} %param.22) | copy-start | bytes 49156
Sparse Core Ops, SparseCore 0:
  320.9 29.4 all-reduce.2
where the time goes:
time: 388 us; the launch traced here: 383 us
  local copies, waits for them, and re-layouts  171 us (44%)
  waiting for transfers between devices  58.1 us (15%)
  other arithmetic  48.7 us (13%)
  matrix products  35.2 us (9%)
  starting transfers between devices  33.1 us (9%)
  blocking collectives  21.4 us (6%)
  between operations  15.3 us (4%)
    gather x2, local copies, waits for them, and re-layouts, body(): jnp.take(press, tile_cells.reshape(-1), axis=1)  122 us
    all_to_all x1, waiting for transfers between devices, body(): lax.all_to_all(send_buf, 'gy', split_axis=0, concat_axis=0, tiled=True)  29.9 us
    psum x1, waiting for transfers between devices, body(): total = lax.psum(local, 'gx')  24.4 us
    unnamed x1, blocking collectives  21.4 us
    add x2, other arithmetic, relax(): nbs = nbs + padded[:, 1:-1, 2:] + padded[:, 1:-1, :-2]  18.8 us
    dot_general x1, matrix products, body(): jnp.einsum('qtc,tcp->tqp', surf, interp, precision=lax.Precision.HIGHEST)  16.6 us
    ppermute x4, starting transfers between devices, with_halo(): lax.ppermute(tail, axis, [(i, (i + 1) % count) for i in range(ends)])  14.5 us
    add x4, other arithmetic, relax(): field = field + 0.8 * jnp.stack([upd_re, upd_im], axis=1)  13.1 us
  transfers between devices with their start and end apart: 11, of which 4 were waited for; matrix products, arithmetic and copies ran while one was open for 65% of the time, Pallas kernels for 0%

commit v1 on v0

v1 whole, which is shorter than its diff:
```python
import functools

import jax
import jax.numpy as jnp
from jax import lax
from jax.experimental import pallas as pl
from jax.experimental.pallas import tpu as pltpu
from jax.sharding import PartitionSpec as P

F32 = jnp.float32
BF16 = jnp.bfloat16
LANES = 128
BLOCK_TILES = 16
VMEM_LIMIT = 48 << 20


def vmem():
    return pl.BlockSpec(memory_space=pltpu.VMEM)


def smem():
    return pl.BlockSpec(memory_space=pltpu.SMEM)


def pack_edges(field_ref, first, planes, up_ref, down_ref, left_ref, right_ref):
    rows, cols = field_ref.shape[1:]
    lane = lax.broadcasted_iota(jnp.int32, (rows, LANES), 1)
    left = left_ref[...]
    right = right_ref[...]
    for k in range(planes):
        up_ref[0, k : k + 1, :] = field_ref[k, 0:1, :]
        down_ref[0, k : k + 1, :] = field_ref[k, rows - 1 : rows, :]
        here = lane == first + k
        left = jnp.where(here, field_ref[k, :, 0:1], left)
        right = jnp.where(here, field_ref[k, :, cols - 1 : cols], right)
    left_ref[...] = left
    right_ref[...] = right


def pack_kernel(state_ref, up_ref, down_ref, left_ref, right_ref):
    mode = pl.program_id(0)
    planes = state_ref.shape[0]

    @pl.when(mode == 0)
    def _():
        left_ref[...] = jnp.zeros_like(left_ref)
        right_ref[...] = jnp.zeros_like(right_ref)

    pack_edges(state_ref, mode * planes, planes, up_ref, down_ref, left_ref, right_ref)


def sweep_kernel(
    last,
    coupling_ref,
    omega_ref,
    coef_ref,
    state_ref,
    rhs_ref,
    sigma_ref,
    above_ref,
    below_ref,
    west_ref,
    east_ref,
    new_ref,
    *rest,
):
    nbs_ref, a_ref, b_ref, press_ref = rest[-4:]
    mode = pl.program_id(0)
    planes, rows, cols = state_ref.shape
    nvar = planes // 2
    parts = 2 * omega_ref.shape[0]
    freq = omega_ref[mode]
    dval = 4.0 + sigma_ref[...]
    scale = 0.8 / (dval * dval + freq * freq)
    a_ref[...] = dval * scale
    b_ref[...] = freq * scale

    row = lax.broadcasted_iota(jnp.int32, (rows, cols), 0)
    lane = lax.broadcasted_iota(jnp.int32, (rows, LANES), 1)
    for k in range(planes):
        comp = mode * planes + k
        plane = state_ref[k]
        total = jnp.where(row == 0, above_ref[0, k : k + 1, :], pltpu.roll(plane, 1, 0))
        total = total + jnp.where(
            row == rows - 1, below_ref[0, k : k + 1, :], pltpu.roll(plane, rows - 1, 0)
        )
        west = pltpu.roll(west_ref[...], lax.rem(LANES - comp, LANES), 1)
        east = pltpu.roll(east_ref[...], LANES - 1 - comp, 1)
        from_west = pltpu.roll(plane, 1, 1)
        from_east = pltpu.roll(plane, cols - 1, 1)
        nbs_ref[k, :, :LANES] = (
            total[:, :LANES]
            + jnp.where(lane == 0, west, from_west[:, :LANES])
            + from_east[:, :LANES]
        )
        nbs_ref[k, :, cols - LANES :] = (
            total[:, cols - LANES :]
            + from_west[:, cols - LANES :]
            + jnp.where(lane == LANES - 1, east, from_east[:, cols - LANES :])
        )

    weight = [[coupling_ref[v, w] for w in range(nvar)] for v in range(nvar)]
    coef = [coef_ref[v] for v in range(nvar)]

    def strip(step, carry):
        here = pl.ds(pl.multiple_of(step * 8, 8), 8)
        nbs = [nbs_ref[k, here, :] for k in range(planes)]
        a = a_ref[here, :]
        b = b_ref[here, :]
        press_re = press_im = None
        for v in range(nvar):
            res_re = rhs_ref[v, here, :]
            res_im = rhs_ref[nvar + v, here, :]
            for w in range(nvar):
                res_re = res_re + weight[v][w] * nbs[w]
                res_im = res_im + weight[v][w] * nbs[nvar + w]
            new_re = 0.2 * state_ref[v, here, :] + a * res_re + b * res_im
            new_im = 0.2 * state_ref[nvar + v, here, :] + a * res_im - b * res_re
            new_ref[v, here, :] = new_re
            new_ref[nvar + v, here, :] = new_im
            if last:
                press_re = coef[v] * new_re if v == 0 else press_re + coef[v] * new_re
                press_im = coef[v] * new_im if v == 0 else press_im + coef[v] * new_im
        if last:
            for part, value in enumerate((press_re, press_im)):
                start = step * (8 * parts) + 2 * mode + part
                for half in range(cols // LANES):
                    piece = value[:, half * LANES : (half + 1) * LANES]
                    press_ref[half, pl.ds(start, 8, stride=parts), :] = piece
        return carry

    lax.fori_loop(0, rows // 8, strip, 0)
    if last:
        table_ref = rest[0]

        @pl.when(mode == pl.num_programs(0) - 1)
        def _():
            size = table_ref.shape[0] // 2
            for half in range(cols // LANES):
                whole = press_ref[half]
                high = whole.astype(BF16)
                span = slice(half * LANES, (half + 1) * LANES)
                table_ref[:size, span] = high
                table_ref[size:, span] = (whole - high.astype(F32)).astype(BF16)

    else:
        up_ref, down_ref, left_ref, right_ref = rest[:4]

        @pl.when(mode == 0)
        def _():
            left_ref[...] = jnp.zeros_like(left_ref)
            right_ref[...] = jnp.zeros_like(right_ref)

        pack_edges(new_ref, mode * planes, planes, up_ref, down_ref, left_ref, right_ref)


def edge_shapes(modes, planes, rows, cols):
    shapes = (
        jax.ShapeDtypeStruct((modes, planes, cols), F32),
        jax.ShapeDtypeStruct((modes, planes, cols), F32),
        jax.ShapeDtypeStruct((rows, LANES), F32),
        jax.ShapeDtypeStruct((rows, LANES), F32),
    )
    row_spec = pl.BlockSpec((1, planes, cols), lambda m: (m, 0, 0))
    col_spec = pl.BlockSpec((rows, LANES), lambda m: (0, 0))
    return shapes, (row_spec, row_spec, col_spec, col_spec)


def pack(state, modes):
    comp, rows, cols = state.shape
    planes = comp // modes
    shapes, specs = edge_shapes(modes, planes, rows, cols)
    return pl.pallas_call(
        pack_kernel,
        grid=(modes,),
        out_shape=shapes,
        in_specs=[pl.BlockSpec((planes, rows, cols), lambda m: (m, 0, 0))],
        out_specs=specs,
        compiler_params=pltpu.CompilerParams(vmem_limit_bytes=VMEM_LIMIT),
        name="pack",
    )(state)


def exchange(edges):
    up, down, left, right = edges
    nx = lax.axis_size("gx")
    ny = lax.axis_size("gy")
    above = lax.ppermute(down, "gx", [(i, i + 1) for i in range(nx - 1)])
    below = lax.ppermute(up, "gx", [(i + 1, i) for i in range(nx - 1)])
    west = lax.ppermute(right, "gy", [(i, i + 1) for i in range(ny - 1)])
    east = lax.ppermute(left, "gy", [(i + 1, i) for i in range(ny - 1)])
    return above, below, west, east


def sweep(last, coupling, omega, coef, field, rhs, sigma, halo):
    comp, rows, cols = field.shape
    modes = omega.shape[0]
    planes = comp // modes
    edges, edge_specs = edge_shapes(modes, planes, rows, cols)
    block = pl.BlockSpec((planes, rows, cols), lambda m: (m, 0, 0))
    if last:
        table = (4 * modes * rows, cols)
        extra = (jax.ShapeDtypeStruct(table, BF16),)
        extra_specs = (pl.BlockSpec(table, lambda m: (0, 0)),)
    else:
        extra, extra_specs = edges, edge_specs
    return pl.pallas_call(
        functools.partial(sweep_kernel, last),
        grid=(modes,),
        out_shape=(jax.ShapeDtypeStruct(field.shape, F32),) + extra,
        in_specs=[
            smem(),
            smem(),
            smem(),
            block,
            block,
            pl.BlockSpec((rows, cols), lambda m: (0, 0)),
            *edge_specs,
        ],
        out_specs=(block,) + extra_specs,
        scratch_shapes=[
            pltpu.VMEM((planes, rows, cols), F32),
            pltpu.VMEM((rows, cols), F32),
            pltpu.VMEM((rows, cols), F32),
            pltpu.VMEM((cols // LANES, 2 * modes * rows if last else 8, LANES), F32),
        ],
        compiler_params=pltpu.CompilerParams(vmem_limit_bytes=VMEM_LIMIT),
        name="sweep",
    )(coupling, omega, coef, field, rhs, sigma, *halo)


def tile_kernel(place_ref, table_ref, cells_ref, interp_ref, keep_ref, send_ref, acc_ref):
    step = pl.program_id(0)
    block = cells_ref.shape[0]
    parts = acc_ref.shape[1]
    size = table_ref.shape[0] // 2
    cols = table_ref.shape[1]
    rows = size // parts
    shift = cols.bit_length() - 1

    @pl.when(step == 0)
    def _():
        acc_ref[...] = jnp.zeros_like(acc_ref)

    col_at = lax.broadcasted_iota(jnp.int16, (cols, 2 * LANES), 0)
    one = jnp.ones((), BF16)
    zero = jnp.zeros((), BF16)
    blank = jnp.zeros((2 * parts, LANES), F32)
    surfs = []
    for pair in range(block // 2):
        cells = jnp.concatenate(
            [cells_ref[2 * pair : 2 * pair + 1, :], cells_ref[2 * pair + 1 : 2 * pair + 2, :]], axis=1
        )
        col = jnp.broadcast_to((cells & (cols - 1)).astype(jnp.int16), (cols, 2 * LANES))
        hot = jnp.where(col_at == col, one, zero)
        found = jnp.dot(table_ref[...], hot, preferred_element_type=F32)
        found = (found[:size] + found[size:]).reshape(rows, parts, 2 * LANES)
        row = jnp.broadcast_to(cells >> shift, (parts, 2 * LANES))
        bit = rows // 2
        while bit:
            found = jnp.where(((row & bit) != 0)[None], found[bit:], found[:bit])
            bit //= 2
        surfs.append(found[0])
    for pair, surf in enumerate(surfs):
        high = surf.astype(BF16).astype(F32)
        split = jnp.concatenate([high, surf - high], axis=0)
        left = jnp.concatenate(
            [
                jnp.concatenate([split[:, :LANES], blank], axis=1),
                jnp.concatenate([blank, split[:, LANES:]], axis=1),
            ],
            axis=0,
        ).astype(BF16)
        weight = interp_ref[2 * pair : 2 * pair + 2].reshape(2 * LANES, LANES)
        weight_high = weight.astype(BF16)
        weight_low = (weight - weight_high.astype(F32)).astype(BF16)
        right = jnp.concatenate([weight_high, weight_low], axis=1)
        out = jnp.dot(left, right, preferred_element_type=F32)
        for side in range(2):
            line = out[side * 2 * parts : (side + 1) * 2 * parts]
            high_part = line[:parts, :LANES] + line[:parts, LANES:]
            at = place_ref[step * block + 2 * pair + side]
            acc_ref[at] += high_part + line[parts:, :LANES]

    @pl.when(step == pl.num_programs(0) - 1)
    def _():
        half = keep_ref.shape[0]
        keep_ref[...] = acc_ref[:half]
        send_ref[...] = acc_ref[half:]


def tile_sums(place, table, cells, interp, panel_tiles, parts):
    tiles = cells.shape[0]
    half = (panel_tiles // 2, parts, LANES)
    block = min(BLOCK_TILES, tiles)
    return pl.pallas_call(
        tile_kernel,
        grid=(tiles // block,),
        out_shape=(jax.ShapeDtypeStruct(half, F32), jax.ShapeDtypeStruct(half, F32)),
        in_specs=[
            smem(),
            pl.BlockSpec(table.shape, lambda i: (0, 0)),
            pl.BlockSpec((block, LANES), lambda i: (i, 0)),
            pl.BlockSpec((block, LANES, LANES), lambda i: (i, 0, 0)),
        ],
        out_specs=(pl.BlockSpec(half, lambda i: (0, 0, 0)), pl.BlockSpec(half, lambda i: (0, 0, 0))),
        scratch_shapes=[pltpu.VMEM((panel_tiles, parts, LANES), F32)],
        compiler_params=pltpu.CompilerParams(vmem_limit_bytes=VMEM_LIMIT),
        name="tiles",
    )(place, table, cells, interp)


def combine_kernel(order, me_ref, keep_ref, got_ref, shapes_ref, next_keep_ref, next_send_ref):
    owners = len(order)
    chunk = keep_ref.shape[0] // owners
    parts = keep_ref.shape[1]
    modes = shapes_ref.shape[0] // owners
    half = keep_ref.shape[0] // 2
    force = jnp.zeros((parts, modes), F32)
    for at, relative in enumerate(order):
        lines = keep_ref[at * chunk : (at + 1) * chunk] + got_ref[at * chunk : (at + 1) * chunk]
        first = at * chunk
        if first < half:
            next_keep_ref[first : first + chunk] = lines
        else:
            next_send_ref[first - half : first - half + chunk] = lines
        flat = jnp.concatenate([lines[k] for k in range(chunk)], axis=1)
        owner = me_ref[0] ^ relative
        shapes = shapes_ref[pl.ds(pl.multiple_of(owner * modes, 8), modes), :]
        force = force + lax.dot_general(
            flat,
            shapes,
            (((1,), (1,)), ((), ())),
            precision=lax.Precision.HIGHEST,
            preferred_element_type=F32,
        )
    tile = jnp.concatenate([force, jnp.zeros((parts, LANES - modes), F32)], axis=1)
    next_keep_ref[half] = tile
    next_send_ref[half] = tile


def fold_kernel(keep_ref, got_ref, *next_refs):
    total = keep_ref[...] + got_ref[...]
    tiles = total.shape[0] - 1
    if len(next_refs) == 1:
        next_refs[0][...] = total
    else:
        half = tiles // 2
        next_refs[0][:half] = total[:half]
        next_refs[0][half] = total[tiles]
        next_refs[1][...] = total[half:]


def finish_kernel(me_ref, total_ref, panel_ref, gaf_ref, turned_ref):
    rows, chunk, parts, lanes = total_ref.shape
    chunk = chunk - 1
    force = total_ref[0, chunk]
    for i in range(rows):
        for k in range(chunk):
            at = (i * chunk + k) * lanes
            panel_ref[:, at : at + lanes] = total_ref[i, k]
        if i:
            force = force + total_ref[i, chunk]
    turned_ref[...] = jnp.transpose(force)
    share = gaf_ref.shape[0]
    gaf_ref[...] = turned_ref[pl.ds(me_ref[0] * share, share), :]


def local_call(kernel, shapes, name, *args, scratch=(), scalars=0):
    return pl.pallas_call(
        kernel,
        out_shape=tuple(jax.ShapeDtypeStruct(shape, F32) for shape in shapes),
        in_specs=[smem()] * scalars + [vmem()] * (len(args) - scalars),
        out_specs=tuple(vmem() for _ in shapes),
        scratch_shapes=list(scratch),
        compiler_params=pltpu.CompilerParams(vmem_limit_bytes=VMEM_LIMIT),
        name=name,
    )(*args)


def reversed_bits(value, count):
    out = jnp.zeros_like(value)
    bit = 1
    while bit < count:
        out = out * 2 + (value // bit) % 2
        bit *= 2
    return out


def places(owner, panel, panel_tiles):
    nx = lax.axis_size("gx")
    ny = lax.axis_size("gy")
    chunk = panel_tiles // nx
    to_x = (panel // chunk) ^ lax.axis_index("gx")
    to_y = owner ^ lax.axis_index("gy")
    return (reversed_bits(to_x, nx) * ny + reversed_bits(to_y, ny)) * chunk + panel % chunk


def swap(send, axis, bit):
    return lax.ppermute(send, axis, [(i, i ^ bit) for i in range(lax.axis_size(axis))])


def bits_of(axis):
    return [1 << b for b in range(lax.axis_size(axis).bit_length() - 1)]


def reduce_chain(keep, send, shapes, me):
    gx_bits = bits_of("gx")
    for bit in gx_bits[:-1]:
        got = swap(send, "gx", bit)
        half = keep.shape[0] // 2
        send = keep[half:] + got[half:]
        keep = keep[:half] + got[:half]
    got = swap(send, "gx", gx_bits[-1])
    owners = lax.axis_size("gy")
    order = [sum(((r >> b) & 1) * (owners >> (b + 1)) for b in range(len(bits_of("gy")))) for r in range(owners)]
    half, parts, lanes = keep.shape[0] // 2, keep.shape[1], keep.shape[2]
    shape = (half + 1, parts, lanes)
    keep, send = local_call(
        functools.partial(combine_kernel, order), (shape, shape), "combine", me, keep, got, shapes, scalars=1
    )
    for bit in bits_of("gy"):
        got = swap(send, "gy", bit)
        tiles = keep.shape[0] - 1
        if bit * 2 == owners:
            outs = (keep.shape,)
        else:
            outs = ((tiles // 2 + 1, parts, lanes),) * 2
        keep, send = (local_call(fold_kernel, outs, "fold", keep, got) + (None,))[:2]
    return keep


def body(
    state,
    right_side,
    sigma,
    coupling,
    omega,
    pressure_coef,
    tile_cells,
    tile_owner,
    tile_panel,
    interp,
    correction,
    mode_shape,
):
    modes = omega.shape[0]
    parts = 2 * modes
    panel_tiles = correction.shape[0] // LANES
    me = lax.axis_index("gy").astype(jnp.int32)[None]
    quarter = mode_shape.shape[1] // lax.axis_size("gx")
    weighted = lax.dynamic_slice_in_dim(
        mode_shape * correction[None, :], lax.axis_index("gx") * quarter, quarter, 1
    )
    shapes = lax.all_gather(weighted, "gy", axis=0, tiled=True)
    place = places(tile_owner[:, 0], tile_panel[:, 0], panel_tiles)
    halo = exchange(pack(state, modes))
    field, *edges = sweep(False, coupling, omega, pressure_coef, state, right_side, sigma, halo)
    halo = exchange(edges)
    field, table = sweep(True, coupling, omega, pressure_coef, field, right_side, sigma, halo)
    keep, send = tile_sums(place, table, tile_cells, interp, panel_tiles * lax.axis_size("gy"), parts)
    chunk = reduce_chain(keep, send, shapes, me)
    total = lax.all_gather(chunk, "gx", axis=0, tiled=False)
    share = mode_shape.shape[0] // lax.axis_size("gy")
    panels, gaf = local_call(
        finish_kernel,
        ((parts, correction.shape[0]), (share, parts)),
        "finish",
        me,
        total,
        scratch=(pltpu.VMEM((LANES, parts), F32),),
        scalars=1,
    )
    return (field, panels, gaf)


def solution(mesh):
    placed = (
        P(None, "gx", "gy"),
        P(None, "gx", "gy"),
        P("gx", "gy"),
        P(),
        P(),
        P(),
        P(("gx", "gy"), None),
        P(("gx", "gy"), None),
        P(("gx", "gy"), None),
        P(("gx", "gy"), None, None),
        P("gy"),
        P(None, "gy"),
    )
    return jax.shard_map(
        body,
        mesh=mesh,
        in_specs=placed,
        out_specs=(P(None, "gx", "gy"), P(None, "gy"), P("gy", None)),
        check_vma=False,
    )
```

time: 388 us -> 127 us (0.33); the launches traced: 383 us -> 126 us
  local copies, waits for them, and re-layouts: 171 us -> 3.83 us
  other arithmetic: 48.7 us -> 1.66 us
  Pallas kernels: 0 us -> 44.2 us
  matrix products: 35.2 us -> 0 us
  waiting for transfers between devices: 58.1 us -> 26.3 us
  blocking collectives: 21.4 us -> 5.46 us
    gather x2 -> x0, local copies, waits for them, and re-layouts: 122 us -> none  [body(): jnp.take(press, tile_cells.reshape(-1), axis=1)]
    pallas_call x0 -> x9, Pallas kernels: none -> 44.2 us  [the longest x1 25.8 us: tile_sums(): pl.pallas_call(tile_kernel, grid=(tiles // block,), out_shape=(jax.ShapeD...]
    dot_general x7 -> x0, matrix products: 35.2 us -> none  [the longest x1 16.6 us: body(): jnp.einsum('qtc,tcp->tqp', surf, interp, precision=lax.Precision.HIGHEST)]
    add x10 -> x2, other arithmetic: 33.3 us -> 0.09 us  [the longest x1 0.05 us: reduce_chain(): send = keep[half:] + got[half:]]
    all_to_all x2 -> x0, waiting for transfers between devices: 29.9 us -> none  [the longest x1 29.9 us: body(): lax.all_to_all(send_buf, 'gy', split_axis=0, concat_axis=0, tiled=True)]
    psum x1 -> x0, waiting for transfers between devices: 24.4 us -> none  [body(): total = lax.psum(local, 'gx')]
    ppermute x8 -> x13, waiting for transfers between devices: 3.65 us -> 26.3 us  [the longest x5 17.3 us: swap(): lax.ppermute(send, axis, [(i, i ^ bit) for i in range(lax.axis_size(axis))])]
    unnamed x1 -> x0, blocking collectives: 21.4 us -> none
  transfers between devices with their start and end apart: 11 -> 14, of which waited for: 4 -> 9; matrix products, arithmetic and copies ran while one was open for 65% -> 0% of each run, Pallas kernels for 0% -> 34%
where the time goes in v1:
time: 127 us; the launch traced here: 126 us
  Pallas kernels  44.2 us (35%)
  starting transfers between devices  30.5 us (24%)
  waiting for transfers between devices  26.3 us (21%)
  between operations  14.3 us (11%)
  blocking collectives  5.46 us (4%)
  local copies, waits for them, and re-layouts  3.83 us (3%)
  other arithmetic  1.66 us (1%)
    pallas_call x1, Pallas kernels, tile_sums(): pl.pallas_call(tile_kernel, grid=(tiles // block,), out_shape=(jax.ShapeD...  25.8 us
    ppermute x5, waiting for transfers between devices, swap(): lax.ppermute(send, axis, [(i, i ^ bit) for i in range(lax.axis_size(axis))])  17.3 us
    pallas_call x2, Pallas kernels, sweep(): pl.pallas_call(functools.partial(sweep_kernel, last), grid=(modes,), out_...  15.5 us
    ppermute x5, starting transfers between devices, swap(): lax.ppermute(send, axis, [(i, i ^ bit) for i in range(lax.axis_size(axis))])  11.3 us
    ppermute x2, starting transfers between devices, exchange(): west = lax.ppermute(right, 'gy', [(i, i + 1) for i in range(ny - 1)])  8.76 us
    ppermute x2, waiting for transfers between devices, exchange(): east = lax.ppermute(left, 'gy', [(i + 1, i) for i in range(ny - 1)])  8.28 us
    all_gather x1, blocking collectives, body(): total = lax.all_gather(chunk, 'gx', axis=0, tiled=False)  5.46 us
    ppermute x2, starting transfers between devices, exchange(): above = lax.ppermute(down, 'gx', [(i, i + 1) for i in range(nx - 1)])  5.24 us
  transfers between devices with their start and end apart: 14, of which 9 were waited for; matrix products, arithmetic and copies ran while one was open for 0% of the time, Pallas kernels for 34%

profile of v1, /device:TPU:0, one launch (start us, length us, event | category | flops | bytes accessed | tf_op | source)
XLA Modules:
  0.0 126.2 jit_solution(2680628044424765452)
XLA Ops:
  7.3 0.7 dynamic-slice
  8.0 1.6 %dynamic-slice_multiply_fusion = f32[32,1024]{1,0:T(8,128)} fusion(f32[32,4096]{1,0:T(8,128)} %param.23, s32[]{:T(128)S(6)} %select_n.56, f32[1024]{0:T(1024)S(1)} %dynamic-slice), kind=kLoop, calls=%fused_computation.2 | loop fusion | flops 32768 | bytes 266244 | tf_op jit(solution)/shard_map/mul | solution.py:453
  9.6 1.9 %copy-done = f32[48,64,256]{2,1,0:T(8,128)S(1)} copy-done((f32[48,64,256]{2,1,0:T(8,128)S(1)}, f32[48,64,256]{2,1,0:T(8,128)}, u32[]{:S(2)}) %copy-start) | copy-done | bytes 3145752
  11.4 1.3 pack.1
  12.7 2.4 %collective-permute-start = (f32[4,12,256]{2,1,0:T(8,128)S(1)}, f32[4,12,256]{2,1,0:T(8,128)S(1)}, u32[]{:S(2)}, u32[]{:S(2)}) collective-permute-start(f32[4,12,256]{2,1,0:T(8,128)S(1)} %get-tuple-element.24), channel_id=1, source_target_pairs={{0,8},{8,16},{16,24},{1,9},{9,17},{17,25},{2,10},{10,18},{18,26},{... | collective-permute-start | bytes 147464 | tf_op jit(solution)/shard_map/ppermute | solution.py:188
  15.1 1.3 %collective-permute-start.1 = (f32[4,12,256]{2,1,0:T(8,128)S(1)}, f32[4,12,256]{2,1,0:T(8,128)S(1)}, u32[]{:S(2)}, u32[]{:S(2)}) collective-permute-start(f32[4,12,256]{2,1,0:T(8,128)S(1)} %get-tuple-element.25), channel_id=1, source_target_pairs={{8,0},{16,8},{24,16},{9,1},{17,9},{25,17},{10,2},{18,10},{26,18},{... | collective-permute-start | bytes 147464 | tf_op jit(solution)/shard_map/ppermute | solution.py:189
  16.4 4.3 %collective-permute-start.2 = (f32[64,128]{1,0:T(8,128)S(1)}, f32[64,128]{1,0:T(8,128)S(1)}, u32[]{:S(2)}, u32[]{:S(2)}) collective-permute-start(f32[64,128]{1,0:T(8,128)S(1)} %get-tuple-element.26), channel_id=1, source_target_pairs={{0,1},{1,2},{2,3},{3,4},{4,5},{5,6},{6,7},{8,9},{9,10},{10,11},{11... | collective-permute-start | bytes 98312 | tf_op jit(solution)/shard_map/ppermute | solution.py:190
  20.6 1.3 %collective-permute-start.3 = (f32[64,128]{1,0:T(8,128)S(1)}, f32[64,128]{1,0:T(8,128)S(1)}, u32[]{:S(2)}, u32[]{:S(2)}) collective-permute-start(f32[64,128]{1,0:T(8,128)S(1)} %get-tuple-element.27), channel_id=1, source_target_pairs={{1,0},{2,1},{3,2},{4,3},{5,4},{6,5},{7,6},{9,8},{10,9},{11,10},{12... | collective-permute-start | bytes 98312 | tf_op jit(solution)/shard_map/ppermute | solution.py:191
  22.0 0.4 collective-permute-done.2.west_ref
  22.4 4.0 %collective-permute-done.3.east_ref = f32[64,128]{1,0:T(8,128)S(1)} collective-permute-done((f32[64,128]{1,0:T(8,128)S(1)}, f32[64,128]{1,0:T(8,128)S(1)}, u32[]{:S(2)}, u32[]{:S(2)}) %collective-permute-start.3) | collective-permute-done | bytes 32800 | tf_op jit(solution)/shard_map/ppermute | solution.py:191
  26.5 7.8 %sweep.2 = (f32[48,64,256]{2,1,0:T(8,128)S(1)}, f32[4,12,256]{2,1,0:T(8,128)S(1)}, f32[4,12,256]{2,1,0:T(8,128)S(1)}, f32[64,128]{1,0:T(8,128)S(1)}, f32[64,128]{1,0:T(8,128)S(1)}) custom-call(f32[6,6]{1,0:T(8,128)S(1)} %copy-done.4, f32[4]{0:T(128)S(1)} %copy-done.5, f32[6]{0:T(128)S(1)} %copy-done.6, f32[48,64,256]{2,1,0:T(8,128)} %state_ref.3, ...), custom_call_target="tpu_custom_call" | custom-call | tf_op jit(solution)/shard_map/sweep/pallas_call | solution.py:207
  34.3 2.9 %collective-permute-start.4 = (f32[4,12,256]{2,1,0:T(8,128)S(1)}, f32[4,12,256]{2,1,0:T(8,128)S(1)}, u32[]{:S(2)}, u32[]{:S(2)}) collective-permute-start(f32[4,12,256]{2,1,0:T(8,128)S(1)} %get-tuple-element.29), channel_id=1, source_target_pairs={{0,8},{8,16},{16,24},{1,9},{9,17},{17,25},{2,10},{10,18},{18,26},{... | collective-permute-start | bytes 147464 | tf_op jit(solution)/shard_map/ppermute | solution.py:188
  37.2 1.3 %collective-permute-start.5 = (f32[4,12,256]{2,1,0:T(8,128)S(1)}, f32[4,12,256]{2,1,0:T(8,128)S(1)}, u32[]{:S(2)}, u32[]{:S(2)}) collective-permute-start(f32[4,12,256]{2,1,0:T(8,128)S(1)} %get-tuple-element.30), channel_id=1, source_target_pairs={{8,0},{16,8},{24,16},{9,1},{17,9},{25,17},{10,2},{18,10},{26,18},{... | collective-permute-start | bytes 147464 | tf_op jit(solution)/shard_map/ppermute | solution.py:189
  38.5 4.5 %collective-permute-start.6 = (f32[64,128]{1,0:T(8,128)S(1)}, f32[64,128]{1,0:T(8,128)S(1)}, u32[]{:S(2)}, u32[]{:S(2)}) collective-permute-start(f32[64,128]{1,0:T(8,128)S(1)} %get-tuple-element.31), channel_id=1, source_target_pairs={{0,1},{1,2},{2,3},{3,4},{4,5},{5,6},{6,7},{8,9},{9,10},{10,11},{11... | collective-permute-start | bytes 98312 | tf_op jit(solution)/shard_map/ppermute | solution.py:190
  43.0 1.3 %collective-permute-start.7 = (f32[64,128]{1,0:T(8,128)S(1)}, f32[64,128]{1,0:T(8,128)S(1)}, u32[]{:S(2)}, u32[]{:S(2)}) collective-permute-start(f32[64,128]{1,0:T(8,128)S(1)} %get-tuple-element.32), channel_id=1, source_target_pairs={{1,0},{2,1},{3,2},{4,3},{5,4},{6,5},{7,6},{9,8},{10,9},{11,10},{12... | collective-permute-start | bytes 98312 | tf_op jit(solution)/shard_map/ppermute | solution.py:191
  44.6 4.2 %collective-permute-done.7.east_ref = f32[64,128]{1,0:T(8,128)S(1)} collective-permute-done((f32[64,128]{1,0:T(8,128)S(1)}, f32[64,128]{1,0:T(8,128)S(1)}, u32[]{:S(2)}, u32[]{:S(2)}) %collective-permute-start.7) | collective-permute-done | bytes 32800 | tf_op jit(solution)/shard_map/ppermute | solution.py:191
  48.8 7.7 %sweep.3 = (f32[48,64,256]{2,1,0:T(8,128)}, bf16[1024,256]{1,0:T(8,128)(2,1)S(1)}) custom-call(f32[6,6]{1,0:T(8,128)S(1)} %copy-done.4, f32[4]{0:T(128)S(1)} %copy-done.5, f32[6]{0:T(128)S(1)} %copy-done.6, f32[48,64,256]{2,1,0:T(8,128)S(1)} %get-tuple-element.28.state_ref, f32[48,64,256]{2,1,0:T(8,128)} %rhs_ref.3, f32[64,256]{1,0:T(8,128)S(1)} %copy-done.2, ...), custom_call_target="tpu_custom_call" | custom-call | tf_op jit(solution)/shard_map/sweep/pallas_call | solution.py:207
  56.5 25.8 %tiles.1 = (f32[128,8,128]{2,1,0:T(8,128)S(1)}, f32[128,8,128]{2,1,0:T(8,128)S(1)}) custom-call(s32[256]{0:T(256)S(1)} %fusion.6.place_ref, bf16[1024,256]{1,0:T(8,128)(2,1)S(1)} %get-tuple-element.34.table_ref, s32[256,128]{1,0:T(8,128)S(1)} %copy-done.3, f32[256,128,128]{2,1,0:T(8,128)} %interp_ref.1), custom_call_target="tpu_custom_call" | custom-call | tf_op jit(solution)/shard_map/tiles/pallas_call | solution.py:296
  82.4 2.9 %collective-permute-start.8 = (f32[128,8,128]{2,1,0:T(8,128)S(1)}, f32[128,8,128]{2,1,0:T(8,128)S(1)}, u32[]{:S(2)}, u32[]{:S(2)}) collective-permute-start(f32[128,8,128]{2,1,0:T(8,128)S(1)} %get-tuple-element.36), channel_id=1, source_target_pairs={{0,8},{8,0},{16,24},{24,16},{1,9},{9,1},{17,25},{25,17},{2,10},{10... | collective-permute-start | bytes 1572872 | tf_op jit(solution)/shard_map/ppermute | solution.py:400
  85.3 1.5 %collective-permute-done.8 = f32[128,8,128]{2,1,0:T(8,128)S(1)} collective-permute-done((f32[128,8,128]{2,1,0:T(8,128)S(1)}, f32[128,8,128]{2,1,0:T(8,128)S(1)}, u32[]{:S(2)}, u32[]{:S(2)}) %collective-permute-start.8) | collective-permute-done | bytes 524320 | tf_op jit(solution)/shard_map/ppermute | solution.py:400
  86.9 3.1 %collective-permute-start.9 = (f32[64,8,128]{2,1,0:T(8,128)S(1)}, f32[64,8,128]{2,1,0:T(8,128)S(1)}, u32[]{:S(2)}, u32[]{:S(2)}) collective-permute-start(f32[64,8,128]{2,1,0:T(8,128)S(1)} %get-tuple-element.45), channel_id=1, source_target_pairs={{0,16},{8,24},{16,0},{24,8},{1,17},{9,25},{17,1},{25,9},{2,18},{10... | collective-permute-start | bytes 786440 | tf_op jit(solution)/shard_map/ppermute | solution.py:400
  90.0 6.6 %collective-permute-done.9.got_ref = f32[64,8,128]{2,1,0:T(8,128)S(1)} collective-permute-done((f32[64,8,128]{2,1,0:T(8,128)S(1)}, f32[64,8,128]{2,1,0:T(8,128)S(1)}, u32[]{:S(2)}, u32[]{:S(2)}) %collective-permute-start.9) | collective-permute-done | bytes 262176 | tf_op jit(solution)/shard_map/ppermute | solution.py:400
  96.6 1.2 copy-done.1
  97.9 0.9 combine.1
  98.8 1.2 collective-permute-start.10
  100.0 3.9 %collective-permute-done.10.got_ref = f32[33,8,128]{2,1,0:T(8,128)S(1)} collective-permute-done((f32[33,8,128]{2,1,0:T(8,128)S(1)}, f32[33,8,128]{2,1,0:T(8,128)S(1)}, u32[]{:S(2)}, u32[]{:S(2)}) %collective-permute-start.10) | collective-permute-done | bytes 135200 | tf_op jit(solution)/shard_map/ppermute | solution.py:400
  103.9 1.6 %collective-permute-start.11 = (f32[17,8,128]{2,1,0:T(8,128)S(1)}, f32[17,8,128]{2,1,0:T(8,128)S(1)}, u32[]{:S(2)}, u32[]{:S(2)}) collective-permute-start(f32[17,8,128]{2,1,0:T(8,128)S(1)} %get-tuple-element.40), channel_id=1, source_target_pairs={{0,2},{1,3},{2,0},{3,1},{4,6},{5,7},{6,4},{7,5},{8,10},{9,11},{10,... | collective-permute-start | bytes 208904 | tf_op jit(solution)/shard_map/ppermute | solution.py:400
  105.5 2.8 %collective-permute-done.11.got_ref = f32[17,8,128]{2,1,0:T(8,128)S(1)} collective-permute-done((f32[17,8,128]{2,1,0:T(8,128)S(1)}, f32[17,8,128]{2,1,0:T(8,128)S(1)}, u32[]{:S(2)}, u32[]{:S(2)}) %collective-permute-start.11) | collective-permute-done | bytes 69664 | tf_op jit(solution)/shard_map/ppermute | solution.py:400
  108.3 2.4 %collective-permute-start.12 = (f32[9,8,128]{2,1,0:T(8,128)S(1)}, f32[9,8,128]{2,1,0:T(8,128)S(1)}, u32[]{:S(2)}, u32[]{:S(2)}) collective-permute-start(f32[9,8,128]{2,1,0:T(8,128)S(1)} %get-tuple-element.42), channel_id=1, source_target_pairs={{0,4},{1,5},{2,6},{3,7},{4,0},{5,1},{6,2},{7,3},{8,12},{9,13},{10,... | collective-permute-start | bytes 110600 | tf_op jit(solution)/shard_map/ppermute | solution.py:400
  110.7 2.5 %collective-permute-done.12.got_ref = f32[9,8,128]{2,1,0:T(8,128)S(1)} collective-permute-done((f32[9,8,128]{2,1,0:T(8,128)S(1)}, f32[9,8,128]{2,1,0:T(8,128)S(1)}, u32[]{:S(2)}, u32[]{:S(2)}) %collective-permute-start.12) | collective-permute-done | bytes 36896 | tf_op jit(solution)/shard_map/ppermute | solution.py:400
  113.2 5.5 %all-gather = f32[36,8,128]{2,1,0:T(8,128)S(1)} all-gather(f32[9,8,128]{2,1,0:T(8,128)S(1)} %fold.5), channel_id=2, replica_groups=mesh['gx'=4,'gy'=8] {'gx'}, dimensions={0}, use_global_device_ids=true | all-gather | bytes 184320 | tf_op jit(solution)/shard_map/all_gather | solution.py:463
  118.7 0.7 finish.1
  (30 shorter events, 0.5 us)
Async XLA Ops:
  7.2 14.8 %copy-start.8 = (s32[256,1]{0,1:T(1,128)S(1)}, s32[256,1]{0,1:T(1,128)}, u32[]{:S(2)}) copy-start(s32[256,1]{0,1:T(1,128)} %param.19) | copy-start | bytes 3076
  7.2 19.3 %copy-start.2 = (f32[64,256]{1,0:T(8,128)S(1)}, f32[64,256]{1,0:T(8,128)}, u32[]{:S(2)}) copy-start(f32[64,256]{1,0:T(8,128)} %sigma_ref.3) | copy-start | bytes 196612
  7.2 19.3 %copy-start.4 = (f32[6,6]{1,0:T(8,128)S(1)}, f32[6,6]{1,0:T(8,128)}, u32[]{:S(2)}) copy-start(f32[6,6]{1,0:T(8,128)} %coupling_ref.3) | copy-start | bytes 436
  7.2 19.3 %copy-start.5 = (f32[4]{0:T(128)S(1)}, f32[4]{0:T(128)}, u32[]{:S(2)}) copy-start(f32[4]{0:T(128)} %omega_ref.3) | copy-start | bytes 52
  7.2 19.3 %copy-start.6 = (f32[6]{0:T(128)S(1)}, f32[6]{0:T(128)}, u32[]{:S(2)}) copy-start(f32[6]{0:T(128)} %coef_ref.3) | copy-start | bytes 76
  7.2 89.4 %all-gather.3.cloned.1.call-start = ((), (), s32[]{:S(2)}) async-start(), calls=%async_computation | async-start | bytes 1179648 | tf_op jit(solution)/shard_map/all_gather | solution.py:455
  9.6 1.9 %copy-start = (f32[48,64,256]{2,1,0:T(8,128)S(1)}, f32[48,64,256]{2,1,0:T(8,128)}, u32[]{:S(2)}) copy-start(f32[48,64,256]{2,1,0:T(8,128)} %state_ref.3) | copy-start | bytes 9437188
  12.7 13.7 %collective-permute-start = (f32[4,12,256]{2,1,0:T(8,128)S(1)}, f32[4,12,256]{2,1,0:T(8,128)S(1)}, u32[]{:S(2)}, u32[]{:S(2)}) collective-permute-start(f32[4,12,256]{2,1,0:T(8,128)S(1)} %get-tuple-element.24), channel_id=1, source_target_pairs={{0,8},{8,16},{16,24},{1,9},{9,17},{17,25},{2,10},{10,18},{18,26},{... | collective-permute-start | bytes 147464 | tf_op jit(solution)/shard_map/ppermute | solution.py:188
  15.1 11.4 %collective-permute-start.1 = (f32[4,12,256]{2,1,0:T(8,128)S(1)}, f32[4,12,256]{2,1,0:T(8,128)S(1)}, u32[]{:S(2)}, u32[]{:S(2)}) collective-permute-start(f32[4,12,256]{2,1,0:T(8,128)S(1)} %get-tuple-element.25), channel_id=1, source_target_pairs={{8,0},{16,8},{24,16},{9,1},{17,9},{25,17},{10,2},{18,10},{26,18},{... | collective-permute-start | bytes 147464 | tf_op jit(solution)/shard_map/ppermute | solution.py:189
  16.4 6.0 %collective-permute-start.2 = (f32[64,128]{1,0:T(8,128)S(1)}, f32[64,128]{1,0:T(8,128)S(1)}, u32[]{:S(2)}, u32[]{:S(2)}) collective-permute-start(f32[64,128]{1,0:T(8,128)S(1)} %get-tuple-element.26), channel_id=1, source_target_pairs={{0,1},{1,2},{2,3},{3,4},{4,5},{5,6},{6,7},{8,9},{9,10},{10,11},{11... | collective-permute-start | bytes 98312 | tf_op jit(solution)/shard_map/ppermute | solution.py:190
  20.6 5.8 %collective-permute-start.3 = (f32[64,128]{1,0:T(8,128)S(1)}, f32[64,128]{1,0:T(8,128)S(1)}, u32[]{:S(2)}, u32[]{:S(2)}) collective-permute-start(f32[64,128]{1,0:T(8,128)S(1)} %get-tuple-element.27), channel_id=1, source_target_pairs={{1,0},{2,1},{3,2},{4,3},{5,4},{6,5},{7,6},{9,8},{10,9},{11,10},{12... | collective-permute-start | bytes 98312 | tf_op jit(solution)/shard_map/ppermute | solution.py:191
  22.0 22.3 %copy-start.7 = (s32[256,1]{0,1:T(1,128)S(1)}, s32[256,1]{0,1:T(1,128)}, u32[]{:S(2)}) copy-start(s32[256,1]{0,1:T(1,128)} %param.20) | copy-start | bytes 3076
  34.3 14.5 %collective-permute-start.4 = (f32[4,12,256]{2,1,0:T(8,128)S(1)}, f32[4,12,256]{2,1,0:T(8,128)S(1)}, u32[]{:S(2)}, u32[]{:S(2)}) collective-permute-start(f32[4,12,256]{2,1,0:T(8,128)S(1)} %get-tuple-element.29), channel_id=1, source_target_pairs={{0,8},{8,16},{16,24},{1,9},{9,17},{17,25},{2,10},{10,18},{18,26},{... | collective-permute-start | bytes 147464 | tf_op jit(solution)/shard_map/ppermute | solution.py:188
  37.2 11.6 %collective-permute-start.5 = (f32[4,12,256]{2,1,0:T(8,128)S(1)}, f32[4,12,256]{2,1,0:T(8,128)S(1)}, u32[]{:S(2)}, u32[]{:S(2)}) collective-permute-start(f32[4,12,256]{2,1,0:T(8,128)S(1)} %get-tuple-element.30), channel_id=1, source_target_pairs={{8,0},{16,8},{24,16},{9,1},{17,9},{25,17},{10,2},{18,10},{26,18},{... | collective-permute-start | bytes 147464 | tf_op jit(solution)/shard_map/ppermute | solution.py:189
  38.5 6.1 %collective-permute-start.6 = (f32[64,128]{1,0:T(8,128)S(1)}, f32[64,128]{1,0:T(8,128)S(1)}, u32[]{:S(2)}, u32[]{:S(2)}) collective-permute-start(f32[64,128]{1,0:T(8,128)S(1)} %get-tuple-element.31), channel_id=1, source_target_pairs={{0,1},{1,2},{2,3},{3,4},{4,5},{5,6},{6,7},{8,9},{9,10},{10,11},{11... | collective-permute-start | bytes 98312 | tf_op jit(solution)/shard_map/ppermute | solution.py:190
  43.0 5.8 %collective-permute-start.7 = (f32[64,128]{1,0:T(8,128)S(1)}, f32[64,128]{1,0:T(8,128)S(1)}, u32[]{:S(2)}, u32[]{:S(2)}) collective-permute-start(f32[64,128]{1,0:T(8,128)S(1)} %get-tuple-element.32), channel_id=1, source_target_pairs={{1,0},{2,1},{3,2},{4,3},{5,4},{6,5},{7,6},{9,8},{10,9},{11,10},{12... | collective-permute-start | bytes 98312 | tf_op jit(solution)/shard_map/ppermute | solution.py:191
  48.8 7.7 %copy-start.3 = (s32[256,128]{1,0:T(8,128)S(1)}, s32[256,128]{1,0:T(8,128)}, u32[]{:S(2)}) copy-start(s32[256,128]{1,0:T(8,128)} %cells_ref.1) | copy-start | bytes 393220
  82.4 4.5 %collective-permute-start.8 = (f32[128,8,128]{2,1,0:T(8,128)S(1)}, f32[128,8,128]{2,1,0:T(8,128)S(1)}, u32[]{:S(2)}, u32[]{:S(2)}) collective-permute-start(f32[128,8,128]{2,1,0:T(8,128)S(1)} %get-tuple-element.36), channel_id=1, source_target_pairs={{0,8},{8,0},{16,24},{24,16},{1,9},{9,1},{17,25},{25,17},{2,10},{10... | collective-permute-start | bytes 1572872 | tf_op jit(solution)/shard_map/ppermute | solution.py:400
  86.9 9.7 %collective-permute-start.9 = (f32[64,8,128]{2,1,0:T(8,128)S(1)}, f32[64,8,128]{2,1,0:T(8,128)S(1)}, u32[]{:S(2)}, u32[]{:S(2)}) collective-permute-start(f32[64,8,128]{2,1,0:T(8,128)S(1)} %get-tuple-element.45), channel_id=1, source_target_pairs={{0,16},{8,24},{16,0},{24,8},{1,17},{9,25},{17,1},{25,9},{2,18},{10... | collective-permute-start | bytes 786440 | tf_op jit(solution)/shard_map/ppermute | solution.py:400
  96.6 1.2 copy-start.1
  98.8 5.1 %collective-permute-start.10 = (f32[33,8,128]{2,1,0:T(8,128)S(1)}, f32[33,8,128]{2,1,0:T(8,128)S(1)}, u32[]{:S(2)}, u32[]{:S(2)}) collective-permute-start(f32[33,8,128]{2,1,0:T(8,128)S(1)} %get-tuple-element.38), channel_id=1, source_target_pairs={{0,1},{1,0},{2,3},{3,2},{4,5},{5,4},{6,7},{7,6},{8,9},{9,8},{10,11... | collective-permute-start | bytes 405512 | tf_op jit(solution)/shard_map/ppermute | solution.py:400
  103.9 4.4 %collective-permute-start.11 = (f32[17,8,128]{2,1,0:T(8,128)S(1)}, f32[17,8,128]{2,1,0:T(8,128)S(1)}, u32[]{:S(2)}, u32[]{:S(2)}) collective-permute-start(f32[17,8,128]{2,1,0:T(8,128)S(1)} %get-tuple-element.40), channel_id=1, source_target_pairs={{0,2},{1,3},{2,0},{3,1},{4,6},{5,7},{6,4},{7,5},{8,10},{9,11},{10,... | collective-permute-start | bytes 208904 | tf_op jit(solution)/shard_map/ppermute | solution.py:400
  108.3 4.9 %collective-permute-start.12 = (f32[9,8,128]{2,1,0:T(8,128)S(1)}, f32[9,8,128]{2,1,0:T(8,128)S(1)}, u32[]{:S(2)}, u32[]{:S(2)}) collective-permute-start(f32[9,8,128]{2,1,0:T(8,128)S(1)} %get-tuple-element.42), channel_id=1, source_target_pairs={{0,4},{1,5},{2,6},{3,7},{4,0},{5,1},{6,2},{7,3},{8,12},{9,13},{10,... | collective-permute-start | bytes 110600 | tf_op jit(solution)/shard_map/ppermute | solution.py:400
Sparse Core Ops, SparseCore 0:
  10.7 42.9 all-gather.2

commit v2 on v1

--- a/solution.py
+++ b/solution.py
@@ -10,8 +10,11 @@
 F32 = jnp.float32
 BF16 = jnp.bfloat16
 LANES = 128
-BLOCK_TILES = 16
-VMEM_LIMIT = 48 << 20
+BLOCK_TILES = 32
+LANE_TILES = 10
+VMEM_LIMIT = 40 << 20
+VMEM_ALL = 60 << 20
+VMEM_SMALL = 12 << 20
 
 
 def vmem():
@@ -22,19 +25,29 @@
     return pl.BlockSpec(memory_space=pltpu.SMEM)
 
 
-def pack_edges(field_ref, first, planes, up_ref, down_ref, left_ref, right_ref):
+def pack_edges(field_ref, first, planes, row1_ref, row2_ref, col1_ref, col2_ref):
     rows, cols = field_ref.shape[1:]
+    even_x = lax.rem(lax.axis_index("gx"), 2) == 0
+    even_y = lax.rem(lax.axis_index("gy"), 2) == 0
     lane = lax.broadcasted_iota(jnp.int32, (rows, LANES), 1)
-    left = left_ref[...]
-    right = right_ref[...]
+    left = jnp.where(even_y, col2_ref[...], col1_ref[...])
+    right = jnp.where(even_y, col1_ref[...], col2_ref[...])
     for k in range(planes):
-        up_ref[0, k : k + 1, :] = field_ref[k, 0:1, :]
-        down_ref[0, k : k + 1, :] = field_ref[k, rows - 1 : rows, :]
+        row1_ref[0, k : k + 1, :] = field_ref[k, 0:1, :]
+        row2_ref[0, k : k + 1, :] = field_ref[k, rows - 1 : rows, :]
         here = lane == first + k
         left = jnp.where(here, field_ref[k, :, 0:1], left)
         right = jnp.where(here, field_ref[k, :, cols - 1 : cols], right)
-    left_ref[...] = left
-    right_ref[...] = right
+    col1_ref[...] = jnp.where(even_y, right, left)
+    col2_ref[...] = jnp.where(even_y, left, right)
+    up = row1_ref[0]
+    down = row2_ref[0]
+    row1_ref[0] = jnp.where(even_x, down, up)
+    row2_ref[0] = jnp.where(even_x, up, down)
+
+
+def weigh_kernel(mine_ref, shape_ref, correction_ref, weighted_ref):
+    weighted_ref[...] = shape_ref[...] * correction_ref[...]
 
 
 def pack_kernel(state_ref, up_ref, down_ref, left_ref, right_ref):
@@ -57,14 +70,16 @@
     state_ref,
     rhs_ref,
     sigma_ref,
-    above_ref,
-    below_ref,
-    west_ref,
-    east_ref,
+    row1_ref,
+    row2_ref,
+    col1_ref,
+    col2_ref,
     new_ref,
     *rest,
 ):
-    nbs_ref, a_ref, b_ref, press_ref = rest[-4:]
+    nbs_ref, a_ref, b_ref = rest[-3:]
+    if last:
+        table_ref, press_ref = rest[:2]
     mode = pl.program_id(0)
     planes, rows, cols = state_ref.shape
     nvar = planes // 2
@@ -75,17 +90,23 @@
     a_ref[...] = dval * scale
     b_ref[...] = freq * scale
 
+    even_x = lax.rem(lax.axis_index("gx"), 2) == 0
+    even_y = lax.rem(lax.axis_index("gy"), 2) == 0
+    above_rows = jnp.where(even_x, row2_ref[0], row1_ref[0])
+    below_rows = jnp.where(even_x, row1_ref[0], row2_ref[0])
+    west_cols = jnp.where(even_y, col2_ref[...], col1_ref[...])
+    east_cols = jnp.where(even_y, col1_ref[...], col2_ref[...])
     row = lax.broadcasted_iota(jnp.int32, (rows, cols), 0)
     lane = lax.broadcasted_iota(jnp.int32, (rows, LANES), 1)
     for k in range(planes):
         comp = mode * planes + k
         plane = state_ref[k]
-        total = jnp.where(row == 0, above_ref[0, k : k + 1, :], pltpu.roll(plane, 1, 0))
+        total = jnp.where(row == 0, above_rows[k : k + 1], pltpu.roll(plane, 1, 0))
         total = total + jnp.where(
-            row == rows - 1, below_ref[0, k : k + 1, :], pltpu.roll(plane, rows - 1, 0)
+            row == rows - 1, below_rows[k : k + 1], pltpu.roll(plane, rows - 1, 0)
         )
-        west = pltpu.roll(west_ref[...], lax.rem(LANES - comp, LANES), 1)
-        east = pltpu.roll(east_ref[...], LANES - 1 - comp, 1)
+        west = pltpu.roll(west_cols, lax.rem(LANES - comp, LANES), 1)
+        east = pltpu.roll(east_cols, LANES - 1 - comp, 1)
         from_west = pltpu.roll(plane, 1, 1)
         from_east = pltpu.roll(plane, cols - 1, 1)
         nbs_ref[k, :, :LANES] = (
@@ -131,7 +152,6 @@
 
     lax.fori_loop(0, rows // 8, strip, 0)
     if last:
-        table_ref = rest[0]
 
         @pl.when(mode == pl.num_programs(0) - 1)
         def _():
@@ -164,6 +184,27 @@
     row_spec = pl.BlockSpec((1, planes, cols), lambda m: (m, 0, 0))
     col_spec = pl.BlockSpec((rows, LANES), lambda m: (0, 0))
     return shapes, (row_spec, row_spec, col_spec, col_spec)
+
+
+def weigh(mode_shape, correction):
+    count, panels = mode_shape.shape
+    share = panels // lax.axis_size("gx")
+    mine = lax.axis_index("gx").astype(jnp.int32)[None]
+    return pl.pallas_call(
+        weigh_kernel,
+        grid_spec=pltpu.PrefetchScalarGridSpec(
+            num_scalar_prefetch=1,
+            grid=(1,),
+            in_specs=[
+                pl.BlockSpec((count, share), lambda g, at: (0, at[0])),
+                pl.BlockSpec((1, share), lambda g, at: (0, at[0])),
+            ],
+            out_specs=pl.BlockSpec((count, share), lambda g, at: (0, 0)),
+        ),
+        out_shape=jax.ShapeDtypeStruct((count, share), F32),
+        compiler_params=pltpu.CompilerParams(vmem_limit_bytes=VMEM_ALL),
+        name="weigh",
+    )(mine, mode_shape, correction[None, :])
 
 
 def pack(state, modes):
@@ -182,14 +223,13 @@
 
 
 def exchange(edges):
-    up, down, left, right = edges
-    nx = lax.axis_size("gx")
-    ny = lax.axis_size("gy")
-    above = lax.ppermute(down, "gx", [(i, i + 1) for i in range(nx - 1)])
-    below = lax.ppermute(up, "gx", [(i + 1, i) for i in range(nx - 1)])
-    west = lax.ppermute(right, "gy", [(i, i + 1) for i in range(ny - 1)])
-    east = lax.ppermute(left, "gy", [(i + 1, i) for i in range(ny - 1)])
-    return above, below, west, east
+    got = []
+    for axis, first, second in (("gx", edges[0], edges[1]), ("gy", edges[2], edges[3])):
+        count = lax.axis_size(axis)
+        got.append(swap(first, axis, 1))
+        pairs = [(i, i + 1) for i in range(1, count - 1, 2)]
+        got.append(lax.ppermute(second, axis, pairs + [(b, a) for a, b in pairs]))
+    return got
 
 
 def sweep(last, coupling, omega, coef, field, rhs, sigma, halo):
@@ -200,8 +240,9 @@
     block = pl.BlockSpec((planes, rows, cols), lambda m: (m, 0, 0))
     if last:
         table = (4 * modes * rows, cols)
-        extra = (jax.ShapeDtypeStruct(table, BF16),)
-        extra_specs = (pl.BlockSpec(table, lambda m: (0, 0)),)
+        press = (cols // LANES, 2 * modes * rows, LANES)
+        extra = (jax.ShapeDtypeStruct(table, BF16), jax.ShapeDtypeStruct(press, F32))
+        extra_specs = (pl.BlockSpec(table, lambda m: (0, 0)), pl.BlockSpec(press, lambda m: (0, 0, 0)))
     else:
         extra, extra_specs = edges, edge_specs
     return pl.pallas_call(
@@ -222,14 +263,14 @@
             pltpu.VMEM((planes, rows, cols), F32),
             pltpu.VMEM((rows, cols), F32),
             pltpu.VMEM((rows, cols), F32),
-            pltpu.VMEM((cols // LANES, 2 * modes * rows if last else 8, LANES), F32),
         ],
         compiler_params=pltpu.CompilerParams(vmem_limit_bytes=VMEM_LIMIT),
+        cost_estimate=pl.CostEstimate(flops=8 * 10**9, bytes_accessed=12 * field.size, transcendentals=0),
         name="sweep",
     )(coupling, omega, coef, field, rhs, sigma, *halo)
 
 
-def tile_kernel(place_ref, table_ref, cells_ref, interp_ref, keep_ref, send_ref, acc_ref):
+def tile_kernel(place_ref, table_ref, press_ref, cells_ref, interp_ref, keep_ref, send_ref, acc_ref):
     step = pl.program_id(0)
     block = cells_ref.shape[0]
     parts = acc_ref.shape[1]
@@ -246,8 +287,8 @@
     one = jnp.ones((), BF16)
     zero = jnp.zeros((), BF16)
     blank = jnp.zeros((2 * parts, LANES), F32)
-    surfs = []
-    for pair in range(block // 2):
+
+    def by_matmul(pair):
         cells = jnp.concatenate(
             [cells_ref[2 * pair : 2 * pair + 1, :], cells_ref[2 * pair + 1 : 2 * pair + 2, :]], axis=1
         )
@@ -260,7 +301,35 @@
         while bit:
             found = jnp.where(((row & bit) != 0)[None], found[bit:], found[:bit])
             bit //= 2
-        surfs.append(found[0])
+        return found[0]
+
+    halves = cols // LANES
+    lane_bits = LANES.bit_length() - 1
+
+    def by_lanes(tile):
+        cells = jnp.broadcast_to(cells_ref[tile : tile + 1, :], (parts, LANES))
+        lane = cells & (LANES - 1)
+        chosen = [(cells >> (lane_bits + b)) & 1 == 1 for b in range((rows * halves).bit_length() - 1)]
+
+        def among(base, bits):
+            if bits == 0:
+                at = base // halves * parts
+                return jnp.take_along_axis(press_ref[base % halves, at : at + parts, :], lane, axis=1)
+            low = among(base, bits - 1)
+            return jnp.where(chosen[bits - 1], among(base + (1 << (bits - 1)), bits - 1), low)
+
+        return among(0, len(chosen))
+
+    by_lane_count = LANE_TILES * block // BLOCK_TILES // 2 * 2
+    pairs = (block - by_lane_count) // 2
+    surfs = []
+    beside = []
+    for pair in range(pairs):
+        for tile in range(pair * by_lane_count // pairs, (pair + 1) * by_lane_count // pairs):
+            beside.append(by_lanes(block - by_lane_count + tile))
+        surfs.append(by_matmul(pair))
+    for pair in range(by_lane_count // 2):
+        surfs.append(jnp.concatenate(beside[2 * pair : 2 * pair + 2], axis=1))
     for pair, surf in enumerate(surfs):
         high = surf.astype(BF16).astype(F32)
         split = jnp.concatenate([high, surf - high], axis=0)
@@ -289,7 +358,7 @@
         send_ref[...] = acc_ref[half:]
 
 
-def tile_sums(place, table, cells, interp, panel_tiles, parts):
+def tile_sums(place, table, press, cells, interp, panel_tiles, parts):
     tiles = cells.shape[0]
     half = (panel_tiles // 2, parts, LANES)
     block = min(BLOCK_TILES, tiles)
@@ -300,70 +369,68 @@
         in_specs=[
             smem(),
             pl.BlockSpec(table.shape, lambda i: (0, 0)),
+            pl.BlockSpec(press.shape, lambda i: (0, 0, 0)),
             pl.BlockSpec((block, LANES), lambda i: (i, 0)),
             pl.BlockSpec((block, LANES, LANES), lambda i: (i, 0, 0)),
         ],
         out_specs=(pl.BlockSpec(half, lambda i: (0, 0, 0)), pl.BlockSpec(half, lambda i: (0, 0, 0))),
         scratch_shapes=[pltpu.VMEM((panel_tiles, parts, LANES), F32)],
         compiler_params=pltpu.CompilerParams(vmem_limit_bytes=VMEM_LIMIT),
+        cost_estimate=pl.CostEstimate(
+            flops=2 * table.size * cells.size, bytes_accessed=4 * interp.size, transcendentals=0
+        ),
         name="tiles",
-    )(place, table, cells, interp)
-
-
-def combine_kernel(order, me_ref, keep_ref, got_ref, shapes_ref, next_keep_ref, next_send_ref):
+    )(place, table, press, cells, interp)
+
+
+def combine_kernel(order, keep_ref, got_ref, shapes_ref, *out_refs):
     owners = len(order)
     chunk = keep_ref.shape[0] // owners
     parts = keep_ref.shape[1]
     modes = shapes_ref.shape[0] // owners
-    half = keep_ref.shape[0] // 2
+    tiles = out_refs[0].shape[0] - 1
     force = jnp.zeros((parts, modes), F32)
     for at, relative in enumerate(order):
-        lines = keep_ref[at * chunk : (at + 1) * chunk] + got_ref[at * chunk : (at + 1) * chunk]
         first = at * chunk
-        if first < half:
-            next_keep_ref[first : first + chunk] = lines
-        else:
-            next_send_ref[first - half : first - half + chunk] = lines
-        flat = jnp.concatenate([lines[k] for k in range(chunk)], axis=1)
-        owner = me_ref[0] ^ relative
-        shapes = shapes_ref[pl.ds(pl.multiple_of(owner * modes, 8), modes), :]
+        lines = keep_ref[first : first + chunk] + got_ref[first : first + chunk]
+        out_refs[first // tiles][first % tiles : first % tiles + chunk] = lines
         force = force + lax.dot_general(
-            flat,
-            shapes,
+            jnp.concatenate([lines[k] for k in range(chunk)], axis=1),
+            shapes_ref[relative * modes : (relative + 1) * modes, :],
             (((1,), (1,)), ((), ())),
             precision=lax.Precision.HIGHEST,
             preferred_element_type=F32,
         )
     tile = jnp.concatenate([force, jnp.zeros((parts, LANES - modes), F32)], axis=1)
-    next_keep_ref[half] = tile
-    next_send_ref[half] = tile
-
-
-def fold_kernel(keep_ref, got_ref, *next_refs):
-    total = keep_ref[...] + got_ref[...]
-    tiles = total.shape[0] - 1
-    if len(next_refs) == 1:
-        next_refs[0][...] = total
-    else:
-        half = tiles // 2
-        next_refs[0][:half] = total[:half]
-        next_refs[0][half] = total[tiles]
-        next_refs[1][...] = total[half:]
-
-
-def finish_kernel(me_ref, total_ref, panel_ref, gaf_ref, turned_ref):
-    rows, chunk, parts, lanes = total_ref.shape
+    for out_ref in out_refs:
+        out_ref[tiles] = tile
+
+
+def fold_kernel(count, *refs):
+    total = refs[0][...]
+    for ref in refs[1:count]:
+        total = total + ref[...]
+    tiles = refs[count].shape[0] - 1
+    for number, ref in enumerate(refs[count:]):
+        ref[:tiles] = total[number * tiles : (number + 1) * tiles]
+        ref[tiles] = total[total.shape[0] - 1]
+
+
+def finish_kernel(*refs):
+    *total_refs, panel_ref, gaf_ref, turned_ref = refs
+    chunk, parts, lanes = total_refs[0].shape
     chunk = chunk - 1
-    force = total_ref[0, chunk]
-    for i in range(rows):
+    here = lax.axis_index("gx")
+    force = total_refs[0][chunk]
+    for relative, total_ref in enumerate(total_refs):
+        first = (here ^ relative) * (chunk * lanes)
         for k in range(chunk):
-            at = (i * chunk + k) * lanes
-            panel_ref[:, at : at + lanes] = total_ref[i, k]
-        if i:
-            force = force + total_ref[i, chunk]
+            panel_ref[:, pl.ds(pl.multiple_of(first + k * lanes, lanes), lanes)] = total_ref[k]
+        if relative:
+            force = force + total_ref[chunk]
     turned_ref[...] = jnp.transpose(force)
     share = gaf_ref.shape[0]
-    gaf_ref[...] = turned_ref[pl.ds(me_ref[0] * share, share), :]
+    gaf_ref[...] = turned_ref[pl.ds(lax.axis_index("gy") * share, share), :]
 
 
 def local_call(kernel, shapes, name, *args, scratch=(), scalars=0):
@@ -373,7 +440,7 @@
         in_specs=[smem()] * scalars + [vmem()] * (len(args) - scalars),
         out_specs=tuple(vmem() for _ in shapes),
         scratch_shapes=list(scratch),
-        compiler_params=pltpu.CompilerParams(vmem_limit_bytes=VMEM_LIMIT),
+        compiler_params=pltpu.CompilerParams(vmem_limit_bytes=VMEM_SMALL),
         name=name,
     )(*args)
 
@@ -393,18 +460,41 @@
     chunk = panel_tiles // nx
     to_x = (panel // chunk) ^ lax.axis_index("gx")
     to_y = owner ^ lax.axis_index("gy")
-    return (reversed_bits(to_x, nx) * ny + reversed_bits(to_y, ny)) * chunk + panel % chunk
+    return (reversed_bits(to_x, nx) * ny + position(to_y, "gy")) * chunk + panel % chunk
 
 
 def swap(send, axis, bit):
     return lax.ppermute(send, axis, [(i, i ^ bit) for i in range(lax.axis_size(axis))])
 
 
+def gather_step(blocks, axis, bit):
+    held = sorted(blocks)
+    got = swap(jnp.concatenate([blocks[r] for r in held], axis=0), axis, bit)
+    return {**blocks, **{r ^ bit: block for r, block in zip(held, jnp.split(got, len(held), axis=0))}}
+
+
 def bits_of(axis):
     return [1 << b for b in range(lax.axis_size(axis).bit_length() - 1)]
 
 
-def reduce_chain(keep, send, shapes, me):
+def levels(axis):
+    found = []
+    base = 1
+    while base < lax.axis_size(axis):
+        size = min(4, lax.axis_size(axis) // base)
+        found.append((base, size))
+        base *= size
+    return found
+
+
+def position(relative, axis):
+    at = 0
+    for base, size in levels(axis):
+        at = at * size + relative // base % size
+    return at
+
+
+def reduce_panels(keep, send, shapes):
     gx_bits = bits_of("gx")
     for bit in gx_bits[:-1]:
         got = swap(send, "gx", bit)
@@ -413,21 +503,19 @@
         keep = keep[:half] + got[:half]
     got = swap(send, "gx", gx_bits[-1])
     owners = lax.axis_size("gy")
-    order = [sum(((r >> b) & 1) * (owners >> (b + 1)) for b in range(len(bits_of("gy")))) for r in range(owners)]
-    half, parts, lanes = keep.shape[0] // 2, keep.shape[1], keep.shape[2]
-    shape = (half + 1, parts, lanes)
-    keep, send = local_call(
-        functools.partial(combine_kernel, order), (shape, shape), "combine", me, keep, got, shapes, scalars=1
+    order = sorted(range(owners), key=lambda relative: position(relative, "gy"))
+    steps = levels("gy")
+    tiles = keep.shape[0] // steps[0][1]
+    lines = keep.shape[1:]
+    held = local_call(
+        functools.partial(combine_kernel, order), ((tiles + 1,) + lines,) * steps[0][1], "combine", keep, got, shapes
     )
-    for bit in bits_of("gy"):
-        got = swap(send, "gy", bit)
-        tiles = keep.shape[0] - 1
-        if bit * 2 == owners:
-            outs = (keep.shape,)
-        else:
-            outs = ((tiles // 2 + 1, parts, lanes),) * 2
-        keep, send = (local_call(fold_kernel, outs, "fold", keep, got) + (None,))[:2]
-    return keep
+    for number, (base, size) in enumerate(steps):
+        held = [held[0]] + [swap(held[r], "gy", base * r) for r in range(1, size)]
+        parts = steps[number + 1][1] if number + 1 < len(steps) else 1
+        tiles = tiles // parts
+        held = local_call(functools.partial(fold_kernel, size), ((tiles + 1,) + lines,) * parts, "fold", *held)
+    return held[0]
 
 
 def body(
@@ -447,29 +535,31 @@
     modes = omega.shape[0]
     parts = 2 * modes
     panel_tiles = correction.shape[0] // LANES
-    me = lax.axis_index("gy").astype(jnp.int32)[None]
-    quarter = mode_shape.shape[1] // lax.axis_size("gx")
-    weighted = lax.dynamic_slice_in_dim(
-        mode_shape * correction[None, :], lax.axis_index("gx") * quarter, quarter, 1
-    )
-    shapes = lax.all_gather(weighted, "gy", axis=0, tiled=True)
     place = places(tile_owner[:, 0], tile_panel[:, 0], panel_tiles)
     halo = exchange(pack(state, modes))
+    weighted = weigh(mode_shape, correction)
+    far = bits_of("gy")[::-1]
+    blocks = gather_step({0: weighted}, "gy", far[0])
     field, *edges = sweep(False, coupling, omega, pressure_coef, state, right_side, sigma, halo)
+    edges, blocks = lax.optimization_barrier((edges, blocks))
     halo = exchange(edges)
-    field, table = sweep(True, coupling, omega, pressure_coef, field, right_side, sigma, halo)
-    keep, send = tile_sums(place, table, tile_cells, interp, panel_tiles * lax.axis_size("gy"), parts)
-    chunk = reduce_chain(keep, send, shapes, me)
-    total = lax.all_gather(chunk, "gx", axis=0, tiled=False)
+    for bit in far[1:-1]:
+        blocks = gather_step(blocks, "gy", bit)
+    field, table, press = sweep(True, coupling, omega, pressure_coef, field, right_side, sigma, halo)
+    table, blocks = lax.optimization_barrier((table, blocks))
+    blocks = gather_step(blocks, "gy", far[-1])
+    shapes = jnp.concatenate([blocks[r] for r in sorted(blocks)], axis=0)
+    keep, send = tile_sums(place, table, press, tile_cells, interp, panel_tiles * lax.axis_size("gy"), parts)
+    send, shapes = lax.optimization_barrier((send, shapes))
+    chunk = reduce_panels(keep, send, shapes)
+    total = [chunk] + [swap(chunk, "gx", relative) for relative in range(1, lax.axis_size("gx"))]
     share = mode_shape.shape[0] // lax.axis_size("gy")
     panels, gaf = local_call(
         finish_kernel,
         ((parts, correction.shape[0]), (share, parts)),
         "finish",
-        me,
-        total,
+        *total,
         scratch=(pltpu.VMEM((LANES, parts), F32),),
-        scalars=1,
     )
     return (field, panels, gaf)
 

time: 127 us -> 96.7 us (0.76)
  between operations: 14.3 us -> 0.94 us
  waiting for transfers between devices: 26.3 us -> 19.4 us
  Pallas kernels: 44.2 us -> 38.2 us
  blocking collectives: 5.46 us -> 0 us
    ppermute x8 -> x4, starting transfers between devices: 19.2 us -> 2.61 us  [exchange(): got.append(lax.ppermute(second, axis, pairs + [(b, a) for a, b in pairs]))]
    ppermute x5 -> x16, starting transfers between devices: 11.3 us -> 27.7 us  [swap(): lax.ppermute(send, axis, [(i, i ^ bit) for i in range(lax.axis_size(axis))])]
    ppermute x8 -> x4, waiting for transfers between devices: 8.94 us -> 0.01 us  [exchange(): got.append(lax.ppermute(second, axis, pairs + [(b, a) for a, b in pairs]))]
    pallas_call x1, Pallas kernels: 25.8 us -> 19 us  [tile_sums(): pl.pallas_call(tile_kernel, grid=(tiles // block,), out_shape=(jax.ShapeD...]
    all_gather x1 -> x0, blocking collectives: 5.46 us -> none  [body(): total = lax.all_gather(chunk, 'gx', axis=0, tiled=False)]
    ppermute x5 -> x16, waiting for transfers between devices: 17.3 us -> 19.4 us  [swap(): lax.ppermute(send, axis, [(i, i ^ bit) for i in range(lax.axis_size(axis))])]
    concatenate x0 -> x2, other arithmetic: none -> 1.87 us  [gather_step(): got = swap(jnp.concatenate([blocks[r] for r in held], axis=0), axis, bit)]
    unnamed x18 -> x29, local copies, waits for them, and re-layouts: 3.14 us -> 4.79 us
  transfers between devices with their start and end apart: 14 -> 20, of which waited for: 9 -> 8; matrix products, arithmetic and copies ran while one was open for 0% -> 2% of each run, Pallas kernels for 34% -> 36%
where the time goes in v2:
time: 96.7 us; the launch traced here: 96.3 us
  Pallas kernels  38.2 us (40%)
  starting transfers between devices  30.3 us (31%)
  waiting for transfers between devices  19.4 us (20%)
  local copies, waits for them, and re-layouts  4.82 us (5%)
  other arithmetic  2.63 us (3%)
    ppermute x16, starting transfers between devices, swap(): lax.ppermute(send, axis, [(i, i ^ bit) for i in range(lax.axis_size(axis))])  27.7 us
    ppermute x16, waiting for transfers between devices, swap(): lax.ppermute(send, axis, [(i, i ^ bit) for i in range(lax.axis_size(axis))])  19.4 us
    pallas_call x1, Pallas kernels, tile_sums(): pl.pallas_call(tile_kernel, grid=(tiles // block,), out_shape=(jax.ShapeD...  19 us
    pallas_call x2, Pallas kernels, sweep(): pl.pallas_call(functools.partial(sweep_kernel, last), grid=(modes,), out_...  14.1 us
    unnamed x29, local copies, waits for them, and re-layouts  4.79 us
    ppermute x4, starting transfers between devices, exchange(): got.append(lax.ppermute(second, axis, pairs + [(b, a) for a, b in pairs]))  2.61 us
  transfers between devices with their start and end apart: 20, of which 8 were waited for; matrix products, arithmetic and copies ran while one was open for 2% of the time, Pallas kernels for 36%

profile of v2, /device:TPU:0, one launch (start us, length us, event | category | flops | bytes accessed | tf_op | source)
XLA Modules:
  0.0 96.3 jit_solution(9611866647168479715)
XLA Ops:
  0.6 1.9 %copy-done = f32[48,64,256]{2,1,0:T(8,128)S(1)} copy-done((f32[48,64,256]{2,1,0:T(8,128)S(1)}, f32[48,64,256]{2,1,0:T(8,128)}, u32[]{:S(2)}) %copy-start) | copy-done | bytes 3145752
  2.6 1.9 %pack.1 = (f32[4,12,256]{2,1,0:T(8,128)S(1)}, f32[4,12,256]{2,1,0:T(8,128)S(1)}, f32[64,128]{1,0:T(8,128)}, f32[64,128]{1,0:T(8,128)}) custom-call(f32[48,64,256]{2,1,0:T(8,128)S(1)} %copy-done), custom_call_target="tpu_custom_call" | custom-call | tf_op jit(solution)/shard_map/pack/pallas_call | solution.py:214
  5.6 2.6 %collective-permute-start.2 = (f32[64,128]{1,0:T(8,128)}, f32[64,128]{1,0:T(8,128)S(1)}, u32[]{:S(2)}, u32[]{:S(2)}) collective-permute-start(f32[64,128]{1,0:T(8,128)} %get-tuple-element.40), channel_id=1, source_target_pairs={{0,1},{1,0},{2,3},{3,2},{4,5},{5,4},{6,7},{7,6},{8,9},{9,8},{10,11... | collective-permute-start | bytes 98312 | tf_op jit(solution)/shard_map/ppermute | solution.py:467
  8.8 1.6 %weigh.1 = f32[32,1024]{1,0:T(8,128)} custom-call(s32[1]{0:T(128)} %bitcast.mine_ref, f32[32,4096]{1,0:T(8,128)} %shape_ref.1, f32[1,4096]{1,0:T(1,128)} %bitcast.4), custom_call_target="tpu_custom_call" | custom-call | tf_op jit(solution)/shard_map/weigh/pallas_call | solution.py:193
  10.4 4.2 %collective-permute-start.4 = (f32[32,1024]{1,0:T(8,128)}, f32[32,1024]{1,0:T(8,128)}, u32[]{:S(2)}, u32[]{:S(2)}) collective-permute-start(f32[32,1024]{1,0:T(8,128)} %weigh.1), channel_id=1, source_target_pairs={{0,4},{1,5},{2,6},{3,7},{4,0},{5,1},{6,2},{7,3},{8,12},{9,13},{10,... | collective-permute-start | bytes 393224 | tf_op jit(solution)/shard_map/ppermute | solution.py:467
  14.6 0.7 fusion.5.place_ref
  15.4 1.9 %copy-done.2 = f32[48,64,256]{2,1,0:T(8,128)S(1)} copy-done((f32[48,64,256]{2,1,0:T(8,128)S(1)}, f32[48,64,256]{2,1,0:T(8,128)}, u32[]{:S(2)}) %copy-start.2) | copy-done | bytes 3145752
  17.3 7.0 %sweep.2 = (f32[48,64,256]{2,1,0:T(8,128)S(1)}, f32[4,12,256]{2,1,0:T(8,128)S(1)}, f32[4,12,256]{2,1,0:T(8,128)S(1)}, f32[64,128]{1,0:T(8,128)S(1)}, f32[64,128]{1,0:T(8,128)S(1)}) custom-call(f32[6,6]{1,0:T(8,128)S(1)} %copy-done.6, f32[4]{0:T(128)S(1)} %copy-done.7, f32[6]{0:T(128)S(1)} %copy-done.8, f32[48,64,256]{2,1,0:T(8,128)S(1)} %copy-done.1, ...), custom_call_target="tpu_custom_call" | custom-call | flops 8000000000 | bytes 9437184 | tf_op jit(solution)/shard_map/sweep/pallas_call | solution.py:248
  24.4 2.1 %collective-permute-start.5 = (f32[4,12,256]{2,1,0:T(8,128)S(1)}, f32[4,12,256]{2,1,0:T(8,128)S(1)}, u32[]{:S(2)}, u32[]{:S(2)}) collective-permute-start(f32[4,12,256]{2,1,0:T(8,128)S(1)} %get-tuple-element.47), channel_id=1, source_target_pairs={{0,8},{8,0},{16,24},{24,16},{1,9},{9,1},{17,25},{25,17},{2,10},{10... | collective-permute-start | bytes 147464 | tf_op jit(solution)/shard_map/ppermute | solution.py:467
  27.1 2.7 %collective-permute-start.7 = (f32[64,128]{1,0:T(8,128)S(1)}, f32[64,128]{1,0:T(8,128)S(1)}, u32[]{:S(2)}, u32[]{:S(2)}) collective-permute-start(f32[64,128]{1,0:T(8,128)S(1)} %get-tuple-element.49), channel_id=1, source_target_pairs={{0,1},{1,0},{2,3},{3,2},{4,5},{5,4},{6,7},{7,6},{8,9},{9,8},{10,11... | collective-permute-start | bytes 98312 | tf_op jit(solution)/shard_map/ppermute | solution.py:467
  30.5 0.9 pad_maximum_fusion.1
  31.4 2.8 %collective-permute-start.9 = (f32[64,1024]{1,0:T(8,128)S(1)}, f32[64,1024]{1,0:T(8,128)S(1)}, u32[]{:S(2)}, u32[]{:S(2)}) collective-permute-start(f32[64,1024]{1,0:T(8,128)S(1)} %pad_maximum_fusion.1), channel_id=1, source_target_pairs={{0,2},{1,3},{2,0},{3,1},{4,6},{5,7},{6,4},{7,5},{8,10},{9,11},{10,... | collective-permute-start | bytes 786440 | tf_op jit(solution)/shard_map/ppermute | solution.py:467
  34.3 7.0 %sweep.3 = (f32[48,64,256]{2,1,0:T(8,128)}, bf16[1024,256]{1,0:T(8,128)(2,1)S(1)}, f32[2,512,128]{2,1,0:T(8,128)S(1)}) custom-call(f32[6,6]{1,0:T(8,128)S(1)} %copy-done.6, f32[4]{0:T(128)S(1)} %copy-done.7, f32[6]{0:T(128)S(1)} %copy-done.8, f32[48,64,256]{2,1,0:T(8,128)S(1)} %get-tuple-element.42.state_ref, f32[48,64,256]{2,1,0:T(8,128)S(1)} %copy-done.3, ...), custom_call_target="tpu_custom_call" | custom-call | flops 8000000000 | bytes 9437184 | tf_op jit(solution)/shard_map/sweep/pallas_call | solution.py:248
  41.3 0.9 pad_maximum_fusion
  42.3 2.4 %collective-permute-start.10 = (f32[128,1024]{1,0:T(8,128)S(1)}, f32[128,1024]{1,0:T(8,128)S(1)}, u32[]{:S(2)}, u32[]{:S(2)}) collective-permute-start(f32[128,1024]{1,0:T(8,128)S(1)} %pad_maximum_fusion), channel_id=1, source_target_pairs={{0,1},{1,0},{2,3},{3,2},{4,5},{5,4},{6,7},{7,6},{8,9},{9,8},{10,11... | collective-permute-start | bytes 1572872 | tf_op jit(solution)/shard_map/ppermute | solution.py:467
  44.7 19.0 %tiles.1 = (f32[128,8,128]{2,1,0:T(8,128)S(1)}, f32[128,8,128]{2,1,0:T(8,128)S(1)}) custom-call(s32[256]{0:T(256)S(1)} %fusion.5.place_ref, bf16[1024,256]{1,0:T(8,128)(2,1)S(1)} %get-tuple-element.55.table_ref, f32[2,512,128]{2,1,0:T(8,128)S(1)} %get-tuple-element.56.press_ref, s32[256,128]{1,0:T(8,128)S(1)} %copy-done.4, f32[256,128,128]{2,1,0:T(8,128)} %interp_ref.1), custom_call_target="tpu_custom_call" | custom-call | flops 17179869184 | bytes 16777216 | tf_op jit(solution)/shard_map/tiles/pallas_call | solution.py:365
  63.7 0.9 constant_dynamic-update-slice_fusion.1
  64.7 1.7 %collective-permute-start.11 = (f32[128,8,128]{2,1,0:T(8,128)S(1)}, f32[128,8,128]{2,1,0:T(8,128)S(1)}, u32[]{:S(2)}, u32[]{:S(2)}) collective-permute-start(f32[128,8,128]{2,1,0:T(8,128)S(1)} %get-tuple-element.63), channel_id=1, source_target_pairs={{0,8},{8,0},{16,24},{24,16},{1,9},{9,1},{17,25},{25,17},{2,10},{10... | collective-permute-start | bytes 1572872 | tf_op jit(solution)/shard_map/ppermute | solution.py:467
  66.4 1.5 %collective-permute-done.11 = f32[128,8,128]{2,1,0:T(8,128)S(1)} collective-permute-done((f32[128,8,128]{2,1,0:T(8,128)S(1)}, f32[128,8,128]{2,1,0:T(8,128)S(1)}, u32[]{:S(2)}, u32[]{:S(2)}) %collective-permute-start.11) | collective-permute-done | bytes 524320 | tf_op jit(solution)/shard_map/ppermute | solution.py:467
  68.0 2.0 %collective-permute-start.12 = (f32[64,8,128]{2,1,0:T(8,128)S(1)}, f32[64,8,128]{2,1,0:T(8,128)S(1)}, u32[]{:S(2)}, u32[]{:S(2)}) collective-permute-start(f32[64,8,128]{2,1,0:T(8,128)S(1)} %get-tuple-element.73), channel_id=1, source_target_pairs={{0,16},{8,24},{16,0},{24,8},{1,17},{9,25},{17,1},{25,9},{2,18},{10... | collective-permute-start | bytes 786440 | tf_op jit(solution)/shard_map/ppermute | solution.py:467
  70.0 6.6 %collective-permute-done.12.got_ref = f32[64,8,128]{2,1,0:T(8,128)S(1)} collective-permute-done((f32[64,8,128]{2,1,0:T(8,128)S(1)}, f32[64,8,128]{2,1,0:T(8,128)S(1)}, u32[]{:S(2)}, u32[]{:S(2)}) %collective-permute-start.12) | collective-permute-done | bytes 262176 | tf_op jit(solution)/shard_map/ppermute | solution.py:467
  76.7 0.9 combine.1
  77.9 2.3 %collective-permute-start.14 = (f32[17,8,128]{2,1,0:T(8,128)S(1)}, f32[17,8,128]{2,1,0:T(8,128)S(1)}, u32[]{:S(2)}, u32[]{:S(2)}) collective-permute-start(f32[17,8,128]{2,1,0:T(8,128)S(1)} %get-tuple-element.67), channel_id=1, source_target_pairs={{0,2},{1,3},{2,0},{3,1},{4,6},{5,7},{6,4},{7,5},{8,10},{9,11},{10,... | collective-permute-start | bytes 208904 | tf_op jit(solution)/shard_map/ppermute | solution.py:467
  80.2 0.9 collective-permute-start.15
  81.1 0.8 collective-permute-done.13.refs_1_
  81.9 1.2 %collective-permute-done.14.refs_2_ = f32[17,8,128]{2,1,0:T(8,128)S(1)} collective-permute-done((f32[17,8,128]{2,1,0:T(8,128)S(1)}, f32[17,8,128]{2,1,0:T(8,128)S(1)}, u32[]{:S(2)}, u32[]{:S(2)}) %collective-permute-start.14) | collective-permute-done | bytes 69664 | tf_op jit(solution)/shard_map/ppermute | solution.py:467
  83.1 2.3 %collective-permute-done.15.refs_3_ = f32[17,8,128]{2,1,0:T(8,128)S(1)} collective-permute-done((f32[17,8,128]{2,1,0:T(8,128)S(1)}, f32[17,8,128]{2,1,0:T(8,128)S(1)}, u32[]{:S(2)}, u32[]{:S(2)}) %collective-permute-start.15) | collective-permute-done | bytes 69664 | tf_op jit(solution)/shard_map/ppermute | solution.py:467
  85.5 1.4 %collective-permute-start.16 = (f32[9,8,128]{2,1,0:T(8,128)S(1)}, f32[9,8,128]{2,1,0:T(8,128)S(1)}, u32[]{:S(2)}, u32[]{:S(2)}) collective-permute-start(f32[9,8,128]{2,1,0:T(8,128)S(1)} %get-tuple-element.70), channel_id=1, source_target_pairs={{0,4},{1,5},{2,6},{3,7},{4,0},{5,1},{6,2},{7,3},{8,12},{9,13},{10,... | collective-permute-start | bytes 110600 | tf_op jit(solution)/shard_map/ppermute | solution.py:467
  86.8 3.5 %collective-permute-done.16.refs_1_ = f32[9,8,128]{2,1,0:T(8,128)S(1)} collective-permute-done((f32[9,8,128]{2,1,0:T(8,128)S(1)}, f32[9,8,128]{2,1,0:T(8,128)S(1)}, u32[]{:S(2)}, u32[]{:S(2)}) %collective-permute-start.16) | collective-permute-done | bytes 36896 | tf_op jit(solution)/shard_map/ppermute | solution.py:467
  90.4 1.8 %collective-permute-start.18 = (f32[9,8,128]{2,1,0:T(8,128)S(1)}, f32[9,8,128]{2,1,0:T(8,128)S(1)}, u32[]{:S(2)}, u32[]{:S(2)}) collective-permute-start(f32[9,8,128]{2,1,0:T(8,128)S(1)} %fold.3.refs_0_), channel_id=1, source_target_pairs={{0,16},{8,24},{16,0},{24,8},{1,17},{9,25},{17,1},{25,9},{2,18},{10... | collective-permute-start | bytes 110600 | tf_op jit(solution)/shard_map/ppermute | solution.py:467
  92.3 2.1 %collective-permute-done.18.refs_2_ = f32[9,8,128]{2,1,0:T(8,128)S(1)} collective-permute-done((f32[9,8,128]{2,1,0:T(8,128)S(1)}, f32[9,8,128]{2,1,0:T(8,128)S(1)}, u32[]{:S(2)}, u32[]{:S(2)}) %collective-permute-start.18) | collective-permute-done | bytes 36896 | tf_op jit(solution)/shard_map/ppermute | solution.py:467
  94.4 1.2 %collective-permute-done.19.refs_3_ = f32[9,8,128]{2,1,0:T(8,128)S(1)} collective-permute-done((f32[9,8,128]{2,1,0:T(8,128)S(1)}, f32[9,8,128]{2,1,0:T(8,128)S(1)}, u32[]{:S(2)}, u32[]{:S(2)}) %collective-permute-start.19) | collective-permute-done | bytes 36896 | tf_op jit(solution)/shard_map/ppermute | solution.py:467
  (53 shorter events, 4.4 us)
Async XLA Ops:
  0.6 1.9 %copy-start = (f32[48,64,256]{2,1,0:T(8,128)S(1)}, f32[48,64,256]{2,1,0:T(8,128)}, u32[]{:S(2)}) copy-start(f32[48,64,256]{2,1,0:T(8,128)} %state_ref.3) | copy-start | bytes 9437188
  2.5 12.1 %copy-start.10 = (s32[256,1]{0,1:T(1,128)S(1)}, s32[256,1]{0,1:T(1,128)}, u32[]{:S(2)}) copy-start(s32[256,1]{0,1:T(1,128)} %param.19) | copy-start | bytes 3076
  2.5 12.9 %copy-start.1 = (f32[48,64,256]{2,1,0:T(8,128)S(1)}, f32[48,64,256]{2,1,0:T(8,128)}, u32[]{:S(2)}) copy-start(f32[48,64,256]{2,1,0:T(8,128)} %state_ref.3) | copy-start | bytes 9437188
  2.5 12.9 %copy-start.5 = (f32[64,256]{1,0:T(8,128)S(1)}, f32[64,256]{1,0:T(8,128)}, u32[]{:S(2)}) copy-start(f32[64,256]{1,0:T(8,128)} %sigma_ref.3) | copy-start | bytes 196612
  2.5 12.9 %copy-start.6 = (f32[6,6]{1,0:T(8,128)S(1)}, f32[6,6]{1,0:T(8,128)}, u32[]{:S(2)}) copy-start(f32[6,6]{1,0:T(8,128)} %coupling_ref.3) | copy-start | bytes 436
  2.5 12.9 %copy-start.7 = (f32[4]{0:T(128)S(1)}, f32[4]{0:T(128)}, u32[]{:S(2)}) copy-start(f32[4]{0:T(128)} %omega_ref.3) | copy-start | bytes 52
  2.5 12.9 %copy-start.8 = (f32[6]{0:T(128)S(1)}, f32[6]{0:T(128)}, u32[]{:S(2)}) copy-start(f32[6]{0:T(128)} %coef_ref.3) | copy-start | bytes 76
  4.5 10.9 %collective-permute-start = (f32[4,12,256]{2,1,0:T(8,128)S(1)}, f32[4,12,256]{2,1,0:T(8,128)S(1)}, u32[]{:S(2)}, u32[]{:S(2)}) collective-permute-start(f32[4,12,256]{2,1,0:T(8,128)S(1)} %get-tuple-element.38), channel_id=1, source_target_pairs={{0,8},{8,0},{16,24},{24,16},{1,9},{9,1},{17,25},{25,17},{2,10},{10... | collective-permute-start | bytes 147464 | tf_op jit(solution)/shard_map/ppermute | solution.py:467
  4.9 10.5 %collective-permute-start.1 = (f32[4,12,256]{2,1,0:T(8,128)S(1)}, f32[4,12,256]{2,1,0:T(8,128)S(1)}, u32[]{:S(2)}, u32[]{:S(2)}) collective-permute-start(f32[4,12,256]{2,1,0:T(8,128)S(1)} %get-tuple-element.39), channel_id=1, source_target_pairs={{8,16},{16,8},{9,17},{17,9},{10,18},{18,10},{11,19},{19,11},{12,20... | collective-permute-start | bytes 147464 | tf_op jit(solution)/shard_map/ppermute | solution.py:231
  5.6 9.8 %collective-permute-start.2 = (f32[64,128]{1,0:T(8,128)}, f32[64,128]{1,0:T(8,128)S(1)}, u32[]{:S(2)}, u32[]{:S(2)}) collective-permute-start(f32[64,128]{1,0:T(8,128)} %get-tuple-element.40), channel_id=1, source_target_pairs={{0,1},{1,0},{2,3},{3,2},{4,5},{5,4},{6,7},{7,6},{8,9},{9,8},{10,11... | collective-permute-start | bytes 98312 | tf_op jit(solution)/shard_map/ppermute | solution.py:467
  8.2 7.2 %collective-permute-start.3 = (f32[64,128]{1,0:T(8,128)}, f32[64,128]{1,0:T(8,128)S(1)}, u32[]{:S(2)}, u32[]{:S(2)}) collective-permute-start(f32[64,128]{1,0:T(8,128)} %get-tuple-element.41), channel_id=1, source_target_pairs={{1,2},{3,4},{5,6},{2,1},{4,3},{6,5},{9,10},{11,12},{13,14},{10,9},... | collective-permute-start | bytes 98312 | tf_op jit(solution)/shard_map/ppermute | solution.py:231
  10.4 14.0 %collective-permute-start.4 = (f32[32,1024]{1,0:T(8,128)}, f32[32,1024]{1,0:T(8,128)}, u32[]{:S(2)}, u32[]{:S(2)}) collective-permute-start(f32[32,1024]{1,0:T(8,128)} %weigh.1), channel_id=1, source_target_pairs={{0,4},{1,5},{2,6},{3,7},{4,0},{5,1},{6,2},{7,3},{8,12},{9,13},{10,... | collective-permute-start | bytes 393224 | tf_op jit(solution)/shard_map/ppermute | solution.py:467
  15.4 1.9 %copy-start.2 = (f32[48,64,256]{2,1,0:T(8,128)S(1)}, f32[48,64,256]{2,1,0:T(8,128)}, u32[]{:S(2)}) copy-start(f32[48,64,256]{2,1,0:T(8,128)} %rhs_ref.3) | copy-start | bytes 9437188
  17.3 13.2 %copy-start.9 = (f32[32,1024]{1,0:T(8,128)S(1)}, f32[32,1024]{1,0:T(8,128)}, u32[]{:S(2)}) copy-start(f32[32,1024]{1,0:T(8,128)} %weigh.1) | copy-start | bytes 393220
  17.3 16.9 %copy-start.3 = (f32[48,64,256]{2,1,0:T(8,128)S(1)}, f32[48,64,256]{2,1,0:T(8,128)}, u32[]{:S(2)}) copy-start(f32[48,64,256]{2,1,0:T(8,128)} %rhs_ref.3) | copy-start | bytes 9437188
  24.4 9.9 %collective-permute-start.5 = (f32[4,12,256]{2,1,0:T(8,128)S(1)}, f32[4,12,256]{2,1,0:T(8,128)S(1)}, u32[]{:S(2)}, u32[]{:S(2)}) collective-permute-start(f32[4,12,256]{2,1,0:T(8,128)S(1)} %get-tuple-element.47), channel_id=1, source_target_pairs={{0,8},{8,0},{16,24},{24,16},{1,9},{9,1},{17,25},{25,17},{2,10},{10... | collective-permute-start | bytes 147464 | tf_op jit(solution)/shard_map/ppermute | solution.py:467
  26.5 7.8 %collective-permute-start.6 = (f32[4,12,256]{2,1,0:T(8,128)S(1)}, f32[4,12,256]{2,1,0:T(8,128)S(1)}, u32[]{:S(2)}, u32[]{:S(2)}) collective-permute-start(f32[4,12,256]{2,1,0:T(8,128)S(1)} %get-tuple-element.48), channel_id=1, source_target_pairs={{8,16},{16,8},{9,17},{17,9},{10,18},{18,10},{11,19},{19,11},{12,20... | collective-permute-start | bytes 147464 | tf_op jit(solution)/shard_map/ppermute | solution.py:231
  27.1 7.1 %collective-permute-start.7 = (f32[64,128]{1,0:T(8,128)S(1)}, f32[64,128]{1,0:T(8,128)S(1)}, u32[]{:S(2)}, u32[]{:S(2)}) collective-permute-start(f32[64,128]{1,0:T(8,128)S(1)} %get-tuple-element.49), channel_id=1, source_target_pairs={{0,1},{1,0},{2,3},{3,2},{4,5},{5,4},{6,7},{7,6},{8,9},{9,8},{10,11... | collective-permute-start | bytes 98312 | tf_op jit(solution)/shard_map/ppermute | solution.py:467
  29.8 4.4 %collective-permute-start.8 = (f32[64,128]{1,0:T(8,128)S(1)}, f32[64,128]{1,0:T(8,128)S(1)}, u32[]{:S(2)}, u32[]{:S(2)}) collective-permute-start(f32[64,128]{1,0:T(8,128)S(1)} %get-tuple-element.50), channel_id=1, source_target_pairs={{1,2},{3,4},{5,6},{2,1},{4,3},{6,5},{9,10},{11,12},{13,14},{10,9},... | collective-permute-start | bytes 98312 | tf_op jit(solution)/shard_map/ppermute | solution.py:231
  31.4 9.9 %collective-permute-start.9 = (f32[64,1024]{1,0:T(8,128)S(1)}, f32[64,1024]{1,0:T(8,128)S(1)}, u32[]{:S(2)}, u32[]{:S(2)}) collective-permute-start(f32[64,1024]{1,0:T(8,128)S(1)} %pad_maximum_fusion.1), channel_id=1, source_target_pairs={{0,2},{1,3},{2,0},{3,1},{4,6},{5,7},{6,4},{7,5},{8,10},{9,11},{10,... | collective-permute-start | bytes 786440 | tf_op jit(solution)/shard_map/ppermute | solution.py:467
  34.3 10.4 %copy-start.4 = (s32[256,128]{1,0:T(8,128)S(1)}, s32[256,128]{1,0:T(8,128)}, u32[]{:S(2)}) copy-start(s32[256,128]{1,0:T(8,128)} %cells_ref.1) | copy-start | bytes 393220
  42.3 21.4 %collective-permute-start.10 = (f32[128,1024]{1,0:T(8,128)S(1)}, f32[128,1024]{1,0:T(8,128)S(1)}, u32[]{:S(2)}, u32[]{:S(2)}) collective-permute-start(f32[128,1024]{1,0:T(8,128)S(1)} %pad_maximum_fusion), channel_id=1, source_target_pairs={{0,1},{1,0},{2,3},{3,2},{4,5},{5,4},{6,7},{7,6},{8,9},{9,8},{10,11... | collective-permute-start | bytes 1572872 | tf_op jit(solution)/shard_map/ppermute | solution.py:467
  64.7 3.2 %collective-permute-start.11 = (f32[128,8,128]{2,1,0:T(8,128)S(1)}, f32[128,8,128]{2,1,0:T(8,128)S(1)}, u32[]{:S(2)}, u32[]{:S(2)}) collective-permute-start(f32[128,8,128]{2,1,0:T(8,128)S(1)} %get-tuple-element.63), channel_id=1, source_target_pairs={{0,8},{8,0},{16,24},{24,16},{1,9},{9,1},{17,25},{25,17},{2,10},{10... | collective-permute-start | bytes 1572872 | tf_op jit(solution)/shard_map/ppermute | solution.py:467
  68.0 8.7 %collective-permute-start.12 = (f32[64,8,128]{2,1,0:T(8,128)S(1)}, f32[64,8,128]{2,1,0:T(8,128)S(1)}, u32[]{:S(2)}, u32[]{:S(2)}) collective-permute-start(f32[64,8,128]{2,1,0:T(8,128)S(1)} %get-tuple-element.73), channel_id=1, source_target_pairs={{0,16},{8,24},{16,0},{24,8},{1,17},{9,25},{17,1},{25,9},{2,18},{10... | collective-permute-start | bytes 786440 | tf_op jit(solution)/shard_map/ppermute | solution.py:467
  77.6 4.3 %collective-permute-start.13 = (f32[17,8,128]{2,1,0:T(8,128)S(1)}, f32[17,8,128]{2,1,0:T(8,128)S(1)}, u32[]{:S(2)}, u32[]{:S(2)}) collective-permute-start(f32[17,8,128]{2,1,0:T(8,128)S(1)} %get-tuple-element.66), channel_id=1, source_target_pairs={{0,1},{1,0},{2,3},{3,2},{4,5},{5,4},{6,7},{7,6},{8,9},{9,8},{10,11... | collective-permute-start | bytes 208904 | tf_op jit(solution)/shard_map/ppermute | solution.py:467
  77.9 5.2 %collective-permute-start.14 = (f32[17,8,128]{2,1,0:T(8,128)S(1)}, f32[17,8,128]{2,1,0:T(8,128)S(1)}, u32[]{:S(2)}, u32[]{:S(2)}) collective-permute-start(f32[17,8,128]{2,1,0:T(8,128)S(1)} %get-tuple-element.67), channel_id=1, source_target_pairs={{0,2},{1,3},{2,0},{3,1},{4,6},{5,7},{6,4},{7,5},{8,10},{9,11},{10,... | collective-permute-start | bytes 208904 | tf_op jit(solution)/shard_map/ppermute | solution.py:467
  80.2 5.2 %collective-permute-start.15 = (f32[17,8,128]{2,1,0:T(8,128)S(1)}, f32[17,8,128]{2,1,0:T(8,128)S(1)}, u32[]{:S(2)}, u32[]{:S(2)}) collective-permute-start(f32[17,8,128]{2,1,0:T(8,128)S(1)} %get-tuple-element.68), channel_id=1, source_target_pairs={{0,3},{1,2},{2,1},{3,0},{4,7},{5,6},{6,5},{7,4},{8,11},{9,10},{10,... | collective-permute-start | bytes 208904 | tf_op jit(solution)/shard_map/ppermute | solution.py:467
  85.5 4.9 %collective-permute-start.16 = (f32[9,8,128]{2,1,0:T(8,128)S(1)}, f32[9,8,128]{2,1,0:T(8,128)S(1)}, u32[]{:S(2)}, u32[]{:S(2)}) collective-permute-start(f32[9,8,128]{2,1,0:T(8,128)S(1)} %get-tuple-element.70), channel_id=1, source_target_pairs={{0,4},{1,5},{2,6},{3,7},{4,0},{5,1},{6,2},{7,3},{8,12},{9,13},{10,... | collective-permute-start | bytes 110600 | tf_op jit(solution)/shard_map/ppermute | solution.py:467
  90.4 1.9 %collective-permute-start.17 = (f32[9,8,128]{2,1,0:T(8,128)S(1)}, f32[9,8,128]{2,1,0:T(8,128)S(1)}, u32[]{:S(2)}, u32[]{:S(2)}) collective-permute-start(f32[9,8,128]{2,1,0:T(8,128)S(1)} %fold.3.refs_0_), channel_id=1, source_target_pairs={{0,8},{8,0},{16,24},{24,16},{1,9},{9,1},{17,25},{25,17},{2,10},{10... | collective-permute-start | bytes 110600 | tf_op jit(solution)/shard_map/ppermute | solution.py:467
  90.4 4.0 %collective-permute-start.18 = (f32[9,8,128]{2,1,0:T(8,128)S(1)}, f32[9,8,128]{2,1,0:T(8,128)S(1)}, u32[]{:S(2)}, u32[]{:S(2)}) collective-permute-start(f32[9,8,128]{2,1,0:T(8,128)S(1)} %fold.3.refs_0_), channel_id=1, source_target_pairs={{0,16},{8,24},{16,0},{24,8},{1,17},{9,25},{17,1},{25,9},{2,18},{10... | collective-permute-start | bytes 110600 | tf_op jit(solution)/shard_map/ppermute | solution.py:467
  92.2 3.4 %collective-permute-start.19 = (f32[9,8,128]{2,1,0:T(8,128)S(1)}, f32[9,8,128]{2,1,0:T(8,128)S(1)}, u32[]{:S(2)}, u32[]{:S(2)}) collective-permute-start(f32[9,8,128]{2,1,0:T(8,128)S(1)} %fold.3.refs_0_), channel_id=1, source_target_pairs={{0,24},{8,16},{16,8},{24,0},{1,25},{9,17},{17,9},{25,1},{2,26},{10... | collective-permute-start | bytes 110600 | tf_op jit(solution)/shard_map/ppermute | solution.py:467

commit v3 on v2

--- a/solution.py
+++ b/solution.py
@@ -14,6 +14,7 @@
 LANE_TILES = 10
 VMEM_LIMIT = 40 << 20
 VMEM_ALL = 60 << 20
+VMEM_SWEEP = 46 << 20
 VMEM_SMALL = 12 << 20
 
 
@@ -46,20 +47,51 @@
     row2_ref[0] = jnp.where(even_x, up, down)
 
 
-def weigh_kernel(mine_ref, shape_ref, correction_ref, weighted_ref):
-    weighted_ref[...] = shape_ref[...] * correction_ref[...]
-
-
-def pack_kernel(state_ref, up_ref, down_ref, left_ref, right_ref):
-    mode = pl.program_id(0)
-    planes = state_ref.shape[0]
-
-    @pl.when(mode == 0)
-    def _():
-        left_ref[...] = jnp.zeros_like(left_ref)
-        right_ref[...] = jnp.zeros_like(right_ref)
-
-    pack_edges(state_ref, mode * planes, planes, up_ref, down_ref, left_ref, right_ref)
+def pack_kernel(
+    modes,
+    state_ref,
+    shape_ref,
+    correction_ref,
+    owner_ref,
+    panel_ref,
+    row1_ref,
+    row2_ref,
+    col1_ref,
+    col2_ref,
+    weighted_ref,
+    place_ref,
+    held_ref,
+    shapes_ref,
+    factor_ref,
+    tiles_ref,
+    sems,
+):
+    planes = state_ref.shape[0] // modes
+    share = weighted_ref.shape[1]
+    copies = []
+    for mode in range(modes):
+        block = pl.ds(mode * planes, planes)
+        copies.append(pltpu.make_async_copy(state_ref.at[block], held_ref.at[block], sems.at[mode]))
+    mine = pl.ds(pl.multiple_of(lax.axis_index("gx") * share, LANES), share)
+    copies.append(pltpu.make_async_copy(shape_ref.at[:, mine], shapes_ref, sems.at[modes]))
+    copies.append(pltpu.make_async_copy(correction_ref.at[:, mine], factor_ref, sems.at[modes + 1]))
+    copies.append(pltpu.make_async_copy(owner_ref, tiles_ref.at[0], sems.at[modes + 2]))
+    copies.append(pltpu.make_async_copy(panel_ref, tiles_ref.at[1], sems.at[modes + 3]))
+    for copy in copies:
+        copy.start()
+    col1_ref[...] = jnp.zeros_like(col1_ref)
+    col2_ref[...] = jnp.zeros_like(col2_ref)
+    for mode in range(modes):
+        copies[mode].wait()
+        here = pl.ds(mode, 1)
+        block = pl.ds(mode * planes, planes)
+        pack_edges(
+            held_ref.at[block], mode * planes, planes, row1_ref.at[here], row2_ref.at[here], col1_ref, col2_ref
+        )
+    for copy in copies[modes:]:
+        copy.wait()
+    weighted_ref[...] = shapes_ref[...] * factor_ref[...]
+    place_ref[...] = places(tiles_ref[0], tiles_ref[1], shape_ref.shape[1] // LANES)
 
 
 def sweep_kernel(
@@ -68,7 +100,7 @@
     omega_ref,
     coef_ref,
     state_ref,
-    rhs_ref,
+    right_ref,
     sigma_ref,
     row1_ref,
     row2_ref,
@@ -77,13 +109,28 @@
     new_ref,
     *rest,
 ):
-    nbs_ref, a_ref, b_ref = rest[-3:]
+    nbs_ref, a_ref, b_ref, rhs_ref, sems = rest[-5:]
     if last:
         table_ref, press_ref = rest[:2]
     mode = pl.program_id(0)
     planes, rows, cols = state_ref.shape
     nvar = planes // 2
     parts = 2 * omega_ref.shape[0]
+    slot = lax.rem(mode, 2)
+
+    def fetch(which):
+        into = lax.rem(which, 2)
+        block = pl.ds(which * planes, planes)
+        return pltpu.make_async_copy(right_ref.at[block], rhs_ref.at[into], sems.at[into])
+
+    @pl.when(mode == 0)
+    def _():
+        fetch(mode).start()
+
+    @pl.when(mode + 1 < pl.num_programs(0))
+    def _():
+        fetch(mode + 1).start()
+
     freq = omega_ref[mode]
     dval = 4.0 + sigma_ref[...]
     scale = 0.8 / (dval * dval + freq * freq)
@@ -130,8 +177,8 @@
         b = b_ref[here, :]
         press_re = press_im = None
         for v in range(nvar):
-            res_re = rhs_ref[v, here, :]
-            res_im = rhs_ref[nvar + v, here, :]
+            res_re = rhs_ref[slot, v, here, :]
+            res_im = rhs_ref[slot, nvar + v, here, :]
             for w in range(nvar):
                 res_re = res_re + weight[v][w] * nbs[w]
                 res_im = res_im + weight[v][w] * nbs[nvar + w]
@@ -150,7 +197,8 @@
                     press_ref[half, pl.ds(start, 8, stride=parts), :] = piece
         return carry
 
-    lax.fori_loop(0, rows // 8, strip, 0)
+    fetch(mode).wait()
+    lax.fori_loop(0, rows // 8, strip, 0, unroll=True)
     if last:
 
         @pl.when(mode == pl.num_programs(0) - 1)
@@ -186,40 +234,26 @@
     return shapes, (row_spec, row_spec, col_spec, col_spec)
 
 
-def weigh(mode_shape, correction):
-    count, panels = mode_shape.shape
-    share = panels // lax.axis_size("gx")
-    mine = lax.axis_index("gx").astype(jnp.int32)[None]
+def pack(state, modes, mode_shape, correction, owner, panel):
+    comp, rows, cols = state.shape
+    shapes, _ = edge_shapes(modes, comp // modes, rows, cols)
+    share = (mode_shape.shape[0], mode_shape.shape[1] // lax.axis_size("gx"))
+    hbm = pl.BlockSpec(memory_space=pltpu.HBM)
     return pl.pallas_call(
-        weigh_kernel,
-        grid_spec=pltpu.PrefetchScalarGridSpec(
-            num_scalar_prefetch=1,
-            grid=(1,),
-            in_specs=[
-                pl.BlockSpec((count, share), lambda g, at: (0, at[0])),
-                pl.BlockSpec((1, share), lambda g, at: (0, at[0])),
-            ],
-            out_specs=pl.BlockSpec((count, share), lambda g, at: (0, 0)),
-        ),
-        out_shape=jax.ShapeDtypeStruct((count, share), F32),
+        functools.partial(pack_kernel, modes),
+        out_shape=shapes + (jax.ShapeDtypeStruct(share, F32), jax.ShapeDtypeStruct(owner.shape, jnp.int32)),
+        in_specs=[hbm] * 5,
+        out_specs=(vmem(),) * 6,
+        scratch_shapes=[
+            pltpu.VMEM(state.shape, F32),
+            pltpu.VMEM(share, F32),
+            pltpu.VMEM((1, share[1]), F32),
+            pltpu.VMEM((2,) + owner.shape, jnp.int32),
+            pltpu.SemaphoreType.DMA((modes + 4,)),
+        ],
         compiler_params=pltpu.CompilerParams(vmem_limit_bytes=VMEM_ALL),
-        name="weigh",
-    )(mine, mode_shape, correction[None, :])
-
-
-def pack(state, modes):
-    comp, rows, cols = state.shape
-    planes = comp // modes
-    shapes, specs = edge_shapes(modes, planes, rows, cols)
-    return pl.pallas_call(
-        pack_kernel,
-        grid=(modes,),
-        out_shape=shapes,
-        in_specs=[pl.BlockSpec((planes, rows, cols), lambda m: (m, 0, 0))],
-        out_specs=specs,
-        compiler_params=pltpu.CompilerParams(vmem_limit_bytes=VMEM_LIMIT),
         name="pack",
-    )(state)
+    )(state, mode_shape, correction[None, :], owner, panel)
 
 
 def exchange(edges):
@@ -254,7 +288,7 @@
             smem(),
             smem(),
             block,
-            block,
+            pl.BlockSpec(memory_space=pltpu.HBM),
             pl.BlockSpec((rows, cols), lambda m: (0, 0)),
             *edge_specs,
         ],
@@ -263,8 +297,10 @@
             pltpu.VMEM((planes, rows, cols), F32),
             pltpu.VMEM((rows, cols), F32),
             pltpu.VMEM((rows, cols), F32),
+            pltpu.VMEM((2, planes, rows, cols), F32),
+            pltpu.SemaphoreType.DMA((2,)),
         ],
-        compiler_params=pltpu.CompilerParams(vmem_limit_bytes=VMEM_LIMIT),
+        compiler_params=pltpu.CompilerParams(vmem_limit_bytes=VMEM_SWEEP),
         cost_estimate=pl.CostEstimate(flops=8 * 10**9, bytes_accessed=12 * field.size, transcendentals=0),
         name="sweep",
     )(coupling, omega, coef, field, rhs, sigma, *halo)
@@ -383,11 +419,13 @@
     )(place, table, press, cells, interp)
 
 
-def combine_kernel(order, keep_ref, got_ref, shapes_ref, *out_refs):
+def combine_kernel(order, where, keep_ref, got_ref, *refs):
     owners = len(order)
     chunk = keep_ref.shape[0] // owners
     parts = keep_ref.shape[1]
-    modes = shapes_ref.shape[0] // owners
+    pieces = 1 + max(piece for piece, _ in where.values())
+    shape_refs, out_refs = refs[:pieces], refs[pieces:]
+    modes = shape_refs[0].shape[0]
     tiles = out_refs[0].shape[0] - 1
     force = jnp.zeros((parts, modes), F32)
     for at, relative in enumerate(order):
@@ -396,7 +434,7 @@
         out_refs[first // tiles][first % tiles : first % tiles + chunk] = lines
         force = force + lax.dot_general(
             jnp.concatenate([lines[k] for k in range(chunk)], axis=1),
-            shapes_ref[relative * modes : (relative + 1) * modes, :],
+            shape_refs[where[relative][0]][where[relative][1] : where[relative][1] + modes, :],
             (((1,), (1,)), ((), ())),
             precision=lax.Precision.HIGHEST,
             preferred_element_type=F32,
@@ -447,10 +485,8 @@
 
 def reversed_bits(value, count):
     out = jnp.zeros_like(value)
-    bit = 1
-    while bit < count:
-        out = out * 2 + (value // bit) % 2
-        bit *= 2
+    for bit in range(count.bit_length() - 1):
+        out = out * 2 + ((value >> bit) & 1)
     return out
 
 
@@ -458,19 +494,28 @@
     nx = lax.axis_size("gx")
     ny = lax.axis_size("gy")
     chunk = panel_tiles // nx
-    to_x = (panel // chunk) ^ lax.axis_index("gx")
+    to_x = (panel >> (chunk.bit_length() - 1)) ^ lax.axis_index("gx")
     to_y = owner ^ lax.axis_index("gy")
-    return (reversed_bits(to_x, nx) * ny + position(to_y, "gy")) * chunk + panel % chunk
+    return (reversed_bits(to_x, nx) * ny + position(to_y, "gy")) * chunk + (panel & (chunk - 1))
 
 
 def swap(send, axis, bit):
     return lax.ppermute(send, axis, [(i, i ^ bit) for i in range(lax.axis_size(axis))])
 
 
-def gather_step(blocks, axis, bit):
-    held = sorted(blocks)
-    got = swap(jnp.concatenate([blocks[r] for r in held], axis=0), axis, bit)
-    return {**blocks, **{r ^ bit: block for r, block in zip(held, jnp.split(got, len(held), axis=0))}}
+def gather_step(pieces, axis, bit):
+    whole = pieces[0] if len(pieces) == 1 else jnp.concatenate(pieces, axis=0)
+    return pieces + [swap(whole, axis, bit)]
+
+
+def gathered(bits, size):
+    laid = [0]
+    where = {0: (0, 0)}
+    for number, bit in enumerate(bits):
+        for at, relative in enumerate(laid):
+            where[relative ^ bit] = (number + 1, at * size)
+        laid = laid + [relative ^ bit for relative in laid]
+    return where
 
 
 def bits_of(axis):
@@ -490,11 +535,11 @@
 def position(relative, axis):
     at = 0
     for base, size in levels(axis):
-        at = at * size + relative // base % size
+        at = at * size + ((relative >> (base.bit_length() - 1)) & (size - 1))
     return at
 
 
-def reduce_panels(keep, send, shapes):
+def reduce_panels(keep, send, pieces, where):
     gx_bits = bits_of("gx")
     for bit in gx_bits[:-1]:
         got = swap(send, "gx", bit)
@@ -508,7 +553,12 @@
     tiles = keep.shape[0] // steps[0][1]
     lines = keep.shape[1:]
     held = local_call(
-        functools.partial(combine_kernel, order), ((tiles + 1,) + lines,) * steps[0][1], "combine", keep, got, shapes
+        functools.partial(combine_kernel, order, where),
+        ((tiles + 1,) + lines,) * steps[0][1],
+        "combine",
+        keep,
+        got,
+        *pieces,
     )
     for number, (base, size) in enumerate(steps):
         held = [held[0]] + [swap(held[r], "gy", base * r) for r in range(1, size)]
@@ -535,23 +585,27 @@
     modes = omega.shape[0]
     parts = 2 * modes
     panel_tiles = correction.shape[0] // LANES
-    place = places(tile_owner[:, 0], tile_panel[:, 0], panel_tiles)
-    halo = exchange(pack(state, modes))
-    weighted = weigh(mode_shape, correction)
+    tiles = tile_cells.shape[0]
+    owner = tile_owner.reshape(tiles // LANES, LANES)
+    panel = tile_panel.reshape(tiles // LANES, LANES)
+    *edges, weighted, place = pack(state, modes, mode_shape, correction, owner, panel)
+    halo = exchange(edges)
     far = bits_of("gy")[::-1]
-    blocks = gather_step({0: weighted}, "gy", far[0])
+    where = gathered(far, mode_shape.shape[0])
+    pieces = gather_step([weighted], "gy", far[0])
     field, *edges = sweep(False, coupling, omega, pressure_coef, state, right_side, sigma, halo)
-    edges, blocks = lax.optimization_barrier((edges, blocks))
+    edges, pieces = lax.optimization_barrier((edges, pieces))
     halo = exchange(edges)
     for bit in far[1:-1]:
-        blocks = gather_step(blocks, "gy", bit)
+        pieces = gather_step(pieces, "gy", bit)
     field, table, press = sweep(True, coupling, omega, pressure_coef, field, right_side, sigma, halo)
-    table, blocks = lax.optimization_barrier((table, blocks))
-    blocks = gather_step(blocks, "gy", far[-1])
-    shapes = jnp.concatenate([blocks[r] for r in sorted(blocks)], axis=0)
-    keep, send = tile_sums(place, table, press, tile_cells, interp, panel_tiles * lax.axis_size("gy"), parts)
-    send, shapes = lax.optimization_barrier((send, shapes))
-    chunk = reduce_panels(keep, send, shapes)
+    table, pieces = lax.optimization_barrier((table, pieces))
+    pieces = gather_step(pieces, "gy", far[-1])
+    keep, send = tile_sums(
+        place.reshape(tiles), table, press, tile_cells, interp, panel_tiles * lax.axis_size("gy"), parts
+    )
+    send, pieces = lax.optimization_barrier((send, pieces))
+    chunk = reduce_panels(keep, send, pieces, where)
     total = [chunk] + [swap(chunk, "gx", relative) for relative in range(1, lax.axis_size("gx"))]
     share = mode_shape.shape[0] // lax.axis_size("gy")
     panels, gaf = local_call(

time: 96.7 us -> 94.1 us (0.973)
  local copies, waits for them, and re-layouts: 4.82 us -> 0.05 us
  other arithmetic: 2.63 us -> 0.11 us
  waiting for transfers between devices: 19.4 us -> 21.7 us
  starting transfers between devices: 30.3 us -> 31.8 us
  Pallas kernels: 38.2 us -> 39.3 us
    unnamed x29 -> x18, local copies, waits for them, and re-layouts: 4.79 us -> 0.05 us
    ppermute x16, waiting for transfers between devices: 19.4 us -> 21.7 us  [swap(): lax.ppermute(send, axis, [(i, i ^ bit) for i in range(lax.axis_size(axis))])]
    concatenate x2, other arithmetic: 1.87 us -> 0.05 us  [gather_step(): whole = pieces[0] if len(pieces) == 1 else jnp.concatenate(pieces, axis=0)]
    ppermute x16, starting transfers between devices: 27.7 us -> 29.2 us  [swap(): lax.ppermute(send, axis, [(i, i ^ bit) for i in range(lax.axis_size(axis))])]
    pallas_call x2 -> x1, Pallas kernels: 3.48 us -> 3.35 us  [pack(): pl.pallas_call(functools.partial(pack_kernel, modes), out_shape=shapes +...]
  transfers between devices with their start and end apart: 20 -> 20, of which waited for: 8 -> 9; matrix products, arithmetic and copies ran while one was open for 2% -> 0% of each run, Pallas kernels for 36% -> 37%
where the time goes in v3:
time: 94.1 us; the launch traced here: 93.9 us
  Pallas kernels  39.3 us (42%)
  starting transfers between devices  31.8 us (34%)
  waiting for transfers between devices  21.7 us (23%)
    ppermute x16, starting transfers between devices, swap(): lax.ppermute(send, axis, [(i, i ^ bit) for i in range(lax.axis_size(axis))])  29.2 us
    ppermute x16, waiting for transfers between devices, swap(): lax.ppermute(send, axis, [(i, i ^ bit) for i in range(lax.axis_size(axis))])  21.7 us
    pallas_call x1, Pallas kernels, tile_sums(): pl.pallas_call(tile_kernel, grid=(tiles // block,), out_shape=(jax.ShapeD...  19.7 us
    pallas_call x2, Pallas kernels, sweep(): pl.pallas_call(functools.partial(sweep_kernel, last), grid=(modes,), out_...  14.6 us
    pallas_call x1, Pallas kernels, pack(): pl.pallas_call(functools.partial(pack_kernel, modes), out_shape=shapes +...  3.35 us
    ppermute x4, starting transfers between devices, exchange(): got.append(lax.ppermute(second, axis, pairs + [(b, a) for a, b in pairs]))  2.61 us
  transfers between devices with their start and end apart: 20, of which 9 were waited for; matrix products, arithmetic and copies ran while one was open for 0% of the time, Pallas kernels for 37%

profile of v3, /device:TPU:0, one launch (start us, length us, event | category | flops | bytes accessed | tf_op | source)
XLA Modules:
  0.0 93.9 jit_solution(11512927614160496983)
XLA Ops:
  0.7 3.4 %pack.1 = (f32[4,12,256]{2,1,0:T(8,128)}, f32[4,12,256]{2,1,0:T(8,128)}, f32[64,128]{1,0:T(8,128)}, f32[64,128]{1,0:T(8,128)}, f32[32,1024]{1,0:T(8,128)}, /*index=5*/s32[2,128]{1,0:T(2,128)}) custom-call(f32[48,64,256]{2,1,0:T(8,128)} %state_ref.3, f32[32,4096]{1,0:T(8,128)} %shape_ref.1, f32[1,4096]{1,0:T(1,128)} %bitcast.5, s32[2,128]{1,0:T(2,128)} %bitcast.6, ...), custom_call_target="tpu_custom_call" | custom-call | tf_op jit(solution)/shard_map/pack/pallas_call | solution.py:242
  4.0 0.5 collective-permute-start
  4.6 0.7 collective-permute-start.1
  5.2 2.6 %collective-permute-start.2 = (f32[64,128]{1,0:T(8,128)}, f32[64,128]{1,0:T(8,128)S(1)}, u32[]{:S(2)}, u32[]{:S(2)}) collective-permute-start(f32[64,128]{1,0:T(8,128)} %get-tuple-element.44), channel_id=1, source_target_pairs={{0,1},{1,0},{2,3},{3,2},{4,5},{5,4},{6,7},{7,6},{8,9},{9,8},{10,11... | collective-permute-start | bytes 98312 | tf_op jit(solution)/shard_map/ppermute | solution.py:503
  7.8 0.7 collective-permute-start.3
  8.5 4.3 %collective-permute-start.4 = (f32[32,1024]{1,0:T(8,128)}, f32[32,1024]{1,0:T(8,128)S(1)}, u32[]{:S(2)}, u32[]{:S(2)}) collective-permute-start(f32[32,1024]{1,0:T(8,128)} %get-tuple-element.69.refs_0_), channel_id=1, source_target_pairs={{0,4},{1,5},{2,6},{3,7},{4,0},{5,1},{6,2},{7,3},{8,12},{9,13},{10,... | collective-permute-start | bytes 393224 | tf_op jit(solution)/shard_map/ppermute | solution.py:503
  12.9 7.6 %sweep.2 = (f32[48,64,256]{2,1,0:T(8,128)S(1)}, f32[4,12,256]{2,1,0:T(8,128)S(1)}, f32[4,12,256]{2,1,0:T(8,128)S(1)}, f32[64,128]{1,0:T(8,128)S(1)}, f32[64,128]{1,0:T(8,128)S(1)}) custom-call(f32[6,6]{1,0:T(8,128)S(1)} %copy-done.5, f32[4]{0:T(128)S(1)} %copy-done.7, f32[6]{0:T(128)S(1)} %copy-done.8, f32[48,64,256]{2,1,0:T(8,128)S(1)} %copy-done, ...), custom_call_target="tpu_custom_call" | custom-call | flops 8000000000 | bytes 9437184 | tf_op jit(solution)/shard_map/sweep/pallas_call | solution.py:282
  20.5 2.1 %collective-permute-start.5 = (f32[4,12,256]{2,1,0:T(8,128)S(1)}, f32[4,12,256]{2,1,0:T(8,128)S(1)}, u32[]{:S(2)}, u32[]{:S(2)}) collective-permute-start(f32[4,12,256]{2,1,0:T(8,128)S(1)} %get-tuple-element.52), channel_id=1, source_target_pairs={{0,8},{8,0},{16,24},{24,16},{1,9},{9,1},{17,25},{25,17},{2,10},{10... | collective-permute-start | bytes 147464 | tf_op jit(solution)/shard_map/ppermute | solution.py:503
  22.6 0.7 collective-permute-start.6
  23.3 3.1 %collective-permute-start.7 = (f32[64,128]{1,0:T(8,128)S(1)}, f32[64,128]{1,0:T(8,128)S(1)}, u32[]{:S(2)}, u32[]{:S(2)}) collective-permute-start(f32[64,128]{1,0:T(8,128)S(1)} %get-tuple-element.54), channel_id=1, source_target_pairs={{0,1},{1,0},{2,3},{3,2},{4,5},{5,4},{6,7},{7,6},{8,9},{9,8},{10,11... | collective-permute-start | bytes 98312 | tf_op jit(solution)/shard_map/ppermute | solution.py:503
  26.3 0.7 collective-permute-start.8
  27.0 4.7 %collective-permute-start.9 = (f32[64,1024]{1,0:T(8,128)S(1)}, f32[64,1024]{1,0:T(8,128)S(1)}, u32[]{:S(2)}, u32[]{:S(2)}) collective-permute-start(f32[64,1024]{1,0:T(8,128)S(1)} %pad_maximum_fusion.1), channel_id=1, source_target_pairs={{0,2},{1,3},{2,0},{3,1},{4,6},{5,7},{6,4},{7,5},{8,10},{9,11},{10,... | collective-permute-start | bytes 786440 | tf_op jit(solution)/shard_map/ppermute | solution.py:503
  31.8 7.0 %sweep.3 = (f32[48,64,256]{2,1,0:T(8,128)}, bf16[1024,256]{1,0:T(8,128)(2,1)S(1)}, f32[2,512,128]{2,1,0:T(8,128)S(1)}) custom-call(f32[6,6]{1,0:T(8,128)S(1)} %copy-done.5, f32[4]{0:T(128)S(1)} %copy-done.7, f32[6]{0:T(128)S(1)} %copy-done.8, f32[48,64,256]{2,1,0:T(8,128)S(1)} %get-tuple-element.46.state_ref, f32[48,64,256]{2,1,0:T(8,128)S(1)} %copy-done.2, ...), custom_call_target="tpu_custom_call" | custom-call | flops 8000000000 | bytes 9437184 | tf_op jit(solution)/shard_map/sweep/pallas_call | solution.py:282
  38.7 0.4 collective-permute-done.9.refs_2_
  39.2 3.0 %collective-permute-start.10 = (f32[128,1024]{1,0:T(8,128)S(1)}, f32[128,1024]{1,0:T(8,128)S(1)}, u32[]{:S(2)}, u32[]{:S(2)}) collective-permute-start(f32[128,1024]{1,0:T(8,128)S(1)} %pad_maximum_fusion), channel_id=1, source_target_pairs={{0,1},{1,0},{2,3},{3,2},{4,5},{5,4},{6,7},{7,6},{8,9},{9,8},{10,11... | collective-permute-start | bytes 1572872 | tf_op jit(solution)/shard_map/ppermute | solution.py:503
  42.2 19.7 %tiles.1 = (f32[128,8,128]{2,1,0:T(8,128)S(1)}, f32[128,8,128]{2,1,0:T(8,128)S(1)}) custom-call(s32[256]{0:T(256)S(1)} %bitcast.4, bf16[1024,256]{1,0:T(8,128)(2,1)S(1)} %get-tuple-element.61.table_ref, f32[2,512,128]{2,1,0:T(8,128)S(1)} %get-tuple-element.62.press_ref, s32[256,128]{1,0:T(8,128)S(1)} %copy-done.3, f32[256,128,128]{2,1,0:T(8,128)} %interp_ref.1), custom_call_target="tpu_custom_call" | custom-call | flops 17179869184 | bytes 16777216 | tf_op jit(solution)/shard_map/tiles/pallas_call | solution.py:401
  61.9 0.1 collective-permute-start.11
  62.0 1.8 %collective-permute-done.11 = f32[128,8,128]{2,1,0:T(8,128)S(1)} collective-permute-done((f32[128,8,128]{2,1,0:T(8,128)S(1)}, f32[128,8,128]{2,1,0:T(8,128)S(1)}, u32[]{:S(2)}, u32[]{:S(2)}) %collective-permute-start.11) | collective-permute-done | bytes 524320 | tf_op jit(solution)/shard_map/ppermute | solution.py:503
  64.0 2.8 %collective-permute-start.12 = (f32[64,8,128]{2,1,0:T(8,128)S(1)}, f32[64,8,128]{2,1,0:T(8,128)S(1)}, u32[]{:S(2)}, u32[]{:S(2)}) collective-permute-start(f32[64,8,128]{2,1,0:T(8,128)S(1)} %get-tuple-element.81), channel_id=1, source_target_pairs={{0,16},{8,24},{16,0},{24,8},{1,17},{9,25},{17,1},{25,9},{2,18},{10... | collective-permute-start | bytes 786440 | tf_op jit(solution)/shard_map/ppermute | solution.py:503
  66.8 6.6 %collective-permute-done.12.got_ref = f32[64,8,128]{2,1,0:T(8,128)S(1)} collective-permute-done((f32[64,8,128]{2,1,0:T(8,128)S(1)}, f32[64,8,128]{2,1,0:T(8,128)S(1)}, u32[]{:S(2)}, u32[]{:S(2)}) %collective-permute-start.12) | collective-permute-done | bytes 262176 | tf_op jit(solution)/shard_map/ppermute | solution.py:503
  73.4 0.9 combine.1
  74.4 3.4 %collective-permute-start.14 = (f32[17,8,128]{2,1,0:T(8,128)S(1)}, f32[17,8,128]{2,1,0:T(8,128)S(1)}, u32[]{:S(2)}, u32[]{:S(2)}) collective-permute-start(f32[17,8,128]{2,1,0:T(8,128)S(1)} %get-tuple-element.75), channel_id=1, source_target_pairs={{0,2},{1,3},{2,0},{3,1},{4,6},{5,7},{6,4},{7,5},{8,10},{9,11},{10,... | collective-permute-start | bytes 208904 | tf_op jit(solution)/shard_map/ppermute | solution.py:503
  77.8 0.8 collective-permute-done.13.refs_1_
  78.6 2.1 %collective-permute-done.14.refs_2_ = f32[17,8,128]{2,1,0:T(8,128)S(1)} collective-permute-done((f32[17,8,128]{2,1,0:T(8,128)S(1)}, f32[17,8,128]{2,1,0:T(8,128)S(1)}, u32[]{:S(2)}, u32[]{:S(2)}) %collective-permute-start.14) | collective-permute-done | bytes 69664 | tf_op jit(solution)/shard_map/ppermute | solution.py:503
  80.7 2.3 %collective-permute-done.15.refs_3_ = f32[17,8,128]{2,1,0:T(8,128)S(1)} collective-permute-done((f32[17,8,128]{2,1,0:T(8,128)S(1)}, f32[17,8,128]{2,1,0:T(8,128)S(1)}, u32[]{:S(2)}, u32[]{:S(2)}) %collective-permute-start.15) | collective-permute-done | bytes 69664 | tf_op jit(solution)/shard_map/ppermute | solution.py:503
  83.0 0.6 collective-permute-start.16
  83.7 4.3 %collective-permute-done.16.refs_1_ = f32[9,8,128]{2,1,0:T(8,128)S(1)} collective-permute-done((f32[9,8,128]{2,1,0:T(8,128)S(1)}, f32[9,8,128]{2,1,0:T(8,128)S(1)}, u32[]{:S(2)}, u32[]{:S(2)}) %collective-permute-start.16) | collective-permute-done | bytes 36896 | tf_op jit(solution)/shard_map/ppermute | solution.py:503
  88.0 1.8 %collective-permute-start.18 = (f32[9,8,128]{2,1,0:T(8,128)S(1)}, f32[9,8,128]{2,1,0:T(8,128)S(1)}, u32[]{:S(2)}, u32[]{:S(2)}) collective-permute-start(f32[9,8,128]{2,1,0:T(8,128)S(1)} %fold.3.refs_0_), channel_id=1, source_target_pairs={{0,16},{8,24},{16,0},{24,8},{1,17},{9,25},{17,1},{25,9},{2,18},{10... | collective-permute-start | bytes 110600 | tf_op jit(solution)/shard_map/ppermute | solution.py:503
  89.8 0.1 collective-permute-start.19
  89.9 2.1 %collective-permute-done.18.refs_2_ = f32[9,8,128]{2,1,0:T(8,128)S(1)} collective-permute-done((f32[9,8,128]{2,1,0:T(8,128)S(1)}, f32[9,8,128]{2,1,0:T(8,128)S(1)}, u32[]{:S(2)}, u32[]{:S(2)}) %collective-permute-start.18) | collective-permute-done | bytes 36896 | tf_op jit(solution)/shard_map/ppermute | solution.py:503
  92.0 1.2 %collective-permute-done.19.refs_3_ = f32[9,8,128]{2,1,0:T(8,128)S(1)} collective-permute-done((f32[9,8,128]{2,1,0:T(8,128)S(1)}, f32[9,8,128]{2,1,0:T(8,128)S(1)}, u32[]{:S(2)}, u32[]{:S(2)}) %collective-permute-start.19) | collective-permute-done | bytes 36896 | tf_op jit(solution)/shard_map/ppermute | solution.py:503
  93.2 0.7 finish.1
  (37 shorter events, 0.3 us)
Async XLA Ops:
  0.6 12.2 %copy-start = (f32[48,64,256]{2,1,0:T(8,128)S(1)}, f32[48,64,256]{2,1,0:T(8,128)}, u32[]{:S(2)}) copy-start(f32[48,64,256]{2,1,0:T(8,128)} %state_ref.3) | copy-start | bytes 9437188
  0.6 12.2 %copy-start.5 = (f32[6,6]{1,0:T(8,128)S(1)}, f32[6,6]{1,0:T(8,128)}, u32[]{:S(2)}) copy-start(f32[6,6]{1,0:T(8,128)} %coupling_ref.3) | copy-start | bytes 436
  0.7 12.2 %copy-start.7 = (f32[4]{0:T(128)S(1)}, f32[4]{0:T(128)}, u32[]{:S(2)}) copy-start(f32[4]{0:T(128)} %omega_ref.3) | copy-start | bytes 52
  0.7 12.2 %copy-start.8 = (f32[6]{0:T(128)S(1)}, f32[6]{0:T(128)}, u32[]{:S(2)}) copy-start(f32[6]{0:T(128)} %coef_ref.3) | copy-start | bytes 76
  0.7 12.2 %copy-start.4 = (f32[64,256]{1,0:T(8,128)S(1)}, f32[64,256]{1,0:T(8,128)}, u32[]{:S(2)}) copy-start(f32[64,256]{1,0:T(8,128)} %sigma_ref.3) | copy-start | bytes 196612
  4.0 8.8 %collective-permute-start = (f32[4,12,256]{2,1,0:T(8,128)}, f32[4,12,256]{2,1,0:T(8,128)S(1)}, u32[]{:S(2)}, u32[]{:S(2)}) collective-permute-start(f32[4,12,256]{2,1,0:T(8,128)} %get-tuple-element.42), channel_id=1, source_target_pairs={{0,8},{8,0},{16,24},{24,16},{1,9},{9,1},{17,25},{25,17},{2,10},{10... | collective-permute-start | bytes 147464 | tf_op jit(solution)/shard_map/ppermute | solution.py:503
  4.6 8.3 %collective-permute-start.1 = (f32[4,12,256]{2,1,0:T(8,128)}, f32[4,12,256]{2,1,0:T(8,128)S(1)}, u32[]{:S(2)}, u32[]{:S(2)}) collective-permute-start(f32[4,12,256]{2,1,0:T(8,128)} %get-tuple-element.43), channel_id=1, source_target_pairs={{8,16},{16,8},{9,17},{17,9},{10,18},{18,10},{11,19},{19,11},{12,20... | collective-permute-start | bytes 147464 | tf_op jit(solution)/shard_map/ppermute | solution.py:265
  5.2 7.6 %collective-permute-start.2 = (f32[64,128]{1,0:T(8,128)}, f32[64,128]{1,0:T(8,128)S(1)}, u32[]{:S(2)}, u32[]{:S(2)}) collective-permute-start(f32[64,128]{1,0:T(8,128)} %get-tuple-element.44), channel_id=1, source_target_pairs={{0,1},{1,0},{2,3},{3,2},{4,5},{5,4},{6,7},{7,6},{8,9},{9,8},{10,11... | collective-permute-start | bytes 98312 | tf_op jit(solution)/shard_map/ppermute | solution.py:503
  7.8 5.0 %collective-permute-start.3 = (f32[64,128]{1,0:T(8,128)}, f32[64,128]{1,0:T(8,128)S(1)}, u32[]{:S(2)}, u32[]{:S(2)}) collective-permute-start(f32[64,128]{1,0:T(8,128)} %get-tuple-element.45), channel_id=1, source_target_pairs={{1,2},{3,4},{5,6},{2,1},{4,3},{6,5},{9,10},{11,12},{13,14},{10,9},... | collective-permute-start | bytes 98312 | tf_op jit(solution)/shard_map/ppermute | solution.py:265
  8.5 18.5 %copy-start.1 = (f32[32,1024]{1,0:T(8,128)S(1)}, f32[32,1024]{1,0:T(8,128)}, u32[]{:S(2)}) copy-start(f32[32,1024]{1,0:T(8,128)} %get-tuple-element.69.refs_0_) | copy-start | bytes 393220
  8.5 23.2 %copy-start.2 = (f32[48,64,256]{2,1,0:T(8,128)S(1)}, f32[48,64,256]{2,1,0:T(8,128)}, u32[]{:S(2)}) copy-start(f32[48,64,256]{2,1,0:T(8,128)} %right_ref.3) | copy-start | bytes 9437188
  8.5 12.0 %collective-permute-start.4 = (f32[32,1024]{1,0:T(8,128)}, f32[32,1024]{1,0:T(8,128)S(1)}, u32[]{:S(2)}, u32[]{:S(2)}) collective-permute-start(f32[32,1024]{1,0:T(8,128)} %get-tuple-element.69.refs_0_), channel_id=1, source_target_pairs={{0,4},{1,5},{2,6},{3,7},{4,0},{5,1},{6,2},{7,3},{8,12},{9,13},{10,... | collective-permute-start | bytes 393224 | tf_op jit(solution)/shard_map/ppermute | solution.py:503
  20.5 11.2 %collective-permute-start.5 = (f32[4,12,256]{2,1,0:T(8,128)S(1)}, f32[4,12,256]{2,1,0:T(8,128)S(1)}, u32[]{:S(2)}, u32[]{:S(2)}) collective-permute-start(f32[4,12,256]{2,1,0:T(8,128)S(1)} %get-tuple-element.52), channel_id=1, source_target_pairs={{0,8},{8,0},{16,24},{24,16},{1,9},{9,1},{17,25},{25,17},{2,10},{10... | collective-permute-start | bytes 147464 | tf_op jit(solution)/shard_map/ppermute | solution.py:503
  22.6 9.1 %collective-permute-start.6 = (f32[4,12,256]{2,1,0:T(8,128)S(1)}, f32[4,12,256]{2,1,0:T(8,128)S(1)}, u32[]{:S(2)}, u32[]{:S(2)}) collective-permute-start(f32[4,12,256]{2,1,0:T(8,128)S(1)} %get-tuple-element.53), channel_id=1, source_target_pairs={{8,16},{16,8},{9,17},{17,9},{10,18},{18,10},{11,19},{19,11},{12,20... | collective-permute-start | bytes 147464 | tf_op jit(solution)/shard_map/ppermute | solution.py:265
  23.3 8.5 %collective-permute-start.7 = (f32[64,128]{1,0:T(8,128)S(1)}, f32[64,128]{1,0:T(8,128)S(1)}, u32[]{:S(2)}, u32[]{:S(2)}) collective-permute-start(f32[64,128]{1,0:T(8,128)S(1)} %get-tuple-element.54), channel_id=1, source_target_pairs={{0,1},{1,0},{2,3},{3,2},{4,5},{5,4},{6,7},{7,6},{8,9},{9,8},{10,11... | collective-permute-start | bytes 98312 | tf_op jit(solution)/shard_map/ppermute | solution.py:503
  26.3 5.4 %collective-permute-start.8 = (f32[64,128]{1,0:T(8,128)S(1)}, f32[64,128]{1,0:T(8,128)S(1)}, u32[]{:S(2)}, u32[]{:S(2)}) collective-permute-start(f32[64,128]{1,0:T(8,128)S(1)} %get-tuple-element.55), channel_id=1, source_target_pairs={{1,2},{3,4},{5,6},{2,1},{4,3},{6,5},{9,10},{11,12},{13,14},{10,9},... | collective-permute-start | bytes 98312 | tf_op jit(solution)/shard_map/ppermute | solution.py:265
  27.0 12.1 %collective-permute-start.9 = (f32[64,1024]{1,0:T(8,128)S(1)}, f32[64,1024]{1,0:T(8,128)S(1)}, u32[]{:S(2)}, u32[]{:S(2)}) collective-permute-start(f32[64,1024]{1,0:T(8,128)S(1)} %pad_maximum_fusion.1), channel_id=1, source_target_pairs={{0,2},{1,3},{2,0},{3,1},{4,6},{5,7},{6,4},{7,5},{8,10},{9,11},{10,... | collective-permute-start | bytes 786440 | tf_op jit(solution)/shard_map/ppermute | solution.py:503
  31.8 10.5 %copy-start.3 = (s32[256,128]{1,0:T(8,128)S(1)}, s32[256,128]{1,0:T(8,128)}, u32[]{:S(2)}) copy-start(s32[256,128]{1,0:T(8,128)} %cells_ref.1) | copy-start | bytes 393220
  31.8 10.4 %copy-start.6 = (s32[2,128]{1,0:T(2,128)S(1)}, s32[2,128]{1,0:T(2,128)}, u32[]{:S(2)}) copy-start(s32[2,128]{1,0:T(2,128)} %get-tuple-element.57) | copy-start | bytes 3076
  39.2 22.7 %collective-permute-start.10 = (f32[128,1024]{1,0:T(8,128)S(1)}, f32[128,1024]{1,0:T(8,128)S(1)}, u32[]{:S(2)}, u32[]{:S(2)}) collective-permute-start(f32[128,1024]{1,0:T(8,128)S(1)} %pad_maximum_fusion), channel_id=1, source_target_pairs={{0,1},{1,0},{2,3},{3,2},{4,5},{5,4},{6,7},{7,6},{8,9},{9,8},{10,11... | collective-permute-start | bytes 1572872 | tf_op jit(solution)/shard_map/ppermute | solution.py:503
  61.9 2.0 %collective-permute-start.11 = (f32[128,8,128]{2,1,0:T(8,128)S(1)}, f32[128,8,128]{2,1,0:T(8,128)S(1)}, u32[]{:S(2)}, u32[]{:S(2)}) collective-permute-start(f32[128,8,128]{2,1,0:T(8,128)S(1)} %get-tuple-element.68), channel_id=1, source_target_pairs={{0,8},{8,0},{16,24},{24,16},{1,9},{9,1},{17,25},{25,17},{2,10},{10... | collective-permute-start | bytes 1572872 | tf_op jit(solution)/shard_map/ppermute | solution.py:503
  64.0 9.4 %collective-permute-start.12 = (f32[64,8,128]{2,1,0:T(8,128)S(1)}, f32[64,8,128]{2,1,0:T(8,128)S(1)}, u32[]{:S(2)}, u32[]{:S(2)}) collective-permute-start(f32[64,8,128]{2,1,0:T(8,128)S(1)} %get-tuple-element.81), channel_id=1, source_target_pairs={{0,16},{8,24},{16,0},{24,8},{1,17},{9,25},{17,1},{25,9},{2,18},{10... | collective-permute-start | bytes 786440 | tf_op jit(solution)/shard_map/ppermute | solution.py:503
  74.3 4.3 %collective-permute-start.13 = (f32[17,8,128]{2,1,0:T(8,128)S(1)}, f32[17,8,128]{2,1,0:T(8,128)S(1)}, u32[]{:S(2)}, u32[]{:S(2)}) collective-permute-start(f32[17,8,128]{2,1,0:T(8,128)S(1)} %get-tuple-element.74), channel_id=1, source_target_pairs={{0,1},{1,0},{2,3},{3,2},{4,5},{5,4},{6,7},{7,6},{8,9},{9,8},{10,11... | collective-permute-start | bytes 208904 | tf_op jit(solution)/shard_map/ppermute | solution.py:503
  74.4 6.3 %collective-permute-start.14 = (f32[17,8,128]{2,1,0:T(8,128)S(1)}, f32[17,8,128]{2,1,0:T(8,128)S(1)}, u32[]{:S(2)}, u32[]{:S(2)}) collective-permute-start(f32[17,8,128]{2,1,0:T(8,128)S(1)} %get-tuple-element.75), channel_id=1, source_target_pairs={{0,2},{1,3},{2,0},{3,1},{4,6},{5,7},{6,4},{7,5},{8,10},{9,11},{10,... | collective-permute-start | bytes 208904 | tf_op jit(solution)/shard_map/ppermute | solution.py:503
  77.8 5.2 %collective-permute-start.15 = (f32[17,8,128]{2,1,0:T(8,128)S(1)}, f32[17,8,128]{2,1,0:T(8,128)S(1)}, u32[]{:S(2)}, u32[]{:S(2)}) collective-permute-start(f32[17,8,128]{2,1,0:T(8,128)S(1)} %get-tuple-element.76), channel_id=1, source_target_pairs={{0,3},{1,2},{2,1},{3,0},{4,7},{5,6},{6,5},{7,4},{8,11},{9,10},{10,... | collective-permute-start | bytes 208904 | tf_op jit(solution)/shard_map/ppermute | solution.py:503
  83.0 4.9 %collective-permute-start.16 = (f32[9,8,128]{2,1,0:T(8,128)S(1)}, f32[9,8,128]{2,1,0:T(8,128)S(1)}, u32[]{:S(2)}, u32[]{:S(2)}) collective-permute-start(f32[9,8,128]{2,1,0:T(8,128)S(1)} %get-tuple-element.78), channel_id=1, source_target_pairs={{0,4},{1,5},{2,6},{3,7},{4,0},{5,1},{6,2},{7,3},{8,12},{9,13},{10,... | collective-permute-start | bytes 110600 | tf_op jit(solution)/shard_map/ppermute | solution.py:503
  88.0 1.9 %collective-permute-start.17 = (f32[9,8,128]{2,1,0:T(8,128)S(1)}, f32[9,8,128]{2,1,0:T(8,128)S(1)}, u32[]{:S(2)}, u32[]{:S(2)}) collective-permute-start(f32[9,8,128]{2,1,0:T(8,128)S(1)} %fold.3.refs_0_), channel_id=1, source_target_pairs={{0,8},{8,0},{16,24},{24,16},{1,9},{9,1},{17,25},{25,17},{2,10},{10... | collective-permute-start | bytes 110600 | tf_op jit(solution)/shard_map/ppermute | solution.py:503
  88.0 4.0 %collective-permute-start.18 = (f32[9,8,128]{2,1,0:T(8,128)S(1)}, f32[9,8,128]{2,1,0:T(8,128)S(1)}, u32[]{:S(2)}, u32[]{:S(2)}) collective-permute-start(f32[9,8,128]{2,1,0:T(8,128)S(1)} %fold.3.refs_0_), channel_id=1, source_target_pairs={{0,16},{8,24},{16,0},{24,8},{1,17},{9,25},{17,1},{25,9},{2,18},{10... | collective-permute-start | bytes 110600 | tf_op jit(solution)/shard_map/ppermute | solution.py:503
  89.8 3.4 %collective-permute-start.19 = (f32[9,8,128]{2,1,0:T(8,128)S(1)}, f32[9,8,128]{2,1,0:T(8,128)S(1)}, u32[]{:S(2)}, u32[]{:S(2)}) collective-permute-start(f32[9,8,128]{2,1,0:T(8,128)S(1)} %fold.3.refs_0_), channel_id=1, source_target_pairs={{0,24},{8,16},{16,8},{24,0},{1,25},{9,17},{17,9},{25,1},{2,26},{10... | collective-permute-start | bytes 110600 | tf_op jit(solution)/shard_map/ppermute | solution.py:503

commit v4 on v3

--- a/solution.py
+++ b/solution.py
@@ -106,60 +106,62 @@
     row2_ref,
     col1_ref,
     col2_ref,
-    new_ref,
     *rest,
 ):
-    nbs_ref, a_ref, b_ref, rhs_ref, sems = rest[-5:]
+    *outs, nbs0_ref, nbs1_ref, a0_ref, a1_ref, b0_ref, b1_ref, rhs_ref, new_ref, in_sems, out_sems = rest
+    nbs_refs, a_refs, b_refs = (nbs0_ref, nbs1_ref), (a0_ref, a1_ref), (b0_ref, b1_ref)
+    modes = omega_ref.shape[0]
+    planes, rows, cols = nbs0_ref.shape
+    nvar = planes // 2
+    parts = 2 * modes
+    blocks = [pl.ds(mode * planes, planes) for mode in range(modes)]
+    fetches = [
+        pltpu.make_async_copy(right_ref.at[block], rhs_ref.at[block], in_sems.at[mode])
+        for mode, block in enumerate(blocks)
+    ]
+    for fetch in fetches:
+        fetch.start()
     if last:
-        table_ref, press_ref = rest[:2]
-    mode = pl.program_id(0)
-    planes, rows, cols = state_ref.shape
-    nvar = planes // 2
-    parts = 2 * omega_ref.shape[0]
-    slot = lax.rem(mode, 2)
-
-    def fetch(which):
-        into = lax.rem(which, 2)
-        block = pl.ds(which * planes, planes)
-        return pltpu.make_async_copy(right_ref.at[block], rhs_ref.at[into], sems.at[into])
-
-    @pl.when(mode == 0)
-    def _():
-        fetch(mode).start()
-
-    @pl.when(mode + 1 < pl.num_programs(0))
-    def _():
-        fetch(mode + 1).start()
-
-    freq = omega_ref[mode]
-    dval = 4.0 + sigma_ref[...]
-    scale = 0.8 / (dval * dval + freq * freq)
-    a_ref[...] = dval * scale
-    b_ref[...] = freq * scale
+        field_ref, table_ref, press_ref = outs
+        sends = [
+            pltpu.make_async_copy(new_ref.at[block], field_ref.at[block], out_sems.at[mode])
+            for mode, block in enumerate(blocks)
+        ]
+    else:
+        new_ref, *edge_refs = outs
+        edge_refs[2][...] = jnp.zeros_like(edge_refs[2])
+        edge_refs[3][...] = jnp.zeros_like(edge_refs[3])
 
     even_x = lax.rem(lax.axis_index("gx"), 2) == 0
     even_y = lax.rem(lax.axis_index("gy"), 2) == 0
-    above_rows = jnp.where(even_x, row2_ref[0], row1_ref[0])
-    below_rows = jnp.where(even_x, row1_ref[0], row2_ref[0])
     west_cols = jnp.where(even_y, col2_ref[...], col1_ref[...])
     east_cols = jnp.where(even_y, col1_ref[...], col2_ref[...])
     row = lax.broadcasted_iota(jnp.int32, (rows, cols), 0)
     lane = lax.broadcasted_iota(jnp.int32, (rows, LANES), 1)
-    for k in range(planes):
+
+    def factors(mode):
+        freq = omega_ref[mode]
+        dval = 4.0 + sigma_ref[...]
+        scale = 0.8 / (dval * dval + freq * freq)
+        a_refs[mode % 2][...] = dval * scale
+        b_refs[mode % 2][...] = freq * scale
+
+    def neighbours(mode, k):
+        nbs_ref = nbs_refs[mode % 2]
         comp = mode * planes + k
-        plane = state_ref[k]
-        total = jnp.where(row == 0, above_rows[k : k + 1], pltpu.roll(plane, 1, 0))
-        total = total + jnp.where(
-            row == rows - 1, below_rows[k : k + 1], pltpu.roll(plane, rows - 1, 0)
-        )
-        west = pltpu.roll(west_cols, lax.rem(LANES - comp, LANES), 1)
+        plane = state_ref[comp]
+        row1 = row1_ref[mode, k : k + 1, :]
+        row2 = row2_ref[mode, k : k + 1, :]
+        above = jnp.where(even_x, row2, row1)
+        below = jnp.where(even_x, row1, row2)
+        total = jnp.where(row == 0, above, pltpu.roll(plane, 1, 0))
+        total = total + jnp.where(row == rows - 1, below, pltpu.roll(plane, rows - 1, 0))
+        west = pltpu.roll(west_cols, (LANES - comp) % LANES, 1)
         east = pltpu.roll(east_cols, LANES - 1 - comp, 1)
         from_west = pltpu.roll(plane, 1, 1)
         from_east = pltpu.roll(plane, cols - 1, 1)
         nbs_ref[k, :, :LANES] = (
-            total[:, :LANES]
-            + jnp.where(lane == 0, west, from_west[:, :LANES])
-            + from_east[:, :LANES]
+            total[:, :LANES] + jnp.where(lane == 0, west, from_west[:, :LANES]) + from_east[:, :LANES]
         )
         nbs_ref[k, :, cols - LANES :] = (
             total[:, cols - LANES :]
@@ -170,22 +172,23 @@
     weight = [[coupling_ref[v, w] for w in range(nvar)] for v in range(nvar)]
     coef = [coef_ref[v] for v in range(nvar)]
 
-    def strip(step, carry):
-        here = pl.ds(pl.multiple_of(step * 8, 8), 8)
-        nbs = [nbs_ref[k, here, :] for k in range(planes)]
-        a = a_ref[here, :]
-        b = b_ref[here, :]
+    def strip(mode, step):
+        here = slice(step * 8, step * 8 + 8)
+        base = mode * planes
+        nbs = [nbs_refs[mode % 2][k, here, :] for k in range(planes)]
+        a = a_refs[mode % 2][here, :]
+        b = b_refs[mode % 2][here, :]
         press_re = press_im = None
         for v in range(nvar):
-            res_re = rhs_ref[slot, v, here, :]
-            res_im = rhs_ref[slot, nvar + v, here, :]
+            res_re = rhs_ref[base + v, here, :]
+            res_im = rhs_ref[base + nvar + v, here, :]
             for w in range(nvar):
                 res_re = res_re + weight[v][w] * nbs[w]
                 res_im = res_im + weight[v][w] * nbs[nvar + w]
-            new_re = 0.2 * state_ref[v, here, :] + a * res_re + b * res_im
-            new_im = 0.2 * state_ref[nvar + v, here, :] + a * res_im - b * res_re
-            new_ref[v, here, :] = new_re
-            new_ref[nvar + v, here, :] = new_im
+            new_re = 0.2 * state_ref[base + v, here, :] + a * res_re + b * res_im
+            new_im = 0.2 * state_ref[base + nvar + v, here, :] + a * res_im - b * res_re
+            new_ref[base + v, here, :] = new_re
+            new_ref[base + nvar + v, here, :] = new_im
             if last:
                 press_re = coef[v] * new_re if v == 0 else press_re + coef[v] * new_re
                 press_im = coef[v] * new_im if v == 0 else press_im + coef[v] * new_im
@@ -195,48 +198,57 @@
                 for half in range(cols // LANES):
                     piece = value[:, half * LANES : (half + 1) * LANES]
                     press_ref[half, pl.ds(start, 8, stride=parts), :] = piece
-        return carry
-
-    fetch(mode).wait()
-    lax.fori_loop(0, rows // 8, strip, 0, unroll=True)
+
+    factors(0)
+    for k in range(planes):
+        neighbours(0, k)
+    steps = rows // 8
+    for mode in range(modes):
+        fetches[mode].wait()
+        if mode + 1 < modes:
+            factors(mode + 1)
+        for step in range(steps):
+            strip(mode, step)
+            if mode + 1 < modes:
+                for k in range(planes * step // steps, planes * (step + 1) // steps):
+                    neighbours(mode + 1, k)
+        if last:
+            sends[mode].start()
+        else:
+            here = pl.ds(mode, 1)
+            pack_edges(
+                new_ref.at[blocks[mode]],
+                mode * planes,
+                planes,
+                edge_refs[0].at[here],
+                edge_refs[1].at[here],
+                edge_refs[2],
+                edge_refs[3],
+            )
     if last:
-
-        @pl.when(mode == pl.num_programs(0) - 1)
-        def _():
-            size = table_ref.shape[0] // 2
-            for half in range(cols // LANES):
-                whole = press_ref[half]
-                high = whole.astype(BF16)
-                span = slice(half * LANES, (half + 1) * LANES)
-                table_ref[:size, span] = high
-                table_ref[size:, span] = (whole - high.astype(F32)).astype(BF16)
-
-    else:
-        up_ref, down_ref, left_ref, right_ref = rest[:4]
-
-        @pl.when(mode == 0)
-        def _():
-            left_ref[...] = jnp.zeros_like(left_ref)
-            right_ref[...] = jnp.zeros_like(right_ref)
-
-        pack_edges(new_ref, mode * planes, planes, up_ref, down_ref, left_ref, right_ref)
+        size = table_ref.shape[0] // 2
+        for half in range(cols // LANES):
+            whole = press_ref[half]
+            high = whole.astype(BF16)
+            span = slice(half * LANES, (half + 1) * LANES)
+            table_ref[:size, span] = high
+            table_ref[size:, span] = (whole - high.astype(F32)).astype(BF16)
+        for send in sends:
+            send.wait()
 
 
 def edge_shapes(modes, planes, rows, cols):
-    shapes = (
+    return (
         jax.ShapeDtypeStruct((modes, planes, cols), F32),
         jax.ShapeDtypeStruct((modes, planes, cols), F32),
         jax.ShapeDtypeStruct((rows, LANES), F32),
         jax.ShapeDtypeStruct((rows, LANES), F32),
     )
-    row_spec = pl.BlockSpec((1, planes, cols), lambda m: (m, 0, 0))
-    col_spec = pl.BlockSpec((rows, LANES), lambda m: (0, 0))
-    return shapes, (row_spec, row_spec, col_spec, col_spec)
 
 
 def pack(state, modes, mode_shape, correction, owner, panel):
     comp, rows, cols = state.shape
-    shapes, _ = edge_shapes(modes, comp // modes, rows, cols)
+    shapes = edge_shapes(modes, comp // modes, rows, cols)
     share = (mode_shape.shape[0], mode_shape.shape[1] // lax.axis_size("gx"))
     hbm = pl.BlockSpec(memory_space=pltpu.HBM)
     return pl.pallas_call(
@@ -270,35 +282,31 @@
     comp, rows, cols = field.shape
     modes = omega.shape[0]
     planes = comp // modes
-    edges, edge_specs = edge_shapes(modes, planes, rows, cols)
-    block = pl.BlockSpec((planes, rows, cols), lambda m: (m, 0, 0))
+    hbm = pl.BlockSpec(memory_space=pltpu.HBM)
     if last:
-        table = (4 * modes * rows, cols)
-        press = (cols // LANES, 2 * modes * rows, LANES)
-        extra = (jax.ShapeDtypeStruct(table, BF16), jax.ShapeDtypeStruct(press, F32))
-        extra_specs = (pl.BlockSpec(table, lambda m: (0, 0)), pl.BlockSpec(press, lambda m: (0, 0, 0)))
+        extra = (
+            jax.ShapeDtypeStruct((4 * modes * rows, cols), BF16),
+            jax.ShapeDtypeStruct((cols // LANES, 2 * modes * rows, LANES), F32),
+        )
     else:
-        extra, extra_specs = edges, edge_specs
+        extra = edge_shapes(modes, planes, rows, cols)
+    plane = pltpu.VMEM((rows, cols), F32)
     return pl.pallas_call(
         functools.partial(sweep_kernel, last),
-        grid=(modes,),
         out_shape=(jax.ShapeDtypeStruct(field.shape, F32),) + extra,
-        in_specs=[
-            smem(),
-            smem(),
-            smem(),
-            block,
-            pl.BlockSpec(memory_space=pltpu.HBM),
-            pl.BlockSpec((rows, cols), lambda m: (0, 0)),
-            *edge_specs,
-        ],
-        out_specs=(block,) + extra_specs,
+        in_specs=[smem(), smem(), smem(), vmem(), hbm] + [vmem()] * 5,
+        out_specs=(hbm if last else vmem(),) + (vmem(),) * len(extra),
         scratch_shapes=[
             pltpu.VMEM((planes, rows, cols), F32),
-            pltpu.VMEM((rows, cols), F32),
-            pltpu.VMEM((rows, cols), F32),
-            pltpu.VMEM((2, planes, rows, cols), F32),
-            pltpu.SemaphoreType.DMA((2,)),
+            pltpu.VMEM((planes, rows, cols), F32),
+            plane,
+            plane,
+            plane,
+            plane,
+            pltpu.VMEM(rhs.shape, F32),
+            pltpu.VMEM(field.shape if last else (8, LANES), F32),
+            pltpu.SemaphoreType.DMA((modes,)),
+            pltpu.SemaphoreType.DMA((modes,)),
         ],
         compiler_params=pltpu.CompilerParams(vmem_limit_bytes=VMEM_SWEEP),
         cost_estimate=pl.CostEstimate(flops=8 * 10**9, bytes_accessed=12 * field.size, transcendentals=0),

time: 94.1 us -> 92.3 us (0.981)
  Pallas kernels: 39.3 us -> 37.5 us
    pallas_call x2, Pallas kernels: 14.6 us -> 12.8 us  [sweep(): pl.pallas_call(functools.partial(sweep_kernel, last), out_shape=(jax.Shap...]
  transfers between devices with their start and end apart: 20 -> 20, of which waited for: 9 -> 9; matrix products, arithmetic and copies ran while one was open for 0% -> 0% of each run, Pallas kernels for 37% -> 35%
where the time goes in v4:
time: 92.3 us; the launch traced here: 92.1 us
  Pallas kernels  37.5 us (41%)
  starting transfers between devices  31.5 us (34%)
  waiting for transfers between devices  22.1 us (24%)
    ppermute x16, starting transfers between devices, swap(): lax.ppermute(send, axis, [(i, i ^ bit) for i in range(lax.axis_size(axis))])  28.7 us
    ppermute x16, waiting for transfers between devices, swap(): lax.ppermute(send, axis, [(i, i ^ bit) for i in range(lax.axis_size(axis))])  22.1 us
    pallas_call x1, Pallas kernels, tile_sums(): pl.pallas_call(tile_kernel, grid=(tiles // block,), out_shape=(jax.ShapeD...  19.7 us
    pallas_call x2, Pallas kernels, sweep(): pl.pallas_call(functools.partial(sweep_kernel, last), out_shape=(jax.Shap...  12.8 us
    pallas_call x1, Pallas kernels, pack(): pl.pallas_call(functools.partial(pack_kernel, modes), out_shape=shapes +...  3.35 us
    ppermute x4, starting transfers between devices, exchange(): got.append(lax.ppermute(second, axis, pairs + [(b, a) for a, b in pairs]))  2.79 us
  transfers between devices with their start and end apart: 20, of which 9 were waited for; matrix products, arithmetic and copies ran while one was open for 0% of the time, Pallas kernels for 35%

profile of v4, /device:TPU:0, one launch (start us, length us, event | category | flops | bytes accessed | tf_op | source)
XLA Modules:
  0.0 92.1 jit_solution(2608837148193816410)
XLA Ops:
  0.7 3.4 %pack.1 = (f32[4,12,256]{2,1,0:T(8,128)}, f32[4,12,256]{2,1,0:T(8,128)}, f32[64,128]{1,0:T(8,128)}, f32[64,128]{1,0:T(8,128)}, f32[32,1024]{1,0:T(8,128)}, /*index=5*/s32[2,128]{1,0:T(2,128)}) custom-call(f32[48,64,256]{2,1,0:T(8,128)} %state_ref.3, f32[32,4096]{1,0:T(8,128)} %shape_ref.1, f32[1,4096]{1,0:T(1,128)} %bitcast.5, s32[2,128]{1,0:T(2,128)} %bitcast.6, ...), custom_call_target="tpu_custom_call" | custom-call | tf_op jit(solution)/shard_map/pack/pallas_call | solution.py:254
  4.0 0.5 collective-permute-start
  4.6 0.7 collective-permute-start.1
  5.2 2.6 %collective-permute-start.2 = (f32[64,128]{1,0:T(8,128)}, f32[64,128]{1,0:T(8,128)S(1)}, u32[]{:S(2)}, u32[]{:S(2)}) collective-permute-start(f32[64,128]{1,0:T(8,128)} %get-tuple-element.44), channel_id=1, source_target_pairs={{0,1},{1,0},{2,3},{3,2},{4,5},{5,4},{6,7},{7,6},{8,9},{9,8},{10,11... | collective-permute-start | bytes 98312 | tf_op jit(solution)/shard_map/ppermute | solution.py:511
  7.8 0.7 collective-permute-start.3
  8.5 4.3 %collective-permute-start.4 = (f32[32,1024]{1,0:T(8,128)}, f32[32,1024]{1,0:T(8,128)S(1)}, u32[]{:S(2)}, u32[]{:S(2)}) collective-permute-start(f32[32,1024]{1,0:T(8,128)} %get-tuple-element.69.refs_0_), channel_id=1, source_target_pairs={{0,4},{1,5},{2,6},{3,7},{4,0},{5,1},{6,2},{7,3},{8,12},{9,13},{10,... | collective-permute-start | bytes 393224 | tf_op jit(solution)/shard_map/ppermute | solution.py:511
  12.9 6.3 %sweep.2 = (f32[48,64,256]{2,1,0:T(8,128)S(1)}, f32[4,12,256]{2,1,0:T(8,128)S(1)}, f32[4,12,256]{2,1,0:T(8,128)S(1)}, f32[64,128]{1,0:T(8,128)S(1)}, f32[64,128]{1,0:T(8,128)S(1)}) custom-call(f32[6,6]{1,0:T(8,128)S(1)} %copy-done.5, f32[4]{0:T(128)S(1)} %copy-done.7, f32[6]{0:T(128)S(1)} %copy-done.8, f32[48,64,256]{2,1,0:T(8,128)S(1)} %copy-done, ...), custom_call_target="tpu_custom_call" | custom-call | flops 8000000000 | bytes 9437184 | tf_op jit(solution)/shard_map/sweep/pallas_call | solution.py:294
  19.2 2.1 %collective-permute-start.5 = (f32[4,12,256]{2,1,0:T(8,128)S(1)}, f32[4,12,256]{2,1,0:T(8,128)S(1)}, u32[]{:S(2)}, u32[]{:S(2)}) collective-permute-start(f32[4,12,256]{2,1,0:T(8,128)S(1)} %get-tuple-element.52), channel_id=1, source_target_pairs={{0,8},{8,0},{16,24},{24,16},{1,9},{9,1},{17,25},{25,17},{2,10},{10... | collective-permute-start | bytes 147464 | tf_op jit(solution)/shard_map/ppermute | solution.py:511
  21.3 0.7 collective-permute-start.6
  22.0 3.1 %collective-permute-start.7 = (f32[64,128]{1,0:T(8,128)S(1)}, f32[64,128]{1,0:T(8,128)S(1)}, u32[]{:S(2)}, u32[]{:S(2)}) collective-permute-start(f32[64,128]{1,0:T(8,128)S(1)} %get-tuple-element.54), channel_id=1, source_target_pairs={{0,1},{1,0},{2,3},{3,2},{4,5},{5,4},{6,7},{7,6},{8,9},{9,8},{10,11... | collective-permute-start | bytes 98312 | tf_op jit(solution)/shard_map/ppermute | solution.py:511
  25.0 0.8 collective-permute-start.8
  25.9 4.7 %collective-permute-start.9 = (f32[64,1024]{1,0:T(8,128)S(1)}, f32[64,1024]{1,0:T(8,128)S(1)}, u32[]{:S(2)}, u32[]{:S(2)}) collective-permute-start(f32[64,1024]{1,0:T(8,128)S(1)} %pad_maximum_fusion.1), channel_id=1, source_target_pairs={{0,2},{1,3},{2,0},{3,1},{4,6},{5,7},{6,4},{7,5},{8,10},{9,11},{10,... | collective-permute-start | bytes 786440 | tf_op jit(solution)/shard_map/ppermute | solution.py:511
  30.7 6.5 %sweep.3 = (f32[48,64,256]{2,1,0:T(8,128)}, bf16[1024,256]{1,0:T(8,128)(2,1)S(1)}, f32[2,512,128]{2,1,0:T(8,128)S(1)}) custom-call(f32[6,6]{1,0:T(8,128)S(1)} %copy-done.5, f32[4]{0:T(128)S(1)} %copy-done.7, f32[6]{0:T(128)S(1)} %copy-done.8, f32[48,64,256]{2,1,0:T(8,128)S(1)} %get-tuple-element.46.state_ref, f32[48,64,256]{2,1,0:T(8,128)S(1)} %copy-done.2, ...), custom_call_target="tpu_custom_call" | custom-call | flops 8000000000 | bytes 9437184 | tf_op jit(solution)/shard_map/sweep/pallas_call | solution.py:294
  37.1 0.7 collective-permute-done.9.refs_2_
  37.9 3.2 %collective-permute-start.10 = (f32[128,1024]{1,0:T(8,128)S(1)}, f32[128,1024]{1,0:T(8,128)S(1)}, u32[]{:S(2)}, u32[]{:S(2)}) collective-permute-start(f32[128,1024]{1,0:T(8,128)S(1)} %pad_maximum_fusion), channel_id=1, source_target_pairs={{0,1},{1,0},{2,3},{3,2},{4,5},{5,4},{6,7},{7,6},{8,9},{9,8},{10,11... | collective-permute-start | bytes 1572872 | tf_op jit(solution)/shard_map/ppermute | solution.py:511
  41.1 19.7 %tiles.1 = (f32[128,8,128]{2,1,0:T(8,128)S(1)}, f32[128,8,128]{2,1,0:T(8,128)S(1)}) custom-call(s32[256]{0:T(256)S(1)} %bitcast.4, bf16[1024,256]{1,0:T(8,128)(2,1)S(1)} %get-tuple-element.61.table_ref, f32[2,512,128]{2,1,0:T(8,128)S(1)} %get-tuple-element.62.press_ref, s32[256,128]{1,0:T(8,128)S(1)} %copy-done.3, f32[256,128,128]{2,1,0:T(8,128)} %interp_ref.1), custom_call_target="tpu_custom_call" | custom-call | flops 17179869184 | bytes 16777216 | tf_op jit(solution)/shard_map/tiles/pallas_call | solution.py:409
  60.8 0.1 collective-permute-start.11
  60.9 1.9 %collective-permute-done.11 = f32[128,8,128]{2,1,0:T(8,128)S(1)} collective-permute-done((f32[128,8,128]{2,1,0:T(8,128)S(1)}, f32[128,8,128]{2,1,0:T(8,128)S(1)}, u32[]{:S(2)}, u32[]{:S(2)}) %collective-permute-start.11) | collective-permute-done | bytes 524320 | tf_op jit(solution)/shard_map/ppermute | solution.py:511
  62.8 2.1 %collective-permute-start.12 = (f32[64,8,128]{2,1,0:T(8,128)S(1)}, f32[64,8,128]{2,1,0:T(8,128)S(1)}, u32[]{:S(2)}, u32[]{:S(2)}) collective-permute-start(f32[64,8,128]{2,1,0:T(8,128)S(1)} %get-tuple-element.81), channel_id=1, source_target_pairs={{0,16},{8,24},{16,0},{24,8},{1,17},{9,25},{17,1},{25,9},{2,18},{10... | collective-permute-start | bytes 786440 | tf_op jit(solution)/shard_map/ppermute | solution.py:511
  65.0 6.6 %collective-permute-done.12.got_ref = f32[64,8,128]{2,1,0:T(8,128)S(1)} collective-permute-done((f32[64,8,128]{2,1,0:T(8,128)S(1)}, f32[64,8,128]{2,1,0:T(8,128)S(1)}, u32[]{:S(2)}, u32[]{:S(2)}) %collective-permute-start.12) | collective-permute-done | bytes 262176 | tf_op jit(solution)/shard_map/ppermute | solution.py:511
  71.6 0.9 combine.1
  72.6 3.4 %collective-permute-start.14 = (f32[17,8,128]{2,1,0:T(8,128)S(1)}, f32[17,8,128]{2,1,0:T(8,128)S(1)}, u32[]{:S(2)}, u32[]{:S(2)}) collective-permute-start(f32[17,8,128]{2,1,0:T(8,128)S(1)} %get-tuple-element.75), channel_id=1, source_target_pairs={{0,2},{1,3},{2,0},{3,1},{4,6},{5,7},{6,4},{7,5},{8,10},{9,11},{10,... | collective-permute-start | bytes 208904 | tf_op jit(solution)/shard_map/ppermute | solution.py:511
  76.0 0.8 collective-permute-done.13.refs_1_
  76.8 2.1 %collective-permute-done.14.refs_2_ = f32[17,8,128]{2,1,0:T(8,128)S(1)} collective-permute-done((f32[17,8,128]{2,1,0:T(8,128)S(1)}, f32[17,8,128]{2,1,0:T(8,128)S(1)}, u32[]{:S(2)}, u32[]{:S(2)}) %collective-permute-start.14) | collective-permute-done | bytes 69664 | tf_op jit(solution)/shard_map/ppermute | solution.py:511
  78.9 2.3 %collective-permute-done.15.refs_3_ = f32[17,8,128]{2,1,0:T(8,128)S(1)} collective-permute-done((f32[17,8,128]{2,1,0:T(8,128)S(1)}, f32[17,8,128]{2,1,0:T(8,128)S(1)}, u32[]{:S(2)}, u32[]{:S(2)}) %collective-permute-start.15) | collective-permute-done | bytes 69664 | tf_op jit(solution)/shard_map/ppermute | solution.py:511
  81.2 0.6 collective-permute-start.16
  81.9 4.3 %collective-permute-done.16.refs_1_ = f32[9,8,128]{2,1,0:T(8,128)S(1)} collective-permute-done((f32[9,8,128]{2,1,0:T(8,128)S(1)}, f32[9,8,128]{2,1,0:T(8,128)S(1)}, u32[]{:S(2)}, u32[]{:S(2)}) %collective-permute-start.16) | collective-permute-done | bytes 36896 | tf_op jit(solution)/shard_map/ppermute | solution.py:511
  86.2 1.8 %collective-permute-start.18 = (f32[9,8,128]{2,1,0:T(8,128)S(1)}, f32[9,8,128]{2,1,0:T(8,128)S(1)}, u32[]{:S(2)}, u32[]{:S(2)}) collective-permute-start(f32[9,8,128]{2,1,0:T(8,128)S(1)} %fold.3.refs_0_), channel_id=1, source_target_pairs={{0,16},{8,24},{16,0},{24,8},{1,17},{9,25},{17,1},{25,9},{2,18},{10... | collective-permute-start | bytes 110600 | tf_op jit(solution)/shard_map/ppermute | solution.py:511
  88.0 0.1 collective-permute-start.19
  88.1 2.1 %collective-permute-done.18.refs_2_ = f32[9,8,128]{2,1,0:T(8,128)S(1)} collective-permute-done((f32[9,8,128]{2,1,0:T(8,128)S(1)}, f32[9,8,128]{2,1,0:T(8,128)S(1)}, u32[]{:S(2)}, u32[]{:S(2)}) %collective-permute-start.18) | collective-permute-done | bytes 36896 | tf_op jit(solution)/shard_map/ppermute | solution.py:511
  90.2 1.2 %collective-permute-done.19.refs_3_ = f32[9,8,128]{2,1,0:T(8,128)S(1)} collective-permute-done((f32[9,8,128]{2,1,0:T(8,128)S(1)}, f32[9,8,128]{2,1,0:T(8,128)S(1)}, u32[]{:S(2)}, u32[]{:S(2)}) %collective-permute-start.19) | collective-permute-done | bytes 36896 | tf_op jit(solution)/shard_map/ppermute | solution.py:511
  91.4 0.7 finish.1
  (37 shorter events, 0.3 us)
Async XLA Ops:
  0.6 12.2 %copy-start = (f32[48,64,256]{2,1,0:T(8,128)S(1)}, f32[48,64,256]{2,1,0:T(8,128)}, u32[]{:S(2)}) copy-start(f32[48,64,256]{2,1,0:T(8,128)} %state_ref.3) | copy-start | bytes 9437188
  0.6 12.2 %copy-start.5 = (f32[6,6]{1,0:T(8,128)S(1)}, f32[6,6]{1,0:T(8,128)}, u32[]{:S(2)}) copy-start(f32[6,6]{1,0:T(8,128)} %coupling_ref.3) | copy-start | bytes 436
  0.7 12.2 %copy-start.7 = (f32[4]{0:T(128)S(1)}, f32[4]{0:T(128)}, u32[]{:S(2)}) copy-start(f32[4]{0:T(128)} %omega_ref.3) | copy-start | bytes 52
  0.7 12.2 %copy-start.8 = (f32[6]{0:T(128)S(1)}, f32[6]{0:T(128)}, u32[]{:S(2)}) copy-start(f32[6]{0:T(128)} %coef_ref.3) | copy-start | bytes 76
  0.7 12.2 %copy-start.4 = (f32[64,256]{1,0:T(8,128)S(1)}, f32[64,256]{1,0:T(8,128)}, u32[]{:S(2)}) copy-start(f32[64,256]{1,0:T(8,128)} %sigma_ref.3) | copy-start | bytes 196612
  4.0 8.8 %collective-permute-start = (f32[4,12,256]{2,1,0:T(8,128)}, f32[4,12,256]{2,1,0:T(8,128)S(1)}, u32[]{:S(2)}, u32[]{:S(2)}) collective-permute-start(f32[4,12,256]{2,1,0:T(8,128)} %get-tuple-element.42), channel_id=1, source_target_pairs={{0,8},{8,0},{16,24},{24,16},{1,9},{9,1},{17,25},{25,17},{2,10},{10... | collective-permute-start | bytes 147464 | tf_op jit(solution)/shard_map/ppermute | solution.py:511
  4.6 8.3 %collective-permute-start.1 = (f32[4,12,256]{2,1,0:T(8,128)}, f32[4,12,256]{2,1,0:T(8,128)S(1)}, u32[]{:S(2)}, u32[]{:S(2)}) collective-permute-start(f32[4,12,256]{2,1,0:T(8,128)} %get-tuple-element.43), channel_id=1, source_target_pairs={{8,16},{16,8},{9,17},{17,9},{10,18},{18,10},{11,19},{19,11},{12,20... | collective-permute-start | bytes 147464 | tf_op jit(solution)/shard_map/ppermute | solution.py:277
  5.2 7.6 %collective-permute-start.2 = (f32[64,128]{1,0:T(8,128)}, f32[64,128]{1,0:T(8,128)S(1)}, u32[]{:S(2)}, u32[]{:S(2)}) collective-permute-start(f32[64,128]{1,0:T(8,128)} %get-tuple-element.44), channel_id=1, source_target_pairs={{0,1},{1,0},{2,3},{3,2},{4,5},{5,4},{6,7},{7,6},{8,9},{9,8},{10,11... | collective-permute-start | bytes 98312 | tf_op jit(solution)/shard_map/ppermute | solution.py:511
  7.8 5.0 %collective-permute-start.3 = (f32[64,128]{1,0:T(8,128)}, f32[64,128]{1,0:T(8,128)S(1)}, u32[]{:S(2)}, u32[]{:S(2)}) collective-permute-start(f32[64,128]{1,0:T(8,128)} %get-tuple-element.45), channel_id=1, source_target_pairs={{1,2},{3,4},{5,6},{2,1},{4,3},{6,5},{9,10},{11,12},{13,14},{10,9},... | collective-permute-start | bytes 98312 | tf_op jit(solution)/shard_map/ppermute | solution.py:277
  8.5 17.4 %copy-start.1 = (f32[32,1024]{1,0:T(8,128)S(1)}, f32[32,1024]{1,0:T(8,128)}, u32[]{:S(2)}) copy-start(f32[32,1024]{1,0:T(8,128)} %get-tuple-element.69.refs_0_) | copy-start | bytes 393220
  8.5 22.1 %copy-start.2 = (f32[48,64,256]{2,1,0:T(8,128)S(1)}, f32[48,64,256]{2,1,0:T(8,128)}, u32[]{:S(2)}) copy-start(f32[48,64,256]{2,1,0:T(8,128)} %right_ref.3) | copy-start | bytes 9437188
  8.5 10.7 %collective-permute-start.4 = (f32[32,1024]{1,0:T(8,128)}, f32[32,1024]{1,0:T(8,128)S(1)}, u32[]{:S(2)}, u32[]{:S(2)}) collective-permute-start(f32[32,1024]{1,0:T(8,128)} %get-tuple-element.69.refs_0_), channel_id=1, source_target_pairs={{0,4},{1,5},{2,6},{3,7},{4,0},{5,1},{6,2},{7,3},{8,12},{9,13},{10,... | collective-permute-start | bytes 393224 | tf_op jit(solution)/shard_map/ppermute | solution.py:511
  19.2 11.4 %collective-permute-start.5 = (f32[4,12,256]{2,1,0:T(8,128)S(1)}, f32[4,12,256]{2,1,0:T(8,128)S(1)}, u32[]{:S(2)}, u32[]{:S(2)}) collective-permute-start(f32[4,12,256]{2,1,0:T(8,128)S(1)} %get-tuple-element.52), channel_id=1, source_target_pairs={{0,8},{8,0},{16,24},{24,16},{1,9},{9,1},{17,25},{25,17},{2,10},{10... | collective-permute-start | bytes 147464 | tf_op jit(solution)/shard_map/ppermute | solution.py:511
  21.3 9.3 %collective-permute-start.6 = (f32[4,12,256]{2,1,0:T(8,128)S(1)}, f32[4,12,256]{2,1,0:T(8,128)S(1)}, u32[]{:S(2)}, u32[]{:S(2)}) collective-permute-start(f32[4,12,256]{2,1,0:T(8,128)S(1)} %get-tuple-element.53), channel_id=1, source_target_pairs={{8,16},{16,8},{9,17},{17,9},{10,18},{18,10},{11,19},{19,11},{12,20... | collective-permute-start | bytes 147464 | tf_op jit(solution)/shard_map/ppermute | solution.py:277
  22.0 8.6 %collective-permute-start.7 = (f32[64,128]{1,0:T(8,128)S(1)}, f32[64,128]{1,0:T(8,128)S(1)}, u32[]{:S(2)}, u32[]{:S(2)}) collective-permute-start(f32[64,128]{1,0:T(8,128)S(1)} %get-tuple-element.54), channel_id=1, source_target_pairs={{0,1},{1,0},{2,3},{3,2},{4,5},{5,4},{6,7},{7,6},{8,9},{9,8},{10,11... | collective-permute-start | bytes 98312 | tf_op jit(solution)/shard_map/ppermute | solution.py:511
  25.0 5.6 %collective-permute-start.8 = (f32[64,128]{1,0:T(8,128)S(1)}, f32[64,128]{1,0:T(8,128)S(1)}, u32[]{:S(2)}, u32[]{:S(2)}) collective-permute-start(f32[64,128]{1,0:T(8,128)S(1)} %get-tuple-element.55), channel_id=1, source_target_pairs={{1,2},{3,4},{5,6},{2,1},{4,3},{6,5},{9,10},{11,12},{13,14},{10,9},... | collective-permute-start | bytes 98312 | tf_op jit(solution)/shard_map/ppermute | solution.py:277
  25.9 11.9 %collective-permute-start.9 = (f32[64,1024]{1,0:T(8,128)S(1)}, f32[64,1024]{1,0:T(8,128)S(1)}, u32[]{:S(2)}, u32[]{:S(2)}) collective-permute-start(f32[64,1024]{1,0:T(8,128)S(1)} %pad_maximum_fusion.1), channel_id=1, source_target_pairs={{0,2},{1,3},{2,0},{3,1},{4,6},{5,7},{6,4},{7,5},{8,10},{9,11},{10,... | collective-permute-start | bytes 786440 | tf_op jit(solution)/shard_map/ppermute | solution.py:511
  30.6 10.5 %copy-start.3 = (s32[256,128]{1,0:T(8,128)S(1)}, s32[256,128]{1,0:T(8,128)}, u32[]{:S(2)}) copy-start(s32[256,128]{1,0:T(8,128)} %cells_ref.1) | copy-start | bytes 393220
  30.6 10.4 %copy-start.6 = (s32[2,128]{1,0:T(2,128)S(1)}, s32[2,128]{1,0:T(2,128)}, u32[]{:S(2)}) copy-start(s32[2,128]{1,0:T(2,128)} %get-tuple-element.57) | copy-start | bytes 3076
  37.9 22.9 %collective-permute-start.10 = (f32[128,1024]{1,0:T(8,128)S(1)}, f32[128,1024]{1,0:T(8,128)S(1)}, u32[]{:S(2)}, u32[]{:S(2)}) collective-permute-start(f32[128,1024]{1,0:T(8,128)S(1)} %pad_maximum_fusion), channel_id=1, source_target_pairs={{0,1},{1,0},{2,3},{3,2},{4,5},{5,4},{6,7},{7,6},{8,9},{9,8},{10,11... | collective-permute-start | bytes 1572872 | tf_op jit(solution)/shard_map/ppermute | solution.py:511
  60.8 2.0 %collective-permute-start.11 = (f32[128,8,128]{2,1,0:T(8,128)S(1)}, f32[128,8,128]{2,1,0:T(8,128)S(1)}, u32[]{:S(2)}, u32[]{:S(2)}) collective-permute-start(f32[128,8,128]{2,1,0:T(8,128)S(1)} %get-tuple-element.68), channel_id=1, source_target_pairs={{0,8},{8,0},{16,24},{24,16},{1,9},{9,1},{17,25},{25,17},{2,10},{10... | collective-permute-start | bytes 1572872 | tf_op jit(solution)/shard_map/ppermute | solution.py:511
  62.8 8.7 %collective-permute-start.12 = (f32[64,8,128]{2,1,0:T(8,128)S(1)}, f32[64,8,128]{2,1,0:T(8,128)S(1)}, u32[]{:S(2)}, u32[]{:S(2)}) collective-permute-start(f32[64,8,128]{2,1,0:T(8,128)S(1)} %get-tuple-element.81), channel_id=1, source_target_pairs={{0,16},{8,24},{16,0},{24,8},{1,17},{9,25},{17,1},{25,9},{2,18},{10... | collective-permute-start | bytes 786440 | tf_op jit(solution)/shard_map/ppermute | solution.py:511
  72.5 4.3 %collective-permute-start.13 = (f32[17,8,128]{2,1,0:T(8,128)S(1)}, f32[17,8,128]{2,1,0:T(8,128)S(1)}, u32[]{:S(2)}, u32[]{:S(2)}) collective-permute-start(f32[17,8,128]{2,1,0:T(8,128)S(1)} %get-tuple-element.74), channel_id=1, source_target_pairs={{0,1},{1,0},{2,3},{3,2},{4,5},{5,4},{6,7},{7,6},{8,9},{9,8},{10,11... | collective-permute-start | bytes 208904 | tf_op jit(solution)/shard_map/ppermute | solution.py:511
  72.6 6.3 %collective-permute-start.14 = (f32[17,8,128]{2,1,0:T(8,128)S(1)}, f32[17,8,128]{2,1,0:T(8,128)S(1)}, u32[]{:S(2)}, u32[]{:S(2)}) collective-permute-start(f32[17,8,128]{2,1,0:T(8,128)S(1)} %get-tuple-element.75), channel_id=1, source_target_pairs={{0,2},{1,3},{2,0},{3,1},{4,6},{5,7},{6,4},{7,5},{8,10},{9,11},{10,... | collective-permute-start | bytes 208904 | tf_op jit(solution)/shard_map/ppermute | solution.py:511
  76.0 5.2 %collective-permute-start.15 = (f32[17,8,128]{2,1,0:T(8,128)S(1)}, f32[17,8,128]{2,1,0:T(8,128)S(1)}, u32[]{:S(2)}, u32[]{:S(2)}) collective-permute-start(f32[17,8,128]{2,1,0:T(8,128)S(1)} %get-tuple-element.76), channel_id=1, source_target_pairs={{0,3},{1,2},{2,1},{3,0},{4,7},{5,6},{6,5},{7,4},{8,11},{9,10},{10,... | collective-permute-start | bytes 208904 | tf_op jit(solution)/shard_map/ppermute | solution.py:511
  81.2 4.9 %collective-permute-start.16 = (f32[9,8,128]{2,1,0:T(8,128)S(1)}, f32[9,8,128]{2,1,0:T(8,128)S(1)}, u32[]{:S(2)}, u32[]{:S(2)}) collective-permute-start(f32[9,8,128]{2,1,0:T(8,128)S(1)} %get-tuple-element.78), channel_id=1, source_target_pairs={{0,4},{1,5},{2,6},{3,7},{4,0},{5,1},{6,2},{7,3},{8,12},{9,13},{10,... | collective-permute-start | bytes 110600 | tf_op jit(solution)/shard_map/ppermute | solution.py:511
  86.2 1.9 %collective-permute-start.17 = (f32[9,8,128]{2,1,0:T(8,128)S(1)}, f32[9,8,128]{2,1,0:T(8,128)S(1)}, u32[]{:S(2)}, u32[]{:S(2)}) collective-permute-start(f32[9,8,128]{2,1,0:T(8,128)S(1)} %fold.3.refs_0_), channel_id=1, source_target_pairs={{0,8},{8,0},{16,24},{24,16},{1,9},{9,1},{17,25},{25,17},{2,10},{10... | collective-permute-start | bytes 110600 | tf_op jit(solution)/shard_map/ppermute | solution.py:511
  86.2 4.0 %collective-permute-start.18 = (f32[9,8,128]{2,1,0:T(8,128)S(1)}, f32[9,8,128]{2,1,0:T(8,128)S(1)}, u32[]{:S(2)}, u32[]{:S(2)}) collective-permute-start(f32[9,8,128]{2,1,0:T(8,128)S(1)} %fold.3.refs_0_), channel_id=1, source_target_pairs={{0,16},{8,24},{16,0},{24,8},{1,17},{9,25},{17,1},{25,9},{2,18},{10... | collective-permute-start | bytes 110600 | tf_op jit(solution)/shard_map/ppermute | solution.py:511
  88.0 3.4 %collective-permute-start.19 = (f32[9,8,128]{2,1,0:T(8,128)S(1)}, f32[9,8,128]{2,1,0:T(8,128)S(1)}, u32[]{:S(2)}, u32[]{:S(2)}) collective-permute-start(f32[9,8,128]{2,1,0:T(8,128)S(1)} %fold.3.refs_0_), channel_id=1, source_target_pairs={{0,24},{8,16},{16,8},{24,0},{1,25},{9,17},{17,9},{25,1},{2,26},{10... | collective-permute-start | bytes 110600 | tf_op jit(solution)/shard_map/ppermute | solution.py:511

commit v5 on v4

--- a/solution.py
+++ b/solution.py
@@ -534,7 +534,8 @@
     found = []
     base = 1
     while base < lax.axis_size(axis):
-        size = min(4, lax.axis_size(axis) // base)
+        left = lax.axis_size(axis) // base
+        size = 2 if left.bit_length() % 2 == 0 else 4
         found.append((base, size))
         base *= size
     return found

time: 92.3 us -> 91.7 us (level)
  waiting for transfers between devices: 22.1 us -> 21.1 us
    ppermute x16, waiting for transfers between devices: 22.1 us -> 21.1 us  [swap(): lax.ppermute(send, axis, [(i, i ^ bit) for i in range(lax.axis_size(axis))])]
  transfers between devices with their start and end apart: 20 -> 20, of which waited for: 9 -> 8; matrix products, arithmetic and copies ran while one was open for 0% -> 0% of each run, Pallas kernels for 35% -> 35%
where the time goes in v5:
time: 91.7 us; the launch traced here: 91.6 us
  Pallas kernels  37.5 us (41%)
  starting transfers between devices  31.9 us (35%)
  waiting for transfers between devices  21.1 us (23%)
    ppermute x16, starting transfers between devices, swap(): lax.ppermute(send, axis, [(i, i ^ bit) for i in range(lax.axis_size(axis))])  29.1 us
    ppermute x16, waiting for transfers between devices, swap(): lax.ppermute(send, axis, [(i, i ^ bit) for i in range(lax.axis_size(axis))])  21.1 us
    pallas_call x1, Pallas kernels, tile_sums(): pl.pallas_call(tile_kernel, grid=(tiles // block,), out_shape=(jax.ShapeD...  19.7 us
    pallas_call x2, Pallas kernels, sweep(): pl.pallas_call(functools.partial(sweep_kernel, last), out_shape=(jax.Shap...  12.8 us
    pallas_call x1, Pallas kernels, pack(): pl.pallas_call(functools.partial(pack_kernel, modes), out_shape=shapes +...  3.35 us
    ppermute x4, starting transfers between devices, exchange(): got.append(lax.ppermute(second, axis, pairs + [(b, a) for a, b in pairs]))  2.79 us
  transfers between devices with their start and end apart: 20, of which 8 were waited for; matrix products, arithmetic and copies ran while one was open for 0% of the time, Pallas kernels for 35%

profile of v5, /device:TPU:0, one launch (start us, length us, event | category | flops | bytes accessed | tf_op | source)
XLA Modules:
  0.0 91.6 jit_solution(4589651213617572879)
XLA Ops:
  0.7 3.4 %pack.1 = (f32[4,12,256]{2,1,0:T(8,128)}, f32[4,12,256]{2,1,0:T(8,128)}, f32[64,128]{1,0:T(8,128)}, f32[64,128]{1,0:T(8,128)}, f32[32,1024]{1,0:T(8,128)}, /*index=5*/s32[2,128]{1,0:T(2,128)}) custom-call(f32[48,64,256]{2,1,0:T(8,128)} %state_ref.3, f32[32,4096]{1,0:T(8,128)} %shape_ref.1, f32[1,4096]{1,0:T(1,128)} %bitcast.5, s32[2,128]{1,0:T(2,128)} %bitcast.6, ...), custom_call_target="tpu_custom_call" | custom-call | tf_op jit(solution)/shard_map/pack/pallas_call | solution.py:254
  4.0 0.5 collective-permute-start
  4.6 0.7 collective-permute-start.1
  5.2 2.6 %collective-permute-start.2 = (f32[64,128]{1,0:T(8,128)}, f32[64,128]{1,0:T(8,128)S(1)}, u32[]{:S(2)}, u32[]{:S(2)}) collective-permute-start(f32[64,128]{1,0:T(8,128)} %get-tuple-element.44), channel_id=1, source_target_pairs={{0,1},{1,0},{2,3},{3,2},{4,5},{5,4},{6,7},{7,6},{8,9},{9,8},{10,11... | collective-permute-start | bytes 98312 | tf_op jit(solution)/shard_map/ppermute | solution.py:511
  7.8 0.7 collective-permute-start.3
  8.5 4.3 %collective-permute-start.4 = (f32[32,1024]{1,0:T(8,128)}, f32[32,1024]{1,0:T(8,128)S(1)}, u32[]{:S(2)}, u32[]{:S(2)}) collective-permute-start(f32[32,1024]{1,0:T(8,128)} %get-tuple-element.69.refs_0_), channel_id=1, source_target_pairs={{0,4},{1,5},{2,6},{3,7},{4,0},{5,1},{6,2},{7,3},{8,12},{9,13},{10,... | collective-permute-start | bytes 393224 | tf_op jit(solution)/shard_map/ppermute | solution.py:511
  12.9 6.3 %sweep.2 = (f32[48,64,256]{2,1,0:T(8,128)S(1)}, f32[4,12,256]{2,1,0:T(8,128)S(1)}, f32[4,12,256]{2,1,0:T(8,128)S(1)}, f32[64,128]{1,0:T(8,128)S(1)}, f32[64,128]{1,0:T(8,128)S(1)}) custom-call(f32[6,6]{1,0:T(8,128)S(1)} %copy-done.5, f32[4]{0:T(128)S(1)} %copy-done.7, f32[6]{0:T(128)S(1)} %copy-done.8, f32[48,64,256]{2,1,0:T(8,128)S(1)} %copy-done, ...), custom_call_target="tpu_custom_call" | custom-call | flops 8000000000 | bytes 9437184 | tf_op jit(solution)/shard_map/sweep/pallas_call | solution.py:294
  19.2 2.1 %collective-permute-start.5 = (f32[4,12,256]{2,1,0:T(8,128)S(1)}, f32[4,12,256]{2,1,0:T(8,128)S(1)}, u32[]{:S(2)}, u32[]{:S(2)}) collective-permute-start(f32[4,12,256]{2,1,0:T(8,128)S(1)} %get-tuple-element.52), channel_id=1, source_target_pairs={{0,8},{8,0},{16,24},{24,16},{1,9},{9,1},{17,25},{25,17},{2,10},{10... | collective-permute-start | bytes 147464 | tf_op jit(solution)/shard_map/ppermute | solution.py:511
  21.3 0.7 collective-permute-start.6
  22.0 3.1 %collective-permute-start.7 = (f32[64,128]{1,0:T(8,128)S(1)}, f32[64,128]{1,0:T(8,128)S(1)}, u32[]{:S(2)}, u32[]{:S(2)}) collective-permute-start(f32[64,128]{1,0:T(8,128)S(1)} %get-tuple-element.54), channel_id=1, source_target_pairs={{0,1},{1,0},{2,3},{3,2},{4,5},{5,4},{6,7},{7,6},{8,9},{9,8},{10,11... | collective-permute-start | bytes 98312 | tf_op jit(solution)/shard_map/ppermute | solution.py:511
  25.0 0.8 collective-permute-start.8
  25.9 4.7 %collective-permute-start.9 = (f32[64,1024]{1,0:T(8,128)S(1)}, f32[64,1024]{1,0:T(8,128)S(1)}, u32[]{:S(2)}, u32[]{:S(2)}) collective-permute-start(f32[64,1024]{1,0:T(8,128)S(1)} %pad_maximum_fusion.1), channel_id=1, source_target_pairs={{0,2},{1,3},{2,0},{3,1},{4,6},{5,7},{6,4},{7,5},{8,10},{9,11},{10,... | collective-permute-start | bytes 786440 | tf_op jit(solution)/shard_map/ppermute | solution.py:511
  30.7 6.5 %sweep.3 = (f32[48,64,256]{2,1,0:T(8,128)}, bf16[1024,256]{1,0:T(8,128)(2,1)S(1)}, f32[2,512,128]{2,1,0:T(8,128)S(1)}) custom-call(f32[6,6]{1,0:T(8,128)S(1)} %copy-done.5, f32[4]{0:T(128)S(1)} %copy-done.7, f32[6]{0:T(128)S(1)} %copy-done.8, f32[48,64,256]{2,1,0:T(8,128)S(1)} %get-tuple-element.46.state_ref, f32[48,64,256]{2,1,0:T(8,128)S(1)} %copy-done.2, ...), custom_call_target="tpu_custom_call" | custom-call | flops 8000000000 | bytes 9437184 | tf_op jit(solution)/shard_map/sweep/pallas_call | solution.py:294
  37.1 0.7 collective-permute-done.9.refs_2_
  37.9 3.2 %collective-permute-start.10 = (f32[128,1024]{1,0:T(8,128)S(1)}, f32[128,1024]{1,0:T(8,128)S(1)}, u32[]{:S(2)}, u32[]{:S(2)}) collective-permute-start(f32[128,1024]{1,0:T(8,128)S(1)} %pad_maximum_fusion), channel_id=1, source_target_pairs={{0,1},{1,0},{2,3},{3,2},{4,5},{5,4},{6,7},{7,6},{8,9},{9,8},{10,11... | collective-permute-start | bytes 1572872 | tf_op jit(solution)/shard_map/ppermute | solution.py:511
  41.1 19.7 %tiles.1 = (f32[128,8,128]{2,1,0:T(8,128)S(1)}, f32[128,8,128]{2,1,0:T(8,128)S(1)}) custom-call(s32[256]{0:T(256)S(1)} %bitcast.4, bf16[1024,256]{1,0:T(8,128)(2,1)S(1)} %get-tuple-element.61.table_ref, f32[2,512,128]{2,1,0:T(8,128)S(1)} %get-tuple-element.62.press_ref, s32[256,128]{1,0:T(8,128)S(1)} %copy-done.3, f32[256,128,128]{2,1,0:T(8,128)} %interp_ref.1), custom_call_target="tpu_custom_call" | custom-call | flops 17179869184 | bytes 16777216 | tf_op jit(solution)/shard_map/tiles/pallas_call | solution.py:409
  60.8 0.1 collective-permute-start.11
  60.9 1.9 %collective-permute-done.11 = f32[128,8,128]{2,1,0:T(8,128)S(1)} collective-permute-done((f32[128,8,128]{2,1,0:T(8,128)S(1)}, f32[128,8,128]{2,1,0:T(8,128)S(1)}, u32[]{:S(2)}, u32[]{:S(2)}) %collective-permute-start.11) | collective-permute-done | bytes 524320 | tf_op jit(solution)/shard_map/ppermute | solution.py:511
  62.8 2.2 %collective-permute-start.12 = (f32[64,8,128]{2,1,0:T(8,128)S(1)}, f32[64,8,128]{2,1,0:T(8,128)S(1)}, u32[]{:S(2)}, u32[]{:S(2)}) collective-permute-start(f32[64,8,128]{2,1,0:T(8,128)S(1)} %get-tuple-element.81), channel_id=1, source_target_pairs={{0,16},{8,24},{16,0},{24,8},{1,17},{9,25},{17,1},{25,9},{2,18},{10... | collective-permute-start | bytes 786440 | tf_op jit(solution)/shard_map/ppermute | solution.py:511
  65.0 6.6 %collective-permute-done.12.got_ref = f32[64,8,128]{2,1,0:T(8,128)S(1)} collective-permute-done((f32[64,8,128]{2,1,0:T(8,128)S(1)}, f32[64,8,128]{2,1,0:T(8,128)S(1)}, u32[]{:S(2)}, u32[]{:S(2)}) %collective-permute-start.12) | collective-permute-done | bytes 262176 | tf_op jit(solution)/shard_map/ppermute | solution.py:511
  71.6 0.9 %combine.1 = (f32[33,8,128]{2,1,0:T(8,128)S(1)}, f32[33,8,128]{2,1,0:T(8,128)S(1)}) custom-call(f32[64,8,128]{2,1,0:T(8,128)S(1)} %get-tuple-element.82.keep_ref, f32[64,8,128]{2,1,0:T(8,128)S(1)} %collective-permute-done.12.got_ref, f32[32,1024]{1,0:T(8,128)S(1)} %copy-done.1, f32[32,1024]{1,0:T(8,128)S(1)} %collective-permute-done.4.refs_1_, ...), custom_call_target="tpu_custom_call" | custom-call | tf_op jit(solution)/shard_map/combine/pallas_call | solution.py:483
  72.6 5.1 %collective-permute-done.13.refs_1_ = f32[33,8,128]{2,1,0:T(8,128)S(1)} collective-permute-done((f32[33,8,128]{2,1,0:T(8,128)S(1)}, f32[33,8,128]{2,1,0:T(8,128)S(1)}, u32[]{:S(2)}, u32[]{:S(2)}) %collective-permute-start.13) | collective-permute-done | bytes 135200 | tf_op jit(solution)/shard_map/ppermute | solution.py:511
  77.7 1.8 %collective-permute-start.14 = (f32[9,8,128]{2,1,0:T(8,128)S(1)}, f32[9,8,128]{2,1,0:T(8,128)S(1)}, u32[]{:S(2)}, u32[]{:S(2)}) collective-permute-start(f32[9,8,128]{2,1,0:T(8,128)S(1)} %get-tuple-element.76), channel_id=1, source_target_pairs={{0,2},{1,3},{2,0},{3,1},{4,6},{5,7},{6,4},{7,5},{8,10},{9,11},{10,... | collective-permute-start | bytes 110600 | tf_op jit(solution)/shard_map/ppermute | solution.py:511
  79.5 0.5 collective-permute-start.15
  80.0 2.1 %collective-permute-start.16 = (f32[9,8,128]{2,1,0:T(8,128)S(1)}, f32[9,8,128]{2,1,0:T(8,128)S(1)}, u32[]{:S(2)}, u32[]{:S(2)}) collective-permute-start(f32[9,8,128]{2,1,0:T(8,128)S(1)} %get-tuple-element.78), channel_id=1, source_target_pairs={{0,6},{1,7},{2,4},{3,5},{4,2},{5,3},{6,0},{7,1},{8,14},{9,15},{10,... | collective-permute-start | bytes 110600 | tf_op jit(solution)/shard_map/ppermute | solution.py:511
  82.1 2.3 %collective-permute-done.15.refs_2_ = f32[9,8,128]{2,1,0:T(8,128)S(1)} collective-permute-done((f32[9,8,128]{2,1,0:T(8,128)S(1)}, f32[9,8,128]{2,1,0:T(8,128)S(1)}, u32[]{:S(2)}, u32[]{:S(2)}) %collective-permute-start.15) | collective-permute-done | bytes 36896 | tf_op jit(solution)/shard_map/ppermute | solution.py:511
  84.5 1.3 %collective-permute-done.16.refs_3_ = f32[9,8,128]{2,1,0:T(8,128)S(1)} collective-permute-done((f32[9,8,128]{2,1,0:T(8,128)S(1)}, f32[9,8,128]{2,1,0:T(8,128)S(1)}, u32[]{:S(2)}, u32[]{:S(2)}) %collective-permute-start.16) | collective-permute-done | bytes 36896 | tf_op jit(solution)/shard_map/ppermute | solution.py:511
  85.9 1.6 %collective-permute-start.18 = (f32[9,8,128]{2,1,0:T(8,128)S(1)}, f32[9,8,128]{2,1,0:T(8,128)S(1)}, u32[]{:S(2)}, u32[]{:S(2)}) collective-permute-start(f32[9,8,128]{2,1,0:T(8,128)S(1)} %fold.3.refs_0_), channel_id=1, source_target_pairs={{0,16},{8,24},{16,0},{24,8},{1,17},{9,25},{17,1},{25,9},{2,18},{10... | collective-permute-start | bytes 110600 | tf_op jit(solution)/shard_map/ppermute | solution.py:511
  87.4 0.3 collective-permute-start.19
  87.7 2.2 %collective-permute-done.18.refs_2_ = f32[9,8,128]{2,1,0:T(8,128)S(1)} collective-permute-done((f32[9,8,128]{2,1,0:T(8,128)S(1)}, f32[9,8,128]{2,1,0:T(8,128)S(1)}, u32[]{:S(2)}, u32[]{:S(2)}) %collective-permute-start.18) | collective-permute-done | bytes 36896 | tf_op jit(solution)/shard_map/ppermute | solution.py:511
  89.9 1.0 %collective-permute-done.19.refs_3_ = f32[9,8,128]{2,1,0:T(8,128)S(1)} collective-permute-done((f32[9,8,128]{2,1,0:T(8,128)S(1)}, f32[9,8,128]{2,1,0:T(8,128)S(1)}, u32[]{:S(2)}, u32[]{:S(2)}) %collective-permute-start.19) | collective-permute-done | bytes 36896 | tf_op jit(solution)/shard_map/ppermute | solution.py:511
  90.9 0.7 finish.1
  (37 shorter events, 0.3 us)
Async XLA Ops:
  0.6 12.2 %copy-start = (f32[48,64,256]{2,1,0:T(8,128)S(1)}, f32[48,64,256]{2,1,0:T(8,128)}, u32[]{:S(2)}) copy-start(f32[48,64,256]{2,1,0:T(8,128)} %state_ref.3) | copy-start | bytes 9437188
  0.6 12.2 %copy-start.5 = (f32[6,6]{1,0:T(8,128)S(1)}, f32[6,6]{1,0:T(8,128)}, u32[]{:S(2)}) copy-start(f32[6,6]{1,0:T(8,128)} %coupling_ref.3) | copy-start | bytes 436
  0.7 12.2 %copy-start.7 = (f32[4]{0:T(128)S(1)}, f32[4]{0:T(128)}, u32[]{:S(2)}) copy-start(f32[4]{0:T(128)} %omega_ref.3) | copy-start | bytes 52
  0.7 12.2 %copy-start.8 = (f32[6]{0:T(128)S(1)}, f32[6]{0:T(128)}, u32[]{:S(2)}) copy-start(f32[6]{0:T(128)} %coef_ref.3) | copy-start | bytes 76
  0.7 12.2 %copy-start.4 = (f32[64,256]{1,0:T(8,128)S(1)}, f32[64,256]{1,0:T(8,128)}, u32[]{:S(2)}) copy-start(f32[64,256]{1,0:T(8,128)} %sigma_ref.3) | copy-start | bytes 196612
  4.0 8.8 %collective-permute-start = (f32[4,12,256]{2,1,0:T(8,128)}, f32[4,12,256]{2,1,0:T(8,128)S(1)}, u32[]{:S(2)}, u32[]{:S(2)}) collective-permute-start(f32[4,12,256]{2,1,0:T(8,128)} %get-tuple-element.42), channel_id=1, source_target_pairs={{0,8},{8,0},{16,24},{24,16},{1,9},{9,1},{17,25},{25,17},{2,10},{10... | collective-permute-start | bytes 147464 | tf_op jit(solution)/shard_map/ppermute | solution.py:511
  4.6 8.3 %collective-permute-start.1 = (f32[4,12,256]{2,1,0:T(8,128)}, f32[4,12,256]{2,1,0:T(8,128)S(1)}, u32[]{:S(2)}, u32[]{:S(2)}) collective-permute-start(f32[4,12,256]{2,1,0:T(8,128)} %get-tuple-element.43), channel_id=1, source_target_pairs={{8,16},{16,8},{9,17},{17,9},{10,18},{18,10},{11,19},{19,11},{12,20... | collective-permute-start | bytes 147464 | tf_op jit(solution)/shard_map/ppermute | solution.py:277
  5.2 7.6 %collective-permute-start.2 = (f32[64,128]{1,0:T(8,128)}, f32[64,128]{1,0:T(8,128)S(1)}, u32[]{:S(2)}, u32[]{:S(2)}) collective-permute-start(f32[64,128]{1,0:T(8,128)} %get-tuple-element.44), channel_id=1, source_target_pairs={{0,1},{1,0},{2,3},{3,2},{4,5},{5,4},{6,7},{7,6},{8,9},{9,8},{10,11... | collective-permute-start | bytes 98312 | tf_op jit(solution)/shard_map/ppermute | solution.py:511
  7.8 5.0 %collective-permute-start.3 = (f32[64,128]{1,0:T(8,128)}, f32[64,128]{1,0:T(8,128)S(1)}, u32[]{:S(2)}, u32[]{:S(2)}) collective-permute-start(f32[64,128]{1,0:T(8,128)} %get-tuple-element.45), channel_id=1, source_target_pairs={{1,2},{3,4},{5,6},{2,1},{4,3},{6,5},{9,10},{11,12},{13,14},{10,9},... | collective-permute-start | bytes 98312 | tf_op jit(solution)/shard_map/ppermute | solution.py:277
  8.5 17.4 %copy-start.1 = (f32[32,1024]{1,0:T(8,128)S(1)}, f32[32,1024]{1,0:T(8,128)}, u32[]{:S(2)}) copy-start(f32[32,1024]{1,0:T(8,128)} %get-tuple-element.69.refs_0_) | copy-start | bytes 393220
  8.5 22.1 %copy-start.2 = (f32[48,64,256]{2,1,0:T(8,128)S(1)}, f32[48,64,256]{2,1,0:T(8,128)}, u32[]{:S(2)}) copy-start(f32[48,64,256]{2,1,0:T(8,128)} %right_ref.3) | copy-start | bytes 9437188
  8.5 10.7 %collective-permute-start.4 = (f32[32,1024]{1,0:T(8,128)}, f32[32,1024]{1,0:T(8,128)S(1)}, u32[]{:S(2)}, u32[]{:S(2)}) collective-permute-start(f32[32,1024]{1,0:T(8,128)} %get-tuple-element.69.refs_0_), channel_id=1, source_target_pairs={{0,4},{1,5},{2,6},{3,7},{4,0},{5,1},{6,2},{7,3},{8,12},{9,13},{10,... | collective-permute-start | bytes 393224 | tf_op jit(solution)/shard_map/ppermute | solution.py:511
  19.2 11.4 %collective-permute-start.5 = (f32[4,12,256]{2,1,0:T(8,128)S(1)}, f32[4,12,256]{2,1,0:T(8,128)S(1)}, u32[]{:S(2)}, u32[]{:S(2)}) collective-permute-start(f32[4,12,256]{2,1,0:T(8,128)S(1)} %get-tuple-element.52), channel_id=1, source_target_pairs={{0,8},{8,0},{16,24},{24,16},{1,9},{9,1},{17,25},{25,17},{2,10},{10... | collective-permute-start | bytes 147464 | tf_op jit(solution)/shard_map/ppermute | solution.py:511
  21.3 9.3 %collective-permute-start.6 = (f32[4,12,256]{2,1,0:T(8,128)S(1)}, f32[4,12,256]{2,1,0:T(8,128)S(1)}, u32[]{:S(2)}, u32[]{:S(2)}) collective-permute-start(f32[4,12,256]{2,1,0:T(8,128)S(1)} %get-tuple-element.53), channel_id=1, source_target_pairs={{8,16},{16,8},{9,17},{17,9},{10,18},{18,10},{11,19},{19,11},{12,20... | collective-permute-start | bytes 147464 | tf_op jit(solution)/shard_map/ppermute | solution.py:277
  22.0 8.6 %collective-permute-start.7 = (f32[64,128]{1,0:T(8,128)S(1)}, f32[64,128]{1,0:T(8,128)S(1)}, u32[]{:S(2)}, u32[]{:S(2)}) collective-permute-start(f32[64,128]{1,0:T(8,128)S(1)} %get-tuple-element.54), channel_id=1, source_target_pairs={{0,1},{1,0},{2,3},{3,2},{4,5},{5,4},{6,7},{7,6},{8,9},{9,8},{10,11... | collective-permute-start | bytes 98312 | tf_op jit(solution)/shard_map/ppermute | solution.py:511
  25.0 5.6 %collective-permute-start.8 = (f32[64,128]{1,0:T(8,128)S(1)}, f32[64,128]{1,0:T(8,128)S(1)}, u32[]{:S(2)}, u32[]{:S(2)}) collective-permute-start(f32[64,128]{1,0:T(8,128)S(1)} %get-tuple-element.55), channel_id=1, source_target_pairs={{1,2},{3,4},{5,6},{2,1},{4,3},{6,5},{9,10},{11,12},{13,14},{10,9},... | collective-permute-start | bytes 98312 | tf_op jit(solution)/shard_map/ppermute | solution.py:277
  25.9 11.9 %collective-permute-start.9 = (f32[64,1024]{1,0:T(8,128)S(1)}, f32[64,1024]{1,0:T(8,128)S(1)}, u32[]{:S(2)}, u32[]{:S(2)}) collective-permute-start(f32[64,1024]{1,0:T(8,128)S(1)} %pad_maximum_fusion.1), channel_id=1, source_target_pairs={{0,2},{1,3},{2,0},{3,1},{4,6},{5,7},{6,4},{7,5},{8,10},{9,11},{10,... | collective-permute-start | bytes 786440 | tf_op jit(solution)/shard_map/ppermute | solution.py:511
  30.6 10.5 %copy-start.3 = (s32[256,128]{1,0:T(8,128)S(1)}, s32[256,128]{1,0:T(8,128)}, u32[]{:S(2)}) copy-start(s32[256,128]{1,0:T(8,128)} %cells_ref.1) | copy-start | bytes 393220
  30.6 10.4 %copy-start.6 = (s32[2,128]{1,0:T(2,128)S(1)}, s32[2,128]{1,0:T(2,128)}, u32[]{:S(2)}) copy-start(s32[2,128]{1,0:T(2,128)} %get-tuple-element.57) | copy-start | bytes 3076
  37.9 22.9 %collective-permute-start.10 = (f32[128,1024]{1,0:T(8,128)S(1)}, f32[128,1024]{1,0:T(8,128)S(1)}, u32[]{:S(2)}, u32[]{:S(2)}) collective-permute-start(f32[128,1024]{1,0:T(8,128)S(1)} %pad_maximum_fusion), channel_id=1, source_target_pairs={{0,1},{1,0},{2,3},{3,2},{4,5},{5,4},{6,7},{7,6},{8,9},{9,8},{10,11... | collective-permute-start | bytes 1572872 | tf_op jit(solution)/shard_map/ppermute | solution.py:511
  60.8 2.0 %collective-permute-start.11 = (f32[128,8,128]{2,1,0:T(8,128)S(1)}, f32[128,8,128]{2,1,0:T(8,128)S(1)}, u32[]{:S(2)}, u32[]{:S(2)}) collective-permute-start(f32[128,8,128]{2,1,0:T(8,128)S(1)} %get-tuple-element.68), channel_id=1, source_target_pairs={{0,8},{8,0},{16,24},{24,16},{1,9},{9,1},{17,25},{25,17},{2,10},{10... | collective-permute-start | bytes 1572872 | tf_op jit(solution)/shard_map/ppermute | solution.py:511
  62.8 8.8 %collective-permute-start.12 = (f32[64,8,128]{2,1,0:T(8,128)S(1)}, f32[64,8,128]{2,1,0:T(8,128)S(1)}, u32[]{:S(2)}, u32[]{:S(2)}) collective-permute-start(f32[64,8,128]{2,1,0:T(8,128)S(1)} %get-tuple-element.81), channel_id=1, source_target_pairs={{0,16},{8,24},{16,0},{24,8},{1,17},{9,25},{17,1},{25,9},{2,18},{10... | collective-permute-start | bytes 786440 | tf_op jit(solution)/shard_map/ppermute | solution.py:511
  72.5 5.1 %collective-permute-start.13 = (f32[33,8,128]{2,1,0:T(8,128)S(1)}, f32[33,8,128]{2,1,0:T(8,128)S(1)}, u32[]{:S(2)}, u32[]{:S(2)}) collective-permute-start(f32[33,8,128]{2,1,0:T(8,128)S(1)} %get-tuple-element.74), channel_id=1, source_target_pairs={{0,1},{1,0},{2,3},{3,2},{4,5},{5,4},{6,7},{7,6},{8,9},{9,8},{10,11... | collective-permute-start | bytes 405512 | tf_op jit(solution)/shard_map/ppermute | solution.py:511
  77.7 4.5 %collective-permute-start.14 = (f32[9,8,128]{2,1,0:T(8,128)S(1)}, f32[9,8,128]{2,1,0:T(8,128)S(1)}, u32[]{:S(2)}, u32[]{:S(2)}) collective-permute-start(f32[9,8,128]{2,1,0:T(8,128)S(1)} %get-tuple-element.76), channel_id=1, source_target_pairs={{0,2},{1,3},{2,0},{3,1},{4,6},{5,7},{6,4},{7,5},{8,10},{9,11},{10,... | collective-permute-start | bytes 110600 | tf_op jit(solution)/shard_map/ppermute | solution.py:511
  79.5 5.0 %collective-permute-start.15 = (f32[9,8,128]{2,1,0:T(8,128)S(1)}, f32[9,8,128]{2,1,0:T(8,128)S(1)}, u32[]{:S(2)}, u32[]{:S(2)}) collective-permute-start(f32[9,8,128]{2,1,0:T(8,128)S(1)} %get-tuple-element.77), channel_id=1, source_target_pairs={{0,4},{1,5},{2,6},{3,7},{4,0},{5,1},{6,2},{7,3},{8,12},{9,13},{10,... | collective-permute-start | bytes 110600 | tf_op jit(solution)/shard_map/ppermute | solution.py:511
  80.0 5.8 %collective-permute-start.16 = (f32[9,8,128]{2,1,0:T(8,128)S(1)}, f32[9,8,128]{2,1,0:T(8,128)S(1)}, u32[]{:S(2)}, u32[]{:S(2)}) collective-permute-start(f32[9,8,128]{2,1,0:T(8,128)S(1)} %get-tuple-element.78), channel_id=1, source_target_pairs={{0,6},{1,7},{2,4},{3,5},{4,2},{5,3},{6,0},{7,1},{8,14},{9,15},{10,... | collective-permute-start | bytes 110600 | tf_op jit(solution)/shard_map/ppermute | solution.py:511
  85.8 1.9 %collective-permute-start.17 = (f32[9,8,128]{2,1,0:T(8,128)S(1)}, f32[9,8,128]{2,1,0:T(8,128)S(1)}, u32[]{:S(2)}, u32[]{:S(2)}) collective-permute-start(f32[9,8,128]{2,1,0:T(8,128)S(1)} %fold.3.refs_0_), channel_id=1, source_target_pairs={{0,8},{8,0},{16,24},{24,16},{1,9},{9,1},{17,25},{25,17},{2,10},{10... | collective-permute-start | bytes 110600 | tf_op jit(solution)/shard_map/ppermute | solution.py:511
  85.9 4.0 %collective-permute-start.18 = (f32[9,8,128]{2,1,0:T(8,128)S(1)}, f32[9,8,128]{2,1,0:T(8,128)S(1)}, u32[]{:S(2)}, u32[]{:S(2)}) collective-permute-start(f32[9,8,128]{2,1,0:T(8,128)S(1)} %fold.3.refs_0_), channel_id=1, source_target_pairs={{0,16},{8,24},{16,0},{24,8},{1,17},{9,25},{17,1},{25,9},{2,18},{10... | collective-permute-start | bytes 110600 | tf_op jit(solution)/shard_map/ppermute | solution.py:511
  87.4 3.4 %collective-permute-start.19 = (f32[9,8,128]{2,1,0:T(8,128)S(1)}, f32[9,8,128]{2,1,0:T(8,128)S(1)}, u32[]{:S(2)}, u32[]{:S(2)}) collective-permute-start(f32[9,8,128]{2,1,0:T(8,128)S(1)} %fold.3.refs_0_), channel_id=1, source_target_pairs={{0,24},{8,16},{16,8},{24,0},{1,25},{9,17},{17,9},{25,1},{2,26},{10... | collective-permute-start | bytes 110600 | tf_op jit(solution)/shard_map/ppermute | solution.py:511
